TPU v7x, 512 devices: a whole 4x8x8 slice. The times are simulated.
512 devices in a mesh: ctx: 8 (over z_hi, x), ep: 64 (over z_lo, y, core).
Axes of the slice: x: 4, y: 8, z: 8 (z_hi: 2, z_lo: 4; z = z_hi * 4 + z_lo), core: 2. Of those that a mesh axis runs over, the one named last changes fastest.
Arguments:
- moe_rows: bfloat16 [65536, 2048], P(('ctx', 'ep')), may hold values from -6 to 6
- expert_ids: int32 [65536, 8], P(('ctx', 'ep')), may hold values from 0 to 127, all different within a row; in each aligned block of 128 rows (0 to 127, 128 to 255, ...) at most 9 rows name the same one
- expert_gates: bfloat16 [65536, 8], P(('ctx', 'ep')), may hold values from 0.049804688 to 1
- expert_weights: bfloat16 [128, 2048, 1536], P('ep', 'ctx'), may hold values from -0.125 to 0.125
Outputs:
- expert_hidden: bfloat16 [8, 128, 64, 9, 768], P('ctx', 'ep')
Inputs may be any that keep to these rules, and one draw needn't show every extreme that they name: `expert_ids`: each token names 8 different experts; in each aligned block of 128 tokens (the tokens of one device) no expert is named more than 9 times, a bound that some block reaches.
All inputs are finite; a program needn't handle non-finite values.
Results may differ from a plain program's by a relative error of at most 0.0012.
Values may be sent and summed in bfloat16 or wider, within the bound.
No kernel may reach another device: no remote copies, remote signals or barrier semaphores. Data moves between devices by JAX's collectives and lax.ppermute only.
A program may use at most 128 MiB of HBM per device.

v0:
```python
import jax
import jax.numpy as jnp
from jax import lax
from jax.sharding import PartitionSpec as P

FF = 768
TOP = 8


def place_rows(block_rows, block_ids, block_gates, experts, capacity):
    flat_ids = block_ids.reshape(-1)
    markers = (flat_ids[:, None] == jnp.arange(experts, dtype=jnp.int32)[None, :]).astype(jnp.int32)
    ranking = jnp.cumsum(markers, axis=0) - markers
    slot_index = jnp.sum(ranking * markers, axis=1)
    places = flat_ids * capacity + slot_index
    owners = jnp.arange(flat_ids.shape[0], dtype=jnp.int32) // block_ids.shape[1]
    buffer = (
        jnp.zeros((experts * capacity, block_rows.shape[1]), block_rows.dtype)
        .at[places]
        .set(block_rows[owners])
    )
    gate_buffer = (
        jnp.zeros((experts * capacity,), block_gates.dtype).at[places].set(block_gates.reshape(-1))
    )
    return (
        buffer.reshape(experts, capacity, block_rows.shape[1]),
        gate_buffer.reshape(experts, capacity),
    )


def project(inputs, weights):
    return jnp.einsum("sucd,udf->uscf", inputs, weights, preferred_element_type=jnp.float32)


def activate(before, gate_values):
    scaled = jnp.transpose(gate_values, (1, 0, 2)).astype(jnp.float32)[..., None]
    return (jax.nn.silu(before[..., :FF]) * before[..., FF:] * scaled).astype(jnp.bfloat16)


def shards(moe_rows, expert_ids, expert_gates, expert_weights):
    sources = lax.axis_size("ep")
    held_experts = expert_weights.shape[0]
    experts = sources * held_experts
    row_count = moe_rows.shape[0]
    capacity = max(2, 9 * row_count * TOP // (8 * experts))
    buffer, gate_buffer = place_rows(moe_rows, expert_ids, expert_gates, experts, capacity)
    buffer = buffer.reshape(sources, held_experts, capacity, buffer.shape[2])
    gate_buffer = gate_buffer.reshape(sources, held_experts, capacity)
    arrived, arrived_gates = (
        lax.all_to_all(buffer, "ep", split_axis=0, concat_axis=0, tiled=True),
        lax.all_to_all(gate_buffer, "ep", split_axis=0, concat_axis=0, tiled=True),
    )
    before = project(arrived, lax.all_gather(expert_weights, "ctx", axis=1, tiled=True))
    hidden = activate(before, arrived_gates)
    return hidden[None]


def solution(mesh):
    in_specs = (
        P(("ctx", "ep"), None),
        P(("ctx", "ep"), None),
        P(("ctx", "ep"), None),
        P("ep", "ctx", None),
    )
    out_specs = P("ctx", "ep", None, None, None)
    return jax.shard_map(shards, mesh=mesh, in_specs=in_specs, out_specs=out_specs, check_vma=False)
```

profile of v0, /device:TPU:216, one launch (start us, length us, event | category | flops | bytes accessed | tf_op | source)
XLA Modules:
  0.0 383.6 jit_solution(16969941079098283597)
XLA Ops:
  6.5 0.0 copy-start
  6.5 0.0 copy-start.1
  6.5 0.0 copy-start.2
  6.5 0.0 all-gather.2.cloned.1.call-start
  6.5 0.7 all-gather.2.cloned.1.call-update
  7.3 0.8 copy.22
  8.1 0.1 eq.29
  8.1 0.1 eq.25
  8.2 0.1 copy.24
  8.3 0.2 fusion.11
  8.6 0.1 copy.25
  8.7 0.0 copy-done.1
  8.8 0.1 copy.21
  8.9 0.1 mul.36
  9.0 0.0 copy-done.2
  9.0 0.1 copy.28
  9.1 0.1 reshape.115
  9.2 0.4 fusion.10
  9.6 7.6 %scatter_custom_fusion.1 = bf16[1152]{0:T(1024)(128)(2,1)S(1)} fusion(s32[1024]{0:T(1024)S(1)} %bitcast.24, bf16[1024]{0:T(1024)(128)(2,1)S(1)} %reshape.115, bf16[]{:T(256)} %constant.26.clone.1), kind=kCustom, calls=%fused_computation.31 | custom fusion | bytes 2306 | tf_op jit(solution)/shard_map/scatter | solution.py:23
  17.2 0.8 reshape_reshape.7
  18.0 10.8 %all-to-all-start.1 = ((bf16[64,2,9]{2,1,0:T(2,128)(2,1)}), bf16[64,2,9]{2,1,0:T(2,128)(2,1)S(1)}, u32[]{:S(2)}, u32[]{:S(2)}) async-start(bf16[64,2,9]{2,1,0:T(2,128)(2,1)} %reshape_reshape.7), calls=%async_computation.1 | async-start | bytes 65536 | tf_op jit(solution)/shard_map/all_to_all | solution.py:51
  28.9 0.0 copy-done
  28.9 22.9 %scatter_custom_fusion = bf16[1152,2048]{1,0:T(8,128)(2,1)} fusion(s32[1024]{0:T(1024)S(1)} %bitcast.25, bf16[128,2048]{1,0:T(8,128)(2,1)S(1)} %copy-done, s32[1024]{0:T(1024)S(1)} %broadcast_clamp_fusion, bf16[]{:T(256)} %constant.26.clone.1), kind=kCustom, calls=%fused_computation.6 | custom fusion | bytes 4718594 | tf_op jit(solution)/shard_map/scatter | solution.py:20
  51.8 8.1 %reshape_reshape.6 = bf16[64,2,9,2048]{3,2,1,0:T(8,128)(2,1)} reshape(bf16[1152,2048]{1,0:T(8,128)(2,1)} %scatter_custom_fusion) | data formatting | bytes 9437184 | tf_op jit(solution)/shard_map/reshape;reshape | solution.py:47
  59.9 11.1 %copy.26 = bf16[64,2,9,2048]{3,1,2,0:T(2,128)(2,1)} copy(bf16[64,2,9,2048]{3,2,1,0:T(8,128)(2,1)} %reshape_reshape.6) | data formatting | bytes 9437184 | tf_op jit(solution)/shard_map/reshape;reshape | solution.py:47
  70.9 0.0 all-to-all-done.1
  70.9 10.9 %all-to-all-start = ((bf16[64,2,9,2048]{3,1,2,0:T(2,128)(2,1)}), bf16[64,2,9,2048]{3,1,2,0:T(2,128)(2,1)}, u32[]{:S(2)}, u32[]{:S(2)}) async-start(bf16[64,2,9,2048]{3,1,2,0:T(2,128)(2,1)} %copy.26), calls=%async_computation | async-start | bytes 9437184 | tf_op jit(solution)/shard_map/all_to_all | solution.py:50
  81.8 0.1 copy.29
  81.9 236.9 %all-to-all-done = bf16[64,2,9,2048]{3,1,2,0:T(2,128)(2,1)} async-done(((bf16[64,2,9,2048]{3,1,2,0:T(2,128)(2,1)}), bf16[64,2,9,2048]{3,1,2,0:T(2,128)(2,1)}, u32[]{:S(2)}, u32[]{:S(2)}) %all-to-all-start) | async-done | bytes 4718624 | tf_op jit(solution)/shard_map/all_to_all | solution.py:50
  318.9 39.1 %all-gather.2.cloned.1.call-done = bf16[2,2048,1536]{2,1,0:T(8,128)(2,1)} async-done(((bf16[2,256,1536]{2,1,0:T(8,128)(2,1)}), bf16[2,2048,1536]{2,1,0:T(8,128)(2,1)}) %all-gather.2.cloned.1.call-update) | async-done | bytes 12582928 | tf_op jit(solution)/shard_map/all_gather | solution.py:53
  358.0 16.8 %fusion = f32[2,64,9,1536]{3,1,2,0:T(8,128)S(1)} fusion(bf16[2,2048,1536]{2,1,0:T(8,128)(2,1)} %all-gather.2.cloned.1.call-done, bf16[64,2,9,2048]{3,1,2,0:T(2,128)(2,1)} %all-to-all-done), kind=kOutput, calls=%fused_computation.3 | convolution fusion | flops 7247757312 | bytes 24379392 | tf_op jit(solution)/shard_map/sucd,udf->uscf/dot_general | solution.py:32
  374.8 2.0 fusion.8
  (9 shorter events, 0.1 us)
Async XLA Ops:
  6.5 22.4 %copy-start = (bf16[128,2048]{1,0:T(8,128)(2,1)S(1)}, bf16[128,2048]{1,0:T(8,128)(2,1)}, u32[]{:S(2)}) copy-start(bf16[128,2048]{1,0:T(8,128)(2,1)} %param.4) | copy-start | bytes 1572868
  6.5 2.2 copy-start.1
  6.5 2.4 copy-start.2
  6.5 351.4 %all-gather.2.cloned.1.call-start = ((), (), s32[]{:S(2)}) async-start(), calls=%async_computation.2 | async-start | bytes 14155776 | tf_op jit(solution)/shard_map/all_gather | solution.py:53
  18.0 52.9 %all-to-all-start.1 = ((bf16[64,2,9]{2,1,0:T(2,128)(2,1)}), bf16[64,2,9]{2,1,0:T(2,128)(2,1)S(1)}, u32[]{:S(2)}, u32[]{:S(2)}) async-start(bf16[64,2,9]{2,1,0:T(2,128)(2,1)} %reshape_reshape.7), calls=%async_computation.1 | async-start | bytes 65536 | tf_op jit(solution)/shard_map/all_to_all | solution.py:51
  70.9 247.9 %all-to-all-start = ((bf16[64,2,9,2048]{3,1,2,0:T(2,128)(2,1)}), bf16[64,2,9,2048]{3,1,2,0:T(2,128)(2,1)}, u32[]{:S(2)}, u32[]{:S(2)}) async-start(bf16[64,2,9,2048]{3,1,2,0:T(2,128)(2,1)} %copy.26), calls=%async_computation | async-start | bytes 9437184 | tf_op jit(solution)/shard_map/all_to_all | solution.py:50
Sparse Core Ops, SparseCore 0:
  10.5 347.4 all-gather.1
where the time goes:
time: 384 us
  waiting for transfers between devices  277 us (72%)
  local copies, waits for them, and re-layouts  52.1 us (14%)
  starting transfers between devices  21.7 us (6%)
  matrix products  16.8 us (4%)
  between operations  13.5 us (4%)
    all_to_all x1, waiting for transfers between devices, shards(): lax.all_to_all(buffer, 'ep', split_axis=0, concat_axis=0, tiled=True)  237 us
    all_gather x1, waiting for transfers between devices, shards(): lax.all_gather(expert_weights, 'ctx', axis=1, tiled=True)  39.1 us
    scatter x1, local copies, waits for them, and re-layouts, place_rows(): buffer = jnp.zeros((experts * capacity, block_rows.shape[1]), block_rows....  22.9 us
    another operation x2, local copies, waits for them, and re-layouts, shards(): buffer = buffer.reshape(sources, held_experts, capacity, buffer.shape[2])  19.1 us
    dot_general x1, matrix products, project(): jnp.einsum('sucd,udf->uscf', inputs, weights, preferred_element_type=jnp....  16.8 us
    all_to_all x1, starting transfers between devices, shards(): lax.all_to_all(buffer, 'ep', split_axis=0, concat_axis=0, tiled=True)  10.9 us
    all_to_all x1, starting transfers between devices, shards(): lax.all_to_all(gate_buffer, 'ep', split_axis=0, concat_axis=0, tiled=True)  10.8 us
  transfers between devices with their start and end apart: 3, of which 2 were waited for; matrix products, arithmetic and copies ran while one was open for 14% of the time, Pallas kernels for 0%

commit v1 on v0

v1 whole, which is shorter than its diff:
```python
import jax
import jax.numpy as jnp
from jax import lax
from jax.experimental import pallas as pl
from jax.experimental.pallas import tpu as pltpu
from jax.sharding import Mesh, PartitionSpec as P

ZH, X, ZL, Y, C = 2, 4, 4, 8, 2
PEERS = Y * C
HELD = 2
CAP = 9
MAIN = CAP - 1
TOP = 8
TOK = 128
D = 2048
FF = 768
KEPT = PEERS * HELD
REST = (ZL - 1) * MAIN
MSG = HELD * CAP * ZL
TAIL = MSG - HELD * ZL
COLS = 512
TILE = 256
INFO = 2 * TOK

f32 = jnp.float32
bf16 = jnp.bfloat16


def iota(shape, dim):
    return lax.broadcasted_iota(jnp.int32, shape, dim)


def earlier():
    return (iota((TOK, TOK), 0) < iota((TOK, TOK), 1)).astype(bf16)


def named(ids, experts):
    hit = (ids[0:1, :] == experts).astype(f32)
    for k in range(1, TOP):
        hit = hit + (ids[k : k + 1, :] == experts).astype(f32)
    return hit


def dispatch_kernel(zl_ref, *refs):
    blocks, out_ref, main_ref, tail_ref = refs[:ZL], refs[ZL], refs[ZL + 1], refs[ZL + 2]

    @pl.when(pl.program_id(0) == 0)
    def _():
        first = zl_ref[0] * KEPT
        before = earlier()
        kept = (iota((KEPT, TOK), 0) + first).astype(f32)
        row = iota((PEERS * ZL * HELD, TOK), 0)
        ending = (first + row // (ZL * HELD) * HELD + row % HELD).astype(f32)
        for b in range(ZL):
            ids = blocks[b][TOK : TOK + TOP, 0:TOK].astype(f32)
            hit = named(ids, kept)
            rank = jnp.dot(hit.astype(bf16), before, preferred_element_type=f32)
            place = jnp.where(hit > 0, rank, -1.0)
            slot = iota((KEPT, MAIN, TOK), 1).astype(f32)
            chosen = (place[:, None, :] == slot).astype(f32)
            main_ref[b] = chosen.reshape(KEPT * MAIN, TOK).astype(bf16)
            hit = jnp.where(row // HELD % ZL == b, named(ids, ending), 0.0)
            rank = jnp.dot(hit.astype(bf16), before, preferred_element_type=f32)
            chosen = jnp.where(rank == MAIN, hit, 0.0)
            tail_ref[b] = chosen.astype(bf16)

    width = out_ref.shape[2]
    last = jnp.zeros((PEERS * ZL * HELD, width), f32)
    for b in range(ZL):
        rows = blocks[b][0:TOK, :]
        moved = jnp.dot(main_ref[b], rows, preferred_element_type=f32).astype(bf16)
        moved = moved.reshape(PEERS, HELD, MAIN, width)
        for e in range(HELD):
            at = e * MAIN if b == 0 else HELD * MAIN + e * REST + (b - 1) * MAIN
            out_ref[:, at : at + MAIN, :] = moved[:, e]
        last = last + jnp.dot(tail_ref[b], rows, preferred_element_type=f32)
    out_ref[:, TAIL:MSG, :] = last.astype(bf16).reshape(PEERS, ZL * HELD, width)


def dispatch(zl, blocks):
    return pl.pallas_call(
        dispatch_kernel,
        grid_spec=pltpu.PrefetchScalarGridSpec(
            num_scalar_prefetch=1,
            grid=(D // COLS,),
            in_specs=[pl.BlockSpec((TOK + TOP, COLS), lambda n, z: (0, n))] * ZL,
            out_specs=pl.BlockSpec((PEERS, MSG, COLS), lambda n, z: (0, 0, n)),
            scratch_shapes=[
                pltpu.VMEM((ZL, KEPT * MAIN, TOK), bf16),
                pltpu.VMEM((ZL, PEERS * ZL * HELD, TOK), bf16),
            ],
        ),
        out_shape=jax.ShapeDtypeStruct((PEERS, MSG, D), bf16),
        compiler_params=pltpu.CompilerParams(vmem_limit_bytes=40 * 1024 * 1024),
        cost_estimate=pl.CostEstimate(
            flops=2 * ZL * 384 * TOK * D, bytes_accessed=7_000_000, transcendentals=0
        ),
    )(zl, *blocks)


def expert_kernel(
    where_ref, x_ref, info_ref, g0_ref, g1_ref, u0_ref, u1_ref, out_ref,
    rows_ref, gate_ref, sort_ref, sort8_ref,
):
    blocks = PEERS * ZL
    count = blocks * MAIN
    zl, zh, first = where_ref[0], where_ref[1], where_ref[2]
    e, n = pl.program_id(0), pl.program_id(1)

    @pl.when((e == 0) & (n == 0))
    def _():
        out_row, in_row = iota((count, count), 0), iota((count, count), 1)
        late = in_row - PEERS * MAIN
        is_late = late >= 0
        peer = jnp.where(is_late, late // REST, in_row // MAIN)
        b = jnp.where(is_late, late % REST // MAIN + 1, 0)
        slot = in_row % MAIN
        source = (zl - b + ZL) % ZL * PEERS + peer
        sort_ref[...] = (out_row == slot * blocks + source).astype(f32).astype(bf16)

    @pl.when(n == 0)
    def _():
        near = pl.ds(pl.multiple_of(zh * (D // 2), D // 2), D // 2)
        far = pl.ds(pl.multiple_of((1 - zh) * (D // 2), D // 2), D // 2)
        for half, cols in enumerate((near, far)):
            to = slice(half * (D // 2), (half + 1) * (D // 2))
            for mine in range(HELD):

                @pl.when(e == mine)
                def _():
                    at = mine * MAIN
                    rows_ref[0 : PEERS * MAIN, to] = x_ref[:, at : at + MAIN, cols].reshape(
                        PEERS * MAIN, D // 2
                    )
                    at = HELD * MAIN + mine * REST
                    rows_ref[PEERS * MAIN : count, to] = x_ref[:, at : at + REST, cols].reshape(
                        PEERS * REST, D // 2
                    )

            rows_ref[count:, to] = x_ref[:, TAIL:MSG, cols].reshape(blocks * HELD, D // 2)

        expert = (first + e).astype(f32)
        hit = jnp.zeros((blocks, TOK), f32)
        gate = jnp.zeros((blocks, TOK), f32)
        for k in range(TOP):
            same = info_ref[k, :, 0:TOK].astype(f32) == expert
            hit = hit + same.astype(f32)
            gate = gate + jnp.where(same, info_ref[k, :, TOK:INFO].astype(f32), 0.0)
        rank = jnp.dot(hit.astype(bf16), earlier(), preferred_element_type=f32)
        ones = jnp.ones((TOK, TILE), bf16)
        slot = iota((blocks, MAIN, TOK), 1).astype(f32)
        chosen = jnp.where(rank[:, None, :] == slot, gate[:, None, :], 0.0)
        near_rows = PEERS * MAIN
        chosen = chosen.reshape(ZL, near_rows, TOK)
        gate_ref[0:near_rows, :] = jnp.dot(
            chosen[0].astype(bf16), ones, preferred_element_type=f32
        )
        others = jnp.concatenate(
            [chosen[b].reshape(PEERS, MAIN, TOK) for b in range(1, ZL)], axis=1
        ).reshape(PEERS * REST, TOK)
        gate_ref[near_rows:count, :] = jnp.dot(
            others.astype(bf16), ones, preferred_element_type=f32
        )
        last = jnp.where(rank == MAIN, gate, 0.0).astype(bf16)
        last = jnp.dot(last, ones, preferred_element_type=f32).astype(bf16)
        row, col = iota((blocks * HELD, blocks), 0), iota((blocks * HELD, blocks), 1)
        peer, b = row // (ZL * HELD), row // HELD % ZL
        spread = (col == b * PEERS + peer).astype(f32).astype(bf16)
        gate_ref[count:, :] = jnp.dot(spread, last, preferred_element_type=f32)
        out_row, in_row = iota((blocks, blocks * HELD), 0), iota((blocks, blocks * HELD), 1)
        peer, b = in_row // (ZL * HELD), in_row // HELD % ZL
        source = (zl - b + ZL) % ZL * PEERS + peer
        keep = (out_row == source) & (in_row % HELD == e)
        sort8_ref[...] = keep.astype(f32).astype(bf16)

    half = D // 2
    left, right = rows_ref[:, 0:half], rows_ref[:, half:]

    def times(near_ref, far_ref):
        return jnp.dot(
            left, near_ref[...].reshape(half, TILE), preferred_element_type=f32
        ) + jnp.dot(right, far_ref[...].reshape(half, TILE), preferred_element_type=f32)

    before = times(g0_ref, g1_ref)
    up = times(u0_ref, u1_ref)
    hidden = (before / (1.0 + jnp.exp(-before)) * up * gate_ref[...]).astype(bf16)
    main = jnp.dot(sort_ref[...], hidden[0:count], preferred_element_type=f32)
    out_ref[0, 0:MAIN] = main.astype(bf16).reshape(MAIN, blocks, TILE)
    last = jnp.dot(sort8_ref[...], hidden[count:], preferred_element_type=f32)
    out_ref[0, MAIN] = last.astype(bf16)


def experts(where, arrived, info, near, far):
    blocks = PEERS * ZL
    tiles = FF // TILE
    rows = blocks * (MAIN + HELD)
    gate = pl.BlockSpec((X, 1, D // 8, TILE), lambda e, n, w: (0, e, 0, n))
    up = pl.BlockSpec((X, 1, D // 8, TILE), lambda e, n, w: (0, e, 0, n + tiles))
    return pl.pallas_call(
        expert_kernel,
        grid_spec=pltpu.PrefetchScalarGridSpec(
            num_scalar_prefetch=1,
            grid=(HELD, tiles),
            in_specs=[
                pl.BlockSpec((PEERS, MSG, D), lambda e, n, w: (0, 0, 0)),
                pl.BlockSpec((TOP, blocks, INFO), lambda e, n, w: (0, 0, 0)),
                gate, gate, up, up,
            ],
            out_specs=pl.BlockSpec((1, CAP, blocks, TILE), lambda e, n, w: (e, 0, 0, n)),
            scratch_shapes=[
                pltpu.VMEM((rows, D), bf16),
                pltpu.VMEM((rows, TILE), f32),
                pltpu.VMEM((blocks * MAIN, blocks * MAIN), bf16),
                pltpu.VMEM((blocks, blocks * HELD), bf16),
            ],
        ),
        out_shape=jax.ShapeDtypeStruct((HELD, CAP, blocks, FF), bf16),
        compiler_params=pltpu.CompilerParams(vmem_limit_bytes=48 * 1024 * 1024),
        cost_estimate=pl.CostEstimate(
            flops=2 * HELD * rows * D * 2 * FF, bytes_accessed=20_000_000, transcendentals=10**6
        ),
    )(where, arrived, info, near, far, near, far)


def shards(moe_rows, expert_ids, expert_gates, expert_weights):
    zh, zl = lax.axis_index("zh"), lax.axis_index("zl")
    peer = lax.axis_index(("y", "c"))
    info = jnp.concatenate([expert_ids.T.astype(bf16), expert_gates.T], axis=1)
    packed = jnp.concatenate([moe_rows, jnp.pad(info, ((0, 0), (0, D - INFO)))], axis=0)
    blocks = [packed] + [
        lax.ppermute(packed, "zl", [(i, (i + b) % ZL) for i in range(ZL)]) for b in range(1, ZL)
    ]
    near = lax.all_gather(expert_weights, "x", axis=0)
    swapped = lax.ppermute(expert_weights, "zh", [(0, 1), (1, 0)])
    far = lax.all_gather(swapped, "x", axis=0)
    message = dispatch(zl.reshape(1), blocks)
    arrived = lax.all_to_all(message, ("y", "c"), split_axis=0, concat_axis=0, tiled=True)
    known = jnp.stack([block[TOK:, 0:INFO] for block in blocks], axis=1)
    known = lax.all_gather(known, ("y", "c"), axis=0)
    known = jnp.transpose(known, (1, 2, 0, 3)).reshape(TOP, ZL * PEERS, INFO)
    where = jnp.stack([zl, zh, (zl * PEERS + peer) * HELD])
    hidden = experts(where, arrived, known, near, far)
    return jnp.transpose(hidden, (0, 2, 1, 3))[None]


def solution(mesh):
    inner = Mesh(mesh.devices.reshape(ZH, X, ZL, Y, C), ("zh", "x", "zl", "y", "c"))
    tokens = P(("zh", "x", "zl", "y", "c"), None)
    in_specs = (tokens, tokens, tokens, P(("zl", "y", "c"), ("zh", "x"), None))
    out_specs = P(("zh", "x"), ("zl", "y", "c"), None, None, None)
    return jax.shard_map(
        shards, mesh=inner, in_specs=in_specs, out_specs=out_specs, check_vma=False
    )
```

time: 384 us -> 288 us (0.75)
  the two profiles are of different devices: /device:TPU:216 before, /device:TPU:69 now
where the time goes in v1:
time: 288 us
  blocking collectives  116 us (40%)
  waiting for transfers between devices  108 us (38%)
  starting transfers between devices  26.6 us (9%)
  Pallas kernels  21 us (7%)
  between operations  13.5 us (5%)
    all_gather x1, blocking collectives, shards(): known = lax.all_gather(known, ('y', 'c'), axis=0)  116 us
    ppermute x1, waiting for transfers between devices, shards(): swapped = lax.ppermute(expert_weights, 'zh', [(0, 1), (1, 0)])  69.9 us
    ppermute x3, waiting for transfers between devices, shards(): lax.ppermute(packed, 'zl', [(i, (i + b) % ZL) for i in range(ZL)])  37.7 us
    pallas_call x1, Pallas kernels, experts(): pl.pallas_call(expert_kernel, grid_spec=pltpu.PrefetchScalarGridSpec(num_...  17.8 us
    ppermute x1, starting transfers between devices, shards(): swapped = lax.ppermute(expert_weights, 'zh', [(0, 1), (1, 0)])  9.74 us
    ppermute x3, starting transfers between devices, shards(): lax.ppermute(packed, 'zl', [(i, (i + b) % ZL) for i in range(ZL)])  9.29 us
    all_to_all x1, starting transfers between devices, shards(): lax.all_to_all(message, ('y', 'c'), split_axis=0, concat_axis=0, tiled=True)  7.52 us
  transfers between devices with their start and end apart: 7, of which 4 were waited for; matrix products, arithmetic and copies ran while one was open for 0% of the time, Pallas kernels for 1%

profile of v1, /device:TPU:69, one launch (start us, length us, event | category | flops | bytes accessed | tf_op | source)
XLA Modules:
  0.0 288.2 jit_solution(17785878631493573268)
XLA Ops:
  6.5 0.0 copy-start.2
  6.5 0.0 copy-start.3
  6.5 0.0 copy-start.1
  6.5 0.0 all-gather.6.cloned.1.call-start
  6.5 0.7 all-gather.6.cloned.1.call-update
  7.3 0.0 all-gather.8.cloned.1.call-start
  7.3 9.7 %collective-permute-start.3 = (bf16[2,256,1536]{2,1,0:T(8,128)(2,1)}, bf16[2,256,1536]{2,1,0:T(8,128)(2,1)}, u32[]{:S(2)}, u32[]{:S(2)}) collective-permute-start(bf16[2,256,1536]{2,1,0:T(8,128)(2,1)} %param.7), channel_id=1, source_target_pairs={{0,256},{256,0},{1,257},{257,1},{2,258},{258,2},{3,259},{259,3},{4... | collective-permute-start | bytes 4718600 | tf_op jit(solution)/shard_map/ppermute | solution.py:234
  17.1 0.0 copy-done.2
  17.1 0.0 copy-done.3
  17.1 0.0 copy-done.1
  17.2 3.1 %collective-permute-start = (bf16[136,2048]{1,0:T(8,128)(2,1)S(1)}, bf16[136,2048]{1,0:T(8,128)(2,1)S(1)}, u32[]{:S(2)}, u32[]{:S(2)}) collective-permute-start(bf16[136,2048]{1,0:T(8,128)(2,1)S(1)} %fusion.1.refs_0_), channel_id=1, source_target_pairs={{0,16},{16,32},{32,48},{48,0},{1,17},{17,33},{33,49},{49,1},{2,18}... | collective-permute-start | bytes 1671176 | tf_op jit(solution)/shard_map/ppermute | solution.py:231
  20.3 3.1 %collective-permute-start.1 = (bf16[136,2048]{1,0:T(8,128)(2,1)S(1)}, bf16[136,2048]{1,0:T(8,128)(2,1)S(1)}, u32[]{:S(2)}, u32[]{:S(2)}) collective-permute-start(bf16[136,2048]{1,0:T(8,128)(2,1)S(1)} %fusion.1.refs_0_), channel_id=1, source_target_pairs={{0,32},{16,48},{32,0},{48,16},{1,33},{17,49},{33,1},{49,17},{2,34}... | collective-permute-start | bytes 1671176 | tf_op jit(solution)/shard_map/ppermute | solution.py:231
  23.3 3.1 %collective-permute-start.2 = (bf16[136,2048]{1,0:T(8,128)(2,1)S(1)}, bf16[136,2048]{1,0:T(8,128)(2,1)S(1)}, u32[]{:S(2)}, u32[]{:S(2)}) collective-permute-start(bf16[136,2048]{1,0:T(8,128)(2,1)S(1)} %fusion.1.refs_0_), channel_id=1, source_target_pairs={{0,48},{16,0},{32,16},{48,32},{1,49},{17,1},{33,17},{49,33},{2,50}... | collective-permute-start | bytes 1671176 | tf_op jit(solution)/shard_map/ppermute | solution.py:231
  26.5 69.9 %collective-permute-done.3 = bf16[2,256,1536]{2,1,0:T(8,128)(2,1)} collective-permute-done((bf16[2,256,1536]{2,1,0:T(8,128)(2,1)}, bf16[2,256,1536]{2,1,0:T(8,128)(2,1)}, u32[]{:S(2)}, u32[]{:S(2)}) %collective-permute-start.3) | collective-permute-done | bytes 1572896 | tf_op jit(solution)/shard_map/ppermute | solution.py:234
  96.4 0.0 all-gather.8.cloned.1.call-update
  96.4 1.0 collective-permute-done.refs_1_
  97.4 35.4 %collective-permute-done.1.refs_2_ = bf16[136,2048]{1,0:T(8,128)(2,1)S(1)} collective-permute-done((bf16[136,2048]{1,0:T(8,128)(2,1)S(1)}, bf16[136,2048]{1,0:T(8,128)(2,1)S(1)}, u32[]{:S(2)}, u32[]{:S(2)}) %collective-permute-start.1) | collective-permute-done | bytes 557088 | tf_op jit(solution)/shard_map/ppermute | solution.py:231
  132.8 1.3 collective-permute-done.2.refs_3_
  134.1 3.2 %shard_map.46 = bf16[16,72,2048]{2,1,0:T(8,128)(2,1)S(1)} custom-call(s32[1]{0:T(128)} %bitcast.zl_ref, bf16[136,2048]{1,0:T(8,128)(2,1)S(1)} %fusion.1.refs_0_, bf16[136,2048]{1,0:T(8,128)(2,1)S(1)} %collective-permute-done.refs_1_, bf16[136,2048]{1,0:T(8,128)(2,1)S(1)} %collective-permute-done.1.refs_2_, bf16[136,2048]{1,0:T(8,128)(2,1)S(1)} %collective-permute-done.2.refs_3_), custom_call_target="tpu_custom_call" | custom-call | flops 805306368 | bytes 7000000 | tf_op jit(solution)/shard_map/pallas_call | solution.py:81
  137.3 0.0 copy-start
  137.3 2.1 copy-done
  139.4 7.5 %all-to-all-start = ((bf16[16,72,2048]{2,1,0:T(8,128)(2,1)}), bf16[16,72,2048]{2,1,0:T(8,128)(2,1)}, u32[]{:S(2)}, u32[]{:S(2)}) async-start(bf16[16,72,2048]{2,1,0:T(8,128)(2,1)} %copy-done), calls=%async_computation | async-start | bytes 9437184 | tf_op jit(solution)/shard_map/all_to_all | solution.py:237
  147.0 0.1 pad_add_fusion.where_ref
  147.1 116.4 %all-gather = bf16[128,4,256]{2,0,1:T(8,128)(2,1)S(1)} all-gather(bf16[8,4,256]{2,0,1:T(8,128)(2,1)S(1)} %pad_maximum_fusion), channel_id=2, replica_groups=mesh['zh'=2,'x'=4,'zl'=4,'y'=8,'c'=2] {'y','c'}, dimensions={0}, use_global_device_ids=true | all-gather | bytes 278528 | tf_op jit(solution)/shard_map/all_gather | solution.py:239
  263.5 0.0 all-to-all-done.x_ref
  263.5 0.0 all-gather.6.cloned.1.call-done
  263.5 0.0 all-gather.8.cloned.1.call-done
  263.6 17.8 %shard_map.47 = bf16[2,9,64,768]{3,2,1,0:T(8,128)(2,1)} custom-call(s32[3]{0:T(128)S(1)} %pad_add_fusion.where_ref, bf16[16,72,2048]{2,1,0:T(8,128)(2,1)} %all-to-all-done.x_ref, bf16[8,64,256]{2,1,0:T(8,128)(2,1)S(1)} %bitcast.23, bf16[4,2,256,1536]{3,2,1,0:T(8,128)(2,1)} %bitcast.24, bf16[4,2,256,1536]{3,2,1,0:T(8,128)(2,1)} %bitcast.26, ...), custom_call_target="tpu_custom_call" | custom-call | flops 8053063680 | bytes 20000000 | tf_op jit(solution)/shard_map/pallas_call | solution.py:199
  (8 shorter events, 0.1 us)
Async XLA Ops:
  6.5 10.5 %copy-start.2 = (s32[128,8]{0,1:T(8,128)S(1)}, s32[128,8]{0,1:T(8,128)}, u32[]{:S(2)}) copy-start(s32[128,8]{0,1:T(8,128)} %param.5) | copy-start | bytes 12292
  6.5 10.5 %copy-start.3 = (bf16[128,8]{0,1:T(8,128)(2,1)S(1)}, bf16[128,8]{0,1:T(8,128)(2,1)}, u32[]{:S(2)}) copy-start(bf16[128,8]{0,1:T(8,128)(2,1)} %param.6) | copy-start | bytes 6148
  6.5 10.6 %copy-start.1 = (bf16[128,2048]{1,0:T(8,128)(2,1)S(1)}, bf16[128,2048]{1,0:T(8,128)(2,1)}, u32[]{:S(2)}) copy-start(bf16[128,2048]{1,0:T(8,128)(2,1)} %param.4) | copy-start | bytes 1572868
  6.5 257.0 %all-gather.6.cloned.1.call-start = ((), (), s32[]{:S(2)}) async-start(), calls=%async_computation.1 | async-start | bytes 7864320 | tf_op jit(solution)/shard_map/all_gather | solution.py:233
  7.3 256.3 %all-gather.8.cloned.1.call-start = ((), (), s32[]{:S(2)}) async-start(), calls=%async_computation.2 | async-start | bytes 7864320 | tf_op jit(solution)/shard_map/all_gather | solution.py:235
  7.3 89.1 %collective-permute-start.3 = (bf16[2,256,1536]{2,1,0:T(8,128)(2,1)}, bf16[2,256,1536]{2,1,0:T(8,128)(2,1)}, u32[]{:S(2)}, u32[]{:S(2)}) collective-permute-start(bf16[2,256,1536]{2,1,0:T(8,128)(2,1)} %param.7), channel_id=1, source_target_pairs={{0,256},{256,0},{1,257},{257,1},{2,258},{258,2},{3,259},{259,3},{4... | collective-permute-start | bytes 4718600 | tf_op jit(solution)/shard_map/ppermute | solution.py:234
  17.2 80.2 %collective-permute-start = (bf16[136,2048]{1,0:T(8,128)(2,1)S(1)}, bf16[136,2048]{1,0:T(8,128)(2,1)S(1)}, u32[]{:S(2)}, u32[]{:S(2)}) collective-permute-start(bf16[136,2048]{1,0:T(8,128)(2,1)S(1)} %fusion.1.refs_0_), channel_id=1, source_target_pairs={{0,16},{16,32},{32,48},{48,0},{1,17},{17,33},{33,49},{49,1},{2,18}... | collective-permute-start | bytes 1671176 | tf_op jit(solution)/shard_map/ppermute | solution.py:231
  20.3 112.5 %collective-permute-start.1 = (bf16[136,2048]{1,0:T(8,128)(2,1)S(1)}, bf16[136,2048]{1,0:T(8,128)(2,1)S(1)}, u32[]{:S(2)}, u32[]{:S(2)}) collective-permute-start(bf16[136,2048]{1,0:T(8,128)(2,1)S(1)} %fusion.1.refs_0_), channel_id=1, source_target_pairs={{0,32},{16,48},{32,0},{48,16},{1,33},{17,49},{33,1},{49,17},{2,34}... | collective-permute-start | bytes 1671176 | tf_op jit(solution)/shard_map/ppermute | solution.py:231
  23.3 110.8 %collective-permute-start.2 = (bf16[136,2048]{1,0:T(8,128)(2,1)S(1)}, bf16[136,2048]{1,0:T(8,128)(2,1)S(1)}, u32[]{:S(2)}, u32[]{:S(2)}) collective-permute-start(bf16[136,2048]{1,0:T(8,128)(2,1)S(1)} %fusion.1.refs_0_), channel_id=1, source_target_pairs={{0,48},{16,0},{32,16},{48,32},{1,49},{17,1},{33,17},{49,33},{2,50}... | collective-permute-start | bytes 1671176 | tf_op jit(solution)/shard_map/ppermute | solution.py:231
  137.3 2.1 copy-start
  139.4 124.1 %all-to-all-start = ((bf16[16,72,2048]{2,1,0:T(8,128)(2,1)}), bf16[16,72,2048]{2,1,0:T(8,128)(2,1)}, u32[]{:S(2)}, u32[]{:S(2)}) async-start(bf16[16,72,2048]{2,1,0:T(8,128)(2,1)} %copy-done), calls=%async_computation | async-start | bytes 9437184 | tf_op jit(solution)/shard_map/all_to_all | solution.py:237
Sparse Core Ops, SparseCore 0:
  9.5 74.2 all-gather.5
  96.5 74.2 all-gather.7

commit v2 on v1

v2 whole, which is shorter than its diff:
```python
import jax
import jax.numpy as jnp
from jax import lax
from jax.experimental import pallas as pl
from jax.experimental.pallas import tpu as pltpu
from jax.sharding import Mesh, PartitionSpec as P

ZH, X, ZL, Y, C = 2, 4, 4, 8, 2
PEERS = Y * C
HELD = 2
CAP = 9
MAIN = CAP - 1
TOP = 8
TOK = 128
D = 2048
FF = 768
KEPT = PEERS * HELD
LEFT = (ZL - 1) * HELD
COLS = 512
TILE = 256
INFO = 2 * TOK

f32 = jnp.float32
bf16 = jnp.bfloat16


def iota(shape, dim):
    return lax.broadcasted_iota(jnp.int32, shape, dim)


def earlier():
    return (iota((TOK, TOK), 0) < iota((TOK, TOK), 1)).astype(bf16)


def named(ids, experts):
    hit = (ids[0:1, :] == experts).astype(f32)
    for k in range(1, TOP):
        hit = hit + (ids[k : k + 1, :] == experts).astype(f32)
    return hit


def chosen_rows(ids, first):
    kept = (iota((KEPT, TOK), 0) + first).astype(f32)
    hit = named(ids, kept)
    rank = jnp.dot(hit.astype(bf16), earlier(), preferred_element_type=f32)
    place = jnp.where(hit > 0, rank, -1.0)
    slot = iota((KEPT, MAIN, TOK), 1).astype(f32)
    chosen = (place[:, None, :] == slot).astype(f32)
    return chosen.reshape(KEPT * MAIN, TOK).astype(bf16)


def moved_rows(chosen, rows):
    moved = jnp.dot(chosen, rows, preferred_element_type=f32).astype(bf16)
    return moved.reshape(PEERS, HELD, MAIN, rows.shape[1])


def ids_of(block):
    return block[TOK : TOK + TOP, 0:TOK].astype(f32)


def own_kernel(zl_ref, block, out_ref, main_ref):
    @pl.when(pl.program_id(0) == 0)
    def _():
        main_ref[...] = chosen_rows(ids_of(block), zl_ref[0] * KEPT)

    out_ref[:, 0:HELD] = moved_rows(main_ref[...], block[0:TOK, :])
    info = block[TOK : TOK + TOP, :]
    out_ref[:, HELD] = jnp.broadcast_to(info[None], (PEERS,) + info.shape)


def rest_kernel(zl_ref, *refs):
    blocks, out_ref, main_ref, tail_ref = refs[:ZL], refs[ZL], refs[ZL + 1], refs[ZL + 2]

    @pl.when(pl.program_id(0) == 0)
    def _():
        first = zl_ref[0] * KEPT
        row = iota((PEERS * ZL * HELD, TOK), 0)
        ending = (first + row // (ZL * HELD) * HELD + row % HELD).astype(f32)
        for b in range(ZL):
            ids = ids_of(blocks[b])
            if b:
                main_ref[b - 1] = chosen_rows(ids, first)
            hit = jnp.where(row // HELD % ZL == b, named(ids, ending), 0.0)
            rank = jnp.dot(hit.astype(bf16), earlier(), preferred_element_type=f32)
            tail_ref[b] = jnp.where(rank == MAIN, hit, 0.0).astype(bf16)

    width = out_ref.shape[3]
    last = jnp.zeros((PEERS * ZL * HELD, width), f32)
    for b in range(ZL):
        rows = blocks[b][0:TOK, :]
        if b:
            moved = moved_rows(main_ref[b - 1], rows)
            for e in range(HELD):
                out_ref[:, e * (ZL - 1) + b - 1] = moved[:, e]
        last = last + jnp.dot(tail_ref[b], rows, preferred_element_type=f32)
    out_ref[:, LEFT] = last.astype(bf16).reshape(PEERS, ZL * HELD, width)


def dispatch(kernel, tiles, scratch, zl, blocks):
    return pl.pallas_call(
        kernel,
        grid_spec=pltpu.PrefetchScalarGridSpec(
            num_scalar_prefetch=1,
            grid=(D // COLS,),
            in_specs=[pl.BlockSpec((TOK + TOP, COLS), lambda n, z: (0, n))] * len(blocks),
            out_specs=pl.BlockSpec((PEERS, tiles, MAIN, COLS), lambda n, z: (0, 0, 0, n)),
            scratch_shapes=scratch,
        ),
        out_shape=jax.ShapeDtypeStruct((PEERS, tiles, MAIN, D), bf16),
        compiler_params=pltpu.CompilerParams(vmem_limit_bytes=40 * 1024 * 1024),
        cost_estimate=pl.CostEstimate(
            flops=2 * len(blocks) * 384 * TOK * D,
            bytes_accessed=PEERS * tiles * MAIN * D * 2,
            transcendentals=0,
        ),
    )(zl, *blocks)


def plan_kernel(where_ref, info_ref, gate_ref, sort_ref, sort8_ref):
    blocks = PEERS * ZL
    count = blocks * MAIN
    near_rows = PEERS * MAIN
    rest = (ZL - 1) * MAIN
    zl, first = where_ref[0], where_ref[2]
    out_row, in_row = iota((count, count), 0), iota((count, count), 1)
    late = in_row - near_rows
    peer = jnp.where(late >= 0, late // rest, in_row // MAIN)
    b = jnp.where(late >= 0, late % rest // MAIN + 1, 0)
    source = (zl - b + ZL) % ZL * PEERS + peer
    sort_ref[...] = (out_row == in_row % MAIN * blocks + source).astype(f32).astype(bf16)
    ones = jnp.ones((TOK, TILE), bf16)
    for e in range(HELD):
        expert = (first + e).astype(f32)
        hit = jnp.zeros((blocks, TOK), f32)
        gate = jnp.zeros((blocks, TOK), f32)
        for k in range(TOP):
            same = info_ref[k, :, 0:TOK].astype(f32) == expert
            hit = hit + same.astype(f32)
            gate = gate + jnp.where(same, info_ref[k, :, TOK:INFO].astype(f32), 0.0)
        rank = jnp.dot(hit.astype(bf16), earlier(), preferred_element_type=f32)
        slot = iota((blocks, MAIN, TOK), 1).astype(f32)
        chosen = jnp.where(rank[:, None, :] == slot, gate[:, None, :], 0.0)
        chosen = chosen.reshape(ZL, near_rows, TOK)
        gate_ref[e, 0:near_rows, :] = jnp.dot(
            chosen[0].astype(bf16), ones, preferred_element_type=f32
        )
        others = jnp.concatenate(
            [chosen[b].reshape(PEERS, MAIN, TOK) for b in range(1, ZL)], axis=1
        ).reshape(PEERS * rest, TOK)
        gate_ref[e, near_rows:count, :] = jnp.dot(
            others.astype(bf16), ones, preferred_element_type=f32
        )
        last = jnp.where(rank == MAIN, gate, 0.0).astype(bf16)
        last = jnp.dot(last, ones, preferred_element_type=f32).astype(bf16)
        row, col = iota((blocks * HELD, blocks), 0), iota((blocks * HELD, blocks), 1)
        spread = (col == row // HELD % ZL * PEERS + row // (ZL * HELD)).astype(f32).astype(bf16)
        gate_ref[e, count:, :] = jnp.dot(spread, last, preferred_element_type=f32)
        out_row, in_row = iota((blocks, blocks * HELD), 0), iota((blocks, blocks * HELD), 1)
        source = (zl - in_row // HELD % ZL + ZL) % ZL * PEERS + in_row // (ZL * HELD)
        keep = (out_row == source) & (in_row % HELD == e)
        sort8_ref[e] = keep.astype(f32).astype(bf16)


def plan(where, info):
    blocks = PEERS * ZL
    rows = blocks * (MAIN + HELD)
    shapes = [
        jax.ShapeDtypeStruct((HELD, rows, TILE), f32),
        jax.ShapeDtypeStruct((blocks * MAIN, blocks * MAIN), bf16),
        jax.ShapeDtypeStruct((HELD, blocks, blocks * HELD), bf16),
    ]
    return pl.pallas_call(
        plan_kernel,
        grid_spec=pltpu.PrefetchScalarGridSpec(
            num_scalar_prefetch=1,
            grid=(1,),
            in_specs=[pl.BlockSpec(info.shape, lambda n, w: (0, 0, 0))],
            out_specs=[
                pl.BlockSpec(s.shape, lambda n, w, r=len(s.shape): (0,) * r) for s in shapes
            ],
        ),
        out_shape=shapes,
        compiler_params=pltpu.CompilerParams(vmem_limit_bytes=32 * 1024 * 1024),
        cost_estimate=pl.CostEstimate(flops=10**8, bytes_accessed=10**6, transcendentals=0),
    )(where, info)


def gather_rows(rows_ref, own_ref, rest_ref, last_ref):
    at = 0
    for ref in (own_ref, rest_ref, last_ref):
        count = ref.shape[0] * ref.shape[1] * ref.shape[2]
        rows_ref[at : at + count, :] = ref[...].reshape(count, ref.shape[3])
        at += count


def near_kernel(where_ref, own_ref, rest_ref, last_ref, weights_ref, out_ref, rows_ref):
    @pl.when(pl.program_id(1) == 0)
    def _():
        gather_rows(rows_ref, own_ref, rest_ref, last_ref)

    weights = weights_ref[...].reshape(D // 2, weights_ref.shape[3])
    out_ref[0] = jnp.dot(rows_ref[...], weights, preferred_element_type=f32)


def near_part(where, own, rest, near):
    rows, half, tile = PEERS * ZL * (MAIN + HELD), D // 2, 2 * TILE
    return pl.pallas_call(
        near_kernel,
        grid_spec=pltpu.PrefetchScalarGridSpec(
            num_scalar_prefetch=1,
            grid=(HELD, 2 * FF // tile),
            in_specs=[
                pl.BlockSpec((PEERS, 1, MAIN, half), lambda e, n, w: (0, e, 0, w[1])),
                pl.BlockSpec((PEERS, ZL - 1, MAIN, half), lambda e, n, w: (0, e, 0, w[1])),
                pl.BlockSpec((PEERS, 1, MAIN, half), lambda e, n, w: (0, LEFT, 0, w[1])),
                pl.BlockSpec((X, 1, D // 8, tile), lambda e, n, w: (0, e, 0, n)),
            ],
            out_specs=pl.BlockSpec((1, rows, tile), lambda e, n, w: (e, 0, n)),
            scratch_shapes=[pltpu.VMEM((rows, half), bf16)],
        ),
        out_shape=jax.ShapeDtypeStruct((HELD, rows, 2 * FF), f32),
        compiler_params=pltpu.CompilerParams(vmem_limit_bytes=40 * 1024 * 1024),
        cost_estimate=pl.CostEstimate(flops=10**11, bytes_accessed=10**7, transcendentals=0),
    )(where, own, rest, rest, near)


def expert_kernel(
    where_ref, own_ref, rest_ref, last_ref, gate_ref, sort_ref, sort8_ref,
    before_ref, up_ref, g_ref, u_ref, *refs,
):
    out_ref, rows_ref = refs[-2:]
    blocks = PEERS * ZL
    count = blocks * MAIN
    half = D // 2

    @pl.when(pl.program_id(0) == 0)
    def _():
        gather_rows(rows_ref, own_ref, rest_ref, last_ref)

    def added(sums_ref, weights_ref):
        weights = weights_ref[...].reshape(half, TILE)
        return sums_ref[0] + jnp.dot(rows_ref[...], weights, preferred_element_type=f32)

    before = added(before_ref, g_ref)
    up = added(up_ref, u_ref)
    hidden = (before / (1.0 + jnp.exp(-before)) * up * gate_ref[0]).astype(bf16)
    main = jnp.dot(sort_ref[...], hidden[0:count], preferred_element_type=f32)
    out_ref[0, 0:MAIN] = main.astype(bf16).reshape(MAIN, blocks, TILE)
    last = jnp.dot(sort8_ref[0], hidden[count:], preferred_element_type=f32)
    out_ref[0, MAIN] = last.astype(bf16)


def expert(e, where, own, rest, slots, sums, far, other=None):
    blocks = PEERS * ZL
    tiles = FF // TILE
    rows, half = blocks * (MAIN + HELD), D // 2
    gates, sort, sort8 = slots
    others = [] if other is None else [other]
    return pl.pallas_call(
        expert_kernel,
        grid_spec=pltpu.PrefetchScalarGridSpec(
            num_scalar_prefetch=1,
            grid=(tiles,),
            in_specs=[
                pl.BlockSpec((PEERS, 1, MAIN, half), lambda n, w: (0, e, 0, 1 - w[1])),
                pl.BlockSpec((PEERS, ZL - 1, MAIN, half), lambda n, w: (0, e, 0, 1 - w[1])),
                pl.BlockSpec((PEERS, 1, MAIN, half), lambda n, w: (0, LEFT, 0, 1 - w[1])),
                pl.BlockSpec((1, rows, TILE), lambda n, w: (e, 0, 0)),
                pl.BlockSpec(sort.shape, lambda n, w: (0, 0)),
                pl.BlockSpec((1,) + sort8.shape[1:], lambda n, w: (e, 0, 0)),
                pl.BlockSpec((1, rows, TILE), lambda n, w: (e, 0, n)),
                pl.BlockSpec((1, rows, TILE), lambda n, w: (e, 0, n + tiles)),
                pl.BlockSpec((X, D // 8, TILE), lambda n, w: (0, 0, n)),
                pl.BlockSpec((X, D // 8, TILE), lambda n, w: (0, 0, n + tiles)),
            ]
            + [pl.BlockSpec(memory_space=pl.ANY)] * len(others),
            out_specs=pl.BlockSpec((1, CAP, blocks, TILE), lambda n, w: (e, 0, 0, n)),
            scratch_shapes=[pltpu.VMEM((rows, half), bf16)],
        ),
        out_shape=jax.ShapeDtypeStruct((HELD, CAP, blocks, FF), bf16),
        input_output_aliases={11: 0} if others else {},
        compiler_params=pltpu.CompilerParams(vmem_limit_bytes=40 * 1024 * 1024),
        cost_estimate=pl.CostEstimate(
            flops=rows * D * 2 * FF, bytes_accessed=10_000_000, transcendentals=10**6
        ),
    )(where, own, rest, rest, gates, sort, sort8, sums, sums, far, far, *others)


def over_zl(block):
    return [block] + [
        lax.ppermute(block, "zl", [(i, (i + b) % ZL) for i in range(ZL)]) for b in range(1, ZL)
    ]


def over_peers(message):
    return lax.all_to_all(message, ("y", "c"), split_axis=0, concat_axis=0, tiled=True)


def take_kernel(*refs):
    refs[-1][...] = refs[0][0]


def marks(*values):
    return [
        lax.slice(v, (0,) * v.ndim, (1,) * (v.ndim - 2) + (8, TOK)).reshape(8, TOK) for v in values
    ]


def take(weights, e, *others):
    shape = weights.shape[1:]
    others = marks(*others)
    return pl.pallas_call(
        take_kernel,
        grid=(1,),
        in_specs=[pl.BlockSpec((1,) + shape, lambda n: (e, 0, 0))]
        + [pl.BlockSpec(memory_space=pl.ANY)] * len(others),
        out_specs=pl.BlockSpec(shape, lambda n: (0, 0)),
        out_shape=jax.ShapeDtypeStruct(shape, weights.dtype),
        cost_estimate=pl.CostEstimate(flops=0, bytes_accessed=1_600_000, transcendentals=0),
    )(weights, *others)


def pass_kernel(*refs):
    pass


def after(value, *others):
    others = marks(*others)
    return pl.pallas_call(
        pass_kernel,
        in_specs=[pl.BlockSpec(memory_space=pl.ANY)] * (1 + len(others)),
        out_specs=pl.BlockSpec(memory_space=pl.ANY),
        out_shape=jax.ShapeDtypeStruct(value.shape, value.dtype),
        input_output_aliases={0: 0},
    )(value, *others)


def shards(moe_rows, expert_ids, expert_gates, expert_weights):
    zh, zl = lax.axis_index("zh"), lax.axis_index("zl")
    peer = lax.axis_index(("y", "c"))
    where = jnp.stack([zl, zh, (zl * PEERS + peer) * HELD])
    info = jnp.concatenate([expert_ids.T.astype(bf16), expert_gates.T], axis=1)
    packed = jnp.concatenate([moe_rows, jnp.pad(info, ((0, 0), (0, D - INFO)))], axis=0)
    near = lax.all_gather(expert_weights, "x", axis=0)
    blocks = over_zl(packed)
    picked = pltpu.VMEM((KEPT * MAIN, TOK), bf16)
    own = over_peers(dispatch(own_kernel, HELD + 1, [picked], zl.reshape(1), [packed]))
    scratch = [
        pltpu.VMEM((ZL - 1, KEPT * MAIN, TOK), bf16),
        pltpu.VMEM((ZL, PEERS * ZL * HELD, TOK), bf16),
    ]
    message = dispatch(rest_kernel, LEFT + 1, scratch, zl.reshape(1), blocks)
    rest = over_peers(message)
    swap = [(0, 1), (1, 0)]
    first = lax.ppermute(take(expert_weights, 0, own, message), "zh", swap)
    second = lax.ppermute(take(expert_weights, 1, first), "zh", swap)
    far = [lax.all_gather(after(first, near), "x", axis=0), lax.all_gather(second, "x", axis=0)]
    known = jnp.stack(over_zl(own[:, HELD, :, 0:INFO]))
    known = jnp.transpose(known, (2, 0, 1, 3)).reshape(TOP, ZL * PEERS, INFO)
    slots = plan(where, known)
    sums = near_part(where, own, rest, near)
    hidden = expert(0, where, own, rest, slots, sums, far[0])
    hidden = expert(1, where, own, rest, slots, sums, far[1], hidden)
    return jnp.transpose(hidden, (0, 2, 1, 3))[None]


def solution(mesh):
    inner = Mesh(mesh.devices.reshape(ZH, X, ZL, Y, C), ("zh", "x", "zl", "y", "c"))
    tokens = P(("zh", "x", "zl", "y", "c"), None)
    in_specs = (tokens, tokens, tokens, P(("zl", "y", "c"), ("zh", "x"), None))
    out_specs = P(("zh", "x"), ("zl", "y", "c"), None, None, None)
    return jax.shard_map(
        shards, mesh=inner, in_specs=in_specs, out_specs=out_specs, check_vma=False
    )
```

time: 288 us -> 247 us (0.86)
  the two profiles are of different devices: /device:TPU:69 before, /device:TPU:1 now
where the time goes in v2:
time: 247 us; the launch traced here: 246 us
  waiting for transfers between devices  105 us (43%)
  starting transfers between devices  79.6 us (32%)
  Pallas kernels  34.4 us (14%)
  between operations  13.3 us (5%)
  local copies, waits for them, and re-layouts  12.2 us (5%)
    ppermute x6, waiting for transfers between devices, over_zl(): lax.ppermute(block, 'zl', [(i, (i + b) % ZL) for i in range(ZL)])  56.9 us
    ppermute x6, starting transfers between devices, over_zl(): lax.ppermute(block, 'zl', [(i, (i + b) % ZL) for i in range(ZL)])  46.6 us
    all_gather x1, waiting for transfers between devices, shards(): lax.all_gather(second, 'x', axis=0)  29.7 us
    ppermute x1, waiting for transfers between devices, shards(): first = lax.ppermute(take(expert_weights, 0, own, message), 'zh', swap)  18.1 us
    all_to_all x2, starting transfers between devices, over_peers(): lax.all_to_all(message, ('y', 'c'), split_axis=0, concat_axis=0, tiled=True)  17.7 us
    pallas_call x2, Pallas kernels, expert(): pl.pallas_call(expert_kernel, grid_spec=pltpu.PrefetchScalarGridSpec(num_...  14.3 us
    pallas_call x1, Pallas kernels, near_part(): pl.pallas_call(near_kernel, grid_spec=pltpu.PrefetchScalarGridSpec(num_sc...  9.3 us
    unnamed x12, local copies, waits for them, and re-layouts  8.49 us
  transfers between devices with their start and end apart: 13, of which 6 were waited for; matrix products, arithmetic and copies ran while one was open for 2% of the time, Pallas kernels for 11%

profile of v2, /device:TPU:1, one launch (start us, length us, event | category | flops | bytes accessed | tf_op | source)
XLA Modules:
  0.0 246.5 jit_solution(16589503283550901818)
XLA Ops:
  6.5 0.0 copy-start.5
  6.5 0.0 all-gather.7.cloned.1.call-start
  6.5 0.7 all-gather.7.cloned.1.call-update
  7.3 0.7 convert_bitcast_fusion
  8.0 0.7 fusion.2
  8.6 0.0 copy-done.5
  8.7 2.4 shard_map.46
  11.1 10.4 %all-to-all-start = ((bf16[16,3,8,2048]{3,2,1,0:T(8,128)(2,1)}), bf16[16,3,8,2048]{3,2,1,0:T(8,128)(2,1)S(1)}, u32[]{:S(2)}, u32[]{:S(2)}) async-start(bf16[16,3,8,2048]{3,2,1,0:T(8,128)(2,1)} %shard_map.46), calls=%async_computation | async-start | bytes 3145728 | tf_op jit(solution)/shard_map/all_to_all | solution.py:296
  21.4 2.3 collective-permute-start
  23.7 5.8 %collective-permute-start.1 = (bf16[136,2048]{1,0:T(8,128)(2,1)S(1)}, bf16[136,2048]{1,0:T(8,128)(2,1)S(1)}, u32[]{:S(2)}, u32[]{:S(2)}) collective-permute-start(bf16[136,2048]{1,0:T(8,128)(2,1)S(1)} %pad_maximum_fusion.block.refs_0_), channel_id=1, source_target_pairs={{0,32},{16,48},{32,0},{48,16},{1,33},{17,49},{33,1},{49,17},{2,34}... | collective-permute-start | bytes 1671176 | tf_op jit(solution)/shard_map/ppermute | solution.py:291
  29.5 2.2 collective-permute-start.2
  31.7 8.5 %collective-permute-done.refs_1_ = bf16[136,2048]{1,0:T(8,128)(2,1)S(1)} collective-permute-done((bf16[136,2048]{1,0:T(8,128)(2,1)S(1)}, bf16[136,2048]{1,0:T(8,128)(2,1)S(1)}, u32[]{:S(2)}, u32[]{:S(2)}) %collective-permute-start) | collective-permute-done | bytes 557088 | tf_op jit(solution)/shard_map/ppermute | solution.py:291
  40.2 24.2 %collective-permute-done.1.refs_2_ = bf16[136,2048]{1,0:T(8,128)(2,1)S(1)} collective-permute-done((bf16[136,2048]{1,0:T(8,128)(2,1)S(1)}, bf16[136,2048]{1,0:T(8,128)(2,1)S(1)}, u32[]{:S(2)}, u32[]{:S(2)}) %collective-permute-start.1) | collective-permute-done | bytes 557088 | tf_op jit(solution)/shard_map/ppermute | solution.py:291
  64.4 0.0 collective-permute-done.2.refs_3_
  64.4 2.8 %shard_map.47 = bf16[16,7,8,2048]{3,2,1,0:T(8,128)(2,1)S(1)} custom-call(s32[1]{0:T(128)} %bitcast.zl_ref, bf16[136,2048]{1,0:T(8,128)(2,1)S(1)} %pad_maximum_fusion.block.refs_0_, bf16[136,2048]{1,0:T(8,128)(2,1)S(1)} %collective-permute-done.refs_1_, bf16[136,2048]{1,0:T(8,128)(2,1)S(1)} %collective-permute-done.1.refs_2_, ...), custom_call_target="tpu_custom_call" | custom-call | flops 805306368 | bytes 3670016 | tf_op jit(solution)/shard_map/pallas_call | solution.py:100
  67.3 0.0 copy-start
  67.3 1.9 copy-done
  69.2 0.0 all-to-all-done.own_ref
  69.2 7.3 %all-to-all-start.1 = ((bf16[16,7,8,2048]{3,2,1,0:T(8,128)(2,1)}), bf16[16,7,8,2048]{3,2,1,0:T(8,128)(2,1)}, u32[]{:S(2)}, u32[]{:S(2)}) async-start(bf16[16,7,8,2048]{3,2,1,0:T(8,128)(2,1)} %copy-done), calls=%async_computation.1 | async-start | bytes 7340032 | tf_op jit(solution)/shard_map/all_to_all | solution.py:296
  76.5 1.2 slice_bitcast_fusion.3.refs_2_
  77.7 0.6 slice_bitcast_fusion.4.refs_1_
  78.3 2.1 shard_map.50
  80.4 8.2 %collective-permute-start.6 = (bf16[256,1536]{1,0:T(8,128)(2,1)}, bf16[256,1536]{1,0:T(8,128)(2,1)S(1)}, u32[]{:S(2)}, u32[]{:S(2)}) collective-permute-start(bf16[256,1536]{1,0:T(8,128)(2,1)} %shard_map.50), channel_id=1, source_target_pairs={{0,256},{256,0},{1,257},{257,1},{2,258},{258,2},{3,259},{259,3},{4... | collective-permute-start | bytes 2359304 | tf_op jit(solution)/shard_map/ppermute | solution.py:355
  88.5 18.1 %collective-permute-done.6.refs_0_ = bf16[256,1536]{1,0:T(8,128)(2,1)S(1)} collective-permute-done((bf16[256,1536]{1,0:T(8,128)(2,1)}, bf16[256,1536]{1,0:T(8,128)(2,1)S(1)}, u32[]{:S(2)}, u32[]{:S(2)}) %collective-permute-start.6) | collective-permute-done | bytes 786464 | tf_op jit(solution)/shard_map/ppermute | solution.py:355
  106.6 0.0 copy-start.4
  106.6 0.6 slice.23.refs_1_
  107.3 0.0 all-gather.11.cloned.1.call-start
  107.3 0.0 all-gather.7.cloned.1.call-done
  107.3 1.3 slice_bitcast_fusion.2.refs_1_
  108.5 0.0 copy-done.4
  108.5 0.0 all-gather.11.cloned.1.call-update
  108.5 0.0 all-gather.9.cloned.1.call-start
  108.6 2.1 shard_map.51
  110.7 7.1 %collective-permute-start.7 = (bf16[256,1536]{1,0:T(8,128)(2,1)}, bf16[256,1536]{1,0:T(8,128)(2,1)}, u32[]{:S(2)}, u32[]{:S(2)}) collective-permute-start(bf16[256,1536]{1,0:T(8,128)(2,1)} %shard_map.51), channel_id=1, source_target_pairs={{0,256},{256,0},{1,257},{257,1},{2,258},{258,2},{3,259},{259,3},{4... | collective-permute-start | bytes 2359304 | tf_op jit(solution)/shard_map/ppermute | solution.py:356
  117.8 30.4 %collective-permute-start.3 = (bf16[16,8,256]{2,1,0:T(8,128)(2,1)S(1)}, bf16[16,8,256]{2,1,0:T(8,128)(2,1)S(1)}, u32[]{:S(2)}, u32[]{:S(2)}) collective-permute-start(bf16[16,8,256]{2,1,0:T(8,128)(2,1)S(1)} %get-tuple-element.12), channel_id=1, source_target_pairs={{0,16},{16,32},{32,48},{48,0},{1,17},{17,33},{33,49},{49,1},{2,18}... | collective-permute-start | bytes 196616 | tf_op jit(solution)/shard_map/ppermute | solution.py:291
  148.2 1.9 collective-permute-start.4
  150.1 4.0 %collective-permute-start.5 = (bf16[16,8,256]{2,1,0:T(8,128)(2,1)S(1)}, bf16[16,8,256]{2,1,0:T(8,128)(2,1)S(1)}, u32[]{:S(2)}, u32[]{:S(2)}) collective-permute-start(bf16[16,8,256]{2,1,0:T(8,128)(2,1)S(1)} %get-tuple-element.12), channel_id=1, source_target_pairs={{0,48},{16,0},{32,16},{48,32},{1,49},{17,1},{33,17},{49,33},{2,50}... | collective-permute-start | bytes 196616 | tf_op jit(solution)/shard_map/ppermute | solution.py:291
  154.1 0.1 pad_add_fusion.where_ref
  154.2 8.5 %collective-permute-done.3 = bf16[16,8,256]{2,1,0:T(8,128)(2,1)S(1)} collective-permute-done((bf16[16,8,256]{2,1,0:T(8,128)(2,1)S(1)}, bf16[16,8,256]{2,1,0:T(8,128)(2,1)S(1)}, u32[]{:S(2)}, u32[]{:S(2)}) %collective-permute-start.3) | collective-permute-done | bytes 65568 | tf_op jit(solution)/shard_map/ppermute | solution.py:291
  162.7 15.7 %collective-permute-done.4 = bf16[16,8,256]{2,1,0:T(8,128)(2,1)S(1)} collective-permute-done((bf16[16,8,256]{2,1,0:T(8,128)(2,1)S(1)}, bf16[16,8,256]{2,1,0:T(8,128)(2,1)S(1)}, u32[]{:S(2)}, u32[]{:S(2)}) %collective-permute-start.4) | collective-permute-done | bytes 65568 | tf_op jit(solution)/shard_map/ppermute | solution.py:291
  178.4 0.0 collective-permute-done.5
  178.5 1.6 shard_map.48
  180.1 0.0 collective-permute-done.7
  180.1 0.0 all-gather.9.cloned.1.call-update
  180.1 0.0 all-to-all-done.1.rest_ref.last_ref
  180.1 0.0 copy-start.3
  180.1 2.8 %copy-done.3 = bf16[8,256,1536]{2,1,0:T(8,128)(2,1)S(1)} copy-done((bf16[8,256,1536]{2,1,0:T(8,128)(2,1)S(1)}, bf16[8,256,1536]{2,1,0:T(8,128)(2,1)}, u32[]{:S(2)}) %copy-start.3) | copy-done | bytes 6291480
  182.9 9.3 %shard_map.49.before_ref.up_ref = f32[2,640,1536]{2,1,0:T(8,128)} custom-call(s32[3]{0:T(128)S(1)} %pad_add_fusion.where_ref, bf16[16,3,8,2048]{3,2,1,0:T(8,128)(2,1)S(1)} %all-to-all-done.own_ref, bf16[16,7,8,2048]{3,2,1,0:T(8,128)(2,1)} %all-to-all-done.1.rest_ref.last_ref, bf16[16,7,8,2048]{3,2,1,0:T(8,128)(2,1)} %all-to-all-done.1.rest_ref.last_ref, ...), custom_call_target="tpu_custom_call" | custom-call | flops 99999997952 | bytes 10000000 | tf_op jit(solution)/shard_map/pallas_call | solution.py:207
  192.2 0.0 all-gather.11.cloned.1.call-done
  192.2 0.0 copy-start.2
  192.2 1.9 copy-done.2
  194.1 7.1 %shard_map.53.refs_0_ = bf16[2,9,64,768]{3,2,1,0:T(8,128)(2,1)} custom-call(s32[3]{0:T(128)S(1)} %pad_add_fusion.where_ref, bf16[16,3,8,2048]{3,2,1,0:T(8,128)(2,1)S(1)} %all-to-all-done.own_ref, bf16[16,7,8,2048]{3,2,1,0:T(8,128)(2,1)} %all-to-all-done.1.rest_ref.last_ref, bf16[16,7,8,2048]{3,2,1,0:T(8,128)(2,1)} %all-to-all-done.1.rest_ref.last_ref, ...), custom_call_target="tpu_custom_call" | custom-call | flops 2013265920 | bytes 10000000 | tf_op jit(solution)/shard_map/pallas_call | solution.py:259
  201.2 29.7 %all-gather.9.cloned.1.call-done = bf16[1024,1536]{1,0:T(8,128)(2,1)} async-done(((bf16[256,1536]{1,0:T(8,128)(2,1)}), bf16[1024,1536]{1,0:T(8,128)(2,1)}) %all-gather.9.cloned.1.call-update) | async-done | bytes 3145744 | tf_op jit(solution)/shard_map/all_gather | solution.py:357
  230.9 0.0 copy-start.1
  230.9 1.9 copy-done.1
  232.8 7.1 %shard_map.54 = bf16[2,9,64,768]{3,2,1,0:T(8,128)(2,1)} custom-call(s32[3]{0:T(128)S(1)} %pad_add_fusion.where_ref, bf16[16,3,8,2048]{3,2,1,0:T(8,128)(2,1)S(1)} %all-to-all-done.own_ref, bf16[16,7,8,2048]{3,2,1,0:T(8,128)(2,1)} %all-to-all-done.1.rest_ref.last_ref, ...), custom_call_target="tpu_custom_call", output_to_operand_aliasing={{}: (11, {})} | custom-call | flops 2013265920 | bytes 10000000 | tf_op jit(solution)/shard_map/pallas_call | solution.py:259
  (5 shorter events, 0.1 us)
Async XLA Ops:
  6.5 2.1 copy-start.5
  6.5 100.7 %all-gather.7.cloned.1.call-start = ((), (), s32[]{:S(2)}) async-start(), calls=%async_computation.2 | async-start | bytes 7864320 | tf_op jit(solution)/shard_map/all_gather | solution.py:344
  11.1 58.1 %all-to-all-start = ((bf16[16,3,8,2048]{3,2,1,0:T(8,128)(2,1)}), bf16[16,3,8,2048]{3,2,1,0:T(8,128)(2,1)S(1)}, u32[]{:S(2)}, u32[]{:S(2)}) async-start(bf16[16,3,8,2048]{3,2,1,0:T(8,128)(2,1)} %shard_map.46), calls=%async_computation | async-start | bytes 3145728 | tf_op jit(solution)/shard_map/all_to_all | solution.py:296
  21.4 18.8 %collective-permute-start = (bf16[136,2048]{1,0:T(8,128)(2,1)S(1)}, bf16[136,2048]{1,0:T(8,128)(2,1)S(1)}, u32[]{:S(2)}, u32[]{:S(2)}) collective-permute-start(bf16[136,2048]{1,0:T(8,128)(2,1)S(1)} %pad_maximum_fusion.block.refs_0_), channel_id=1, source_target_pairs={{0,16},{16,32},{32,48},{48,0},{1,17},{17,33},{33,49},{49,1},{2,18}... | collective-permute-start | bytes 1671176 | tf_op jit(solution)/shard_map/ppermute | solution.py:291
  23.7 40.7 %collective-permute-start.1 = (bf16[136,2048]{1,0:T(8,128)(2,1)S(1)}, bf16[136,2048]{1,0:T(8,128)(2,1)S(1)}, u32[]{:S(2)}, u32[]{:S(2)}) collective-permute-start(bf16[136,2048]{1,0:T(8,128)(2,1)S(1)} %pad_maximum_fusion.block.refs_0_), channel_id=1, source_target_pairs={{0,32},{16,48},{32,0},{48,16},{1,33},{17,49},{33,1},{49,17},{2,34}... | collective-permute-start | bytes 1671176 | tf_op jit(solution)/shard_map/ppermute | solution.py:291
  29.5 34.9 %collective-permute-start.2 = (bf16[136,2048]{1,0:T(8,128)(2,1)S(1)}, bf16[136,2048]{1,0:T(8,128)(2,1)S(1)}, u32[]{:S(2)}, u32[]{:S(2)}) collective-permute-start(bf16[136,2048]{1,0:T(8,128)(2,1)S(1)} %pad_maximum_fusion.block.refs_0_), channel_id=1, source_target_pairs={{0,48},{16,0},{32,16},{48,32},{1,49},{17,1},{33,17},{49,33},{2,50}... | collective-permute-start | bytes 1671176 | tf_op jit(solution)/shard_map/ppermute | solution.py:291
  67.3 1.9 copy-start
  69.2 110.9 %all-to-all-start.1 = ((bf16[16,7,8,2048]{3,2,1,0:T(8,128)(2,1)}), bf16[16,7,8,2048]{3,2,1,0:T(8,128)(2,1)}, u32[]{:S(2)}, u32[]{:S(2)}) async-start(bf16[16,7,8,2048]{3,2,1,0:T(8,128)(2,1)} %copy-done), calls=%async_computation.1 | async-start | bytes 7340032 | tf_op jit(solution)/shard_map/all_to_all | solution.py:296
  80.4 26.3 %collective-permute-start.6 = (bf16[256,1536]{1,0:T(8,128)(2,1)}, bf16[256,1536]{1,0:T(8,128)(2,1)S(1)}, u32[]{:S(2)}, u32[]{:S(2)}) collective-permute-start(bf16[256,1536]{1,0:T(8,128)(2,1)} %shard_map.50), channel_id=1, source_target_pairs={{0,256},{256,0},{1,257},{257,1},{2,258},{258,2},{3,259},{259,3},{4... | collective-permute-start | bytes 2359304 | tf_op jit(solution)/shard_map/ppermute | solution.py:355
  106.6 1.9 copy-start.4
  107.3 85.0 %all-gather.11.cloned.1.call-start = ((), (), s32[]{:S(2)}) async-start(), calls=%async_computation.4 | async-start | bytes 3932160 | tf_op jit(solution)/shard_map/all_gather | solution.py:357
  108.5 122.4 %all-gather.9.cloned.1.call-start = ((), (), s32[]{:S(2)}) async-start(), calls=%async_computation.3 | async-start | bytes 3932160 | tf_op jit(solution)/shard_map/all_gather | solution.py:357
  110.7 69.4 %collective-permute-start.7 = (bf16[256,1536]{1,0:T(8,128)(2,1)}, bf16[256,1536]{1,0:T(8,128)(2,1)}, u32[]{:S(2)}, u32[]{:S(2)}) collective-permute-start(bf16[256,1536]{1,0:T(8,128)(2,1)} %shard_map.51), channel_id=1, source_target_pairs={{0,256},{256,0},{1,257},{257,1},{2,258},{258,2},{3,259},{259,3},{4... | collective-permute-start | bytes 2359304 | tf_op jit(solution)/shard_map/ppermute | solution.py:356
  117.8 45.0 %collective-permute-start.3 = (bf16[16,8,256]{2,1,0:T(8,128)(2,1)S(1)}, bf16[16,8,256]{2,1,0:T(8,128)(2,1)S(1)}, u32[]{:S(2)}, u32[]{:S(2)}) collective-permute-start(bf16[16,8,256]{2,1,0:T(8,128)(2,1)S(1)} %get-tuple-element.12), channel_id=1, source_target_pairs={{0,16},{16,32},{32,48},{48,0},{1,17},{17,33},{33,49},{49,1},{2,18}... | collective-permute-start | bytes 196616 | tf_op jit(solution)/shard_map/ppermute | solution.py:291
  148.2 30.2 %collective-permute-start.4 = (bf16[16,8,256]{2,1,0:T(8,128)(2,1)S(1)}, bf16[16,8,256]{2,1,0:T(8,128)(2,1)S(1)}, u32[]{:S(2)}, u32[]{:S(2)}) collective-permute-start(bf16[16,8,256]{2,1,0:T(8,128)(2,1)S(1)} %get-tuple-element.12), channel_id=1, source_target_pairs={{0,32},{16,48},{32,0},{48,16},{1,33},{17,49},{33,1},{49,17},{2,34}... | collective-permute-start | bytes 196616 | tf_op jit(solution)/shard_map/ppermute | solution.py:291
  150.1 28.3 %collective-permute-start.5 = (bf16[16,8,256]{2,1,0:T(8,128)(2,1)S(1)}, bf16[16,8,256]{2,1,0:T(8,128)(2,1)S(1)}, u32[]{:S(2)}, u32[]{:S(2)}) collective-permute-start(bf16[16,8,256]{2,1,0:T(8,128)(2,1)S(1)} %get-tuple-element.12), channel_id=1, source_target_pairs={{0,48},{16,0},{32,16},{48,32},{1,49},{17,1},{33,17},{49,33},{2,50}... | collective-permute-start | bytes 196616 | tf_op jit(solution)/shard_map/ppermute | solution.py:291
  180.1 2.8 %copy-start.3 = (bf16[8,256,1536]{2,1,0:T(8,128)(2,1)S(1)}, bf16[8,256,1536]{2,1,0:T(8,128)(2,1)}, u32[]{:S(2)}) copy-start(bf16[8,256,1536]{2,1,0:T(8,128)(2,1)} %all-gather.7.cloned.1.call-done) | copy-start | bytes 18874372
  192.2 1.9 copy-start.2
  230.9 1.9 copy-start.1
Sparse Core Ops, SparseCore 0:
  9.5 76.4 all-gather.6
  110.2 73.4 all-gather.10
  185.8 45.1 all-gather.8

commit v3 on v2

v3 whole, which is shorter than its diff:
```python
import jax
import jax.numpy as jnp
from jax import lax
from jax.experimental import pallas as pl
from jax.experimental.pallas import tpu as pltpu
from jax.sharding import Mesh, PartitionSpec as P

ZH, X, ZL, Y, C = 2, 4, 4, 8, 2
PEERS = Y * C
HELD = 2
CAP = 9
MAIN = CAP - 1
TOP = 8
TOK = 128
D = 2048
FF = 768
KEPT = PEERS * HELD
LEFT = (ZL - 1) * HELD
COLS = HELD * 2 * TOK
SAID = MAIN - HELD
TILE = 256
INFO = 2 * TOK

f32 = jnp.float32
bf16 = jnp.bfloat16


def iota(shape, dim):
    return lax.broadcasted_iota(jnp.int32, shape, dim)


def earlier():
    return (iota((TOK, TOK), 0) < iota((TOK, TOK), 1)).astype(bf16)


def named(ids, experts):
    hit = (ids[0:1, :] == experts).astype(f32)
    for k in range(1, TOP):
        hit = hit + (ids[k : k + 1, :] == experts).astype(f32)
    return hit


def chosen_rows(ids, first):
    kept = (iota((KEPT, TOK), 0) + first).astype(f32)
    hit = named(ids, kept)
    rank = jnp.dot(hit.astype(bf16), earlier(), preferred_element_type=f32)
    place = jnp.where(hit > 0, rank, -1.0)
    slot = iota((KEPT, MAIN, TOK), 1).astype(f32)
    chosen = (place[:, None, :] == slot).astype(f32)
    return chosen.reshape(KEPT * MAIN, TOK).astype(bf16)


def moved_rows(chosen, rows):
    moved = jnp.dot(chosen, rows, preferred_element_type=f32).astype(bf16)
    return moved.reshape(PEERS, HELD, MAIN, rows.shape[1])


def ids_of(block):
    return block[TOK : TOK + TOP, 0:TOK].astype(f32)


def ending_rows(ids, first, b):
    row = iota((PEERS * MAIN, TOK), 0)
    experts = (first + row // MAIN * HELD + row % HELD).astype(f32)
    hit = jnp.where((row % MAIN // HELD + 1) % ZL == b, named(ids, experts), 0.0)
    rank = jnp.dot(hit.astype(bf16), earlier(), preferred_element_type=f32)
    return jnp.where(rank == MAIN, hit, 0.0).astype(bf16)


def own_kernel(zl_ref, block, out_ref, main_ref, tail_ref):
    @pl.when(pl.program_id(0) == 0)
    def _():
        first = zl_ref[0] * KEPT
        main_ref[...] = chosen_rows(ids_of(block), first)
        tail_ref[...] = ending_rows(ids_of(block), first, 0)

    rows = block[0:TOK, :]
    out_ref[:, 0:HELD] = moved_rows(main_ref[...], rows)
    last = jnp.dot(tail_ref[...], rows, preferred_element_type=f32).astype(bf16)
    out_ref[:, HELD] = last.reshape(PEERS, MAIN, rows.shape[1])


def rest_kernel(zl_ref, *refs):
    blocks, (out_ref, main_ref, tail_ref, said_ref) = refs[:ZL], refs[-4:]

    @pl.when(pl.program_id(0) == 0)
    def _():
        first = zl_ref[0] * KEPT
        kept = (iota((KEPT, TOK), 0) + first).astype(f32)
        for b in range(ZL):
            ids = ids_of(blocks[b])
            gates = blocks[b][TOK : TOK + TOP, TOK:INFO].astype(f32)
            gate = jnp.zeros((KEPT, TOK), f32)
            for k in range(TOP):
                gate = gate + jnp.where(ids[k : k + 1, :] == kept, gates[k : k + 1, :], 0.0)
            said_ref[b, :, 0:TOK] = named(ids, kept).astype(bf16)
            said_ref[b, :, TOK:INFO] = gate.astype(bf16)
            if b:
                main_ref[b - 1] = chosen_rows(ids, first)
                tail_ref[b - 1] = ending_rows(ids, first, b)

    width = out_ref.shape[3]
    row, col = iota((PEERS * MAIN, KEPT), 0), iota((PEERS * MAIN, KEPT), 1)
    said = []
    for e in range(HELD):
        pick = (row % MAIN == SAID) & (col == row // MAIN * HELD + e)
        said.append(
            jnp.dot(
                pick.astype(f32).astype(bf16),
                said_ref[pl.program_id(0)],
                preferred_element_type=f32,
            )
        )
    last = jnp.concatenate(said, axis=1)
    for b in range(1, ZL):
        rows = blocks[b][0:TOK, :]
        moved = moved_rows(main_ref[b - 1], rows)
        for e in range(HELD):
            out_ref[:, e * (ZL - 1) + b - 1] = moved[:, e]
        last = last + jnp.dot(tail_ref[b - 1], rows, preferred_element_type=f32)
    out_ref[:, LEFT] = last.astype(bf16).reshape(PEERS, MAIN, width)


def dispatch(zl, blocks, *others):
    whole = len(blocks) == ZL
    tiles = LEFT + 1 if whole else HELD + 1
    scratch = [pltpu.VMEM((KEPT * MAIN, TOK), bf16), pltpu.VMEM((PEERS * MAIN, TOK), bf16)]
    if whole:
        scratch = [
            pltpu.VMEM((ZL - 1, KEPT * MAIN, TOK), bf16),
            pltpu.VMEM((ZL - 1, PEERS * MAIN, TOK), bf16),
            pltpu.VMEM((ZL, KEPT, INFO), bf16),
        ]
    return pl.pallas_call(
        rest_kernel if whole else own_kernel,
        grid_spec=pltpu.PrefetchScalarGridSpec(
            num_scalar_prefetch=1,
            grid=(D // COLS,),
            in_specs=[pl.BlockSpec((TOK + TOP, COLS), lambda n, z: (0, n))] * len(blocks)
            + [pl.BlockSpec(memory_space=pl.ANY)] * len(others),
            out_specs=pl.BlockSpec((PEERS, tiles, MAIN, COLS), lambda n, z: (0, 0, 0, n)),
            scratch_shapes=scratch,
        ),
        out_shape=jax.ShapeDtypeStruct((PEERS, tiles, MAIN, D), bf16),
        compiler_params=pltpu.CompilerParams(vmem_limit_bytes=40 * 1024 * 1024),
        cost_estimate=pl.CostEstimate(
            flops=2 * len(blocks) * 384 * TOK * D,
            bytes_accessed=PEERS * tiles * MAIN * D * 2,
            transcendentals=0,
        ),
    )(zl, *blocks, *others)


def plan_kernel(where_ref, last_ref, gate_ref, sort_ref, sort8_ref):
    blocks = PEERS * ZL
    count = blocks * MAIN
    near_rows = PEERS * MAIN
    rest = (ZL - 1) * MAIN
    zl = where_ref[0]
    out_row, in_row = iota((count, count), 0), iota((count, count), 1)
    late = in_row - near_rows
    peer = jnp.where(late >= 0, late // rest, in_row // MAIN)
    b = jnp.where(late >= 0, late % rest // MAIN + 1, 0)
    source = (zl - b + ZL) % ZL * PEERS + peer
    sort_ref[...] = (out_row == in_row % MAIN * blocks + source).astype(f32).astype(bf16)
    ones = jnp.ones((TOK, TILE), bf16)
    said = last_ref[...].astype(f32).reshape(PEERS, MAIN, D)[:, SAID, :]
    for e in range(HELD):
        starts = [(b * HELD + e) * INFO for b in range(ZL)]
        hit = jnp.concatenate([said[:, at : at + TOK] for at in starts], axis=0)
        gate = jnp.concatenate([said[:, at + TOK : at + INFO] for at in starts], axis=0)
        rank = jnp.dot(hit.astype(bf16), earlier(), preferred_element_type=f32)
        slot = iota((blocks, MAIN, TOK), 1).astype(f32)
        chosen = jnp.where(rank[:, None, :] == slot, gate[:, None, :], 0.0)
        chosen = chosen.reshape(ZL, near_rows, TOK)
        gate_ref[e, 0:near_rows, :] = jnp.dot(
            chosen[0].astype(bf16), ones, preferred_element_type=f32
        )
        others = jnp.concatenate(
            [chosen[b].reshape(PEERS, MAIN, TOK) for b in range(1, ZL)], axis=1
        ).reshape(PEERS * rest, TOK)
        gate_ref[e, near_rows:count, :] = jnp.dot(
            others.astype(bf16), ones, preferred_element_type=f32
        )
        last = jnp.where(rank == MAIN, gate, 0.0).astype(bf16)
        last = jnp.dot(last, ones, preferred_element_type=f32).astype(bf16)
        row, col = iota((blocks * HELD, blocks), 0), iota((blocks * HELD, blocks), 1)
        b = (row // HELD + 1) % ZL
        spread = (col == b * PEERS + row // MAIN).astype(f32).astype(bf16)
        gate_ref[e, count:, :] = jnp.dot(spread, last, preferred_element_type=f32)
        out_row, in_row = iota((blocks, blocks * HELD), 0), iota((blocks, blocks * HELD), 1)
        source = (zl - (in_row // HELD + 1) % ZL + ZL) % ZL * PEERS + in_row // MAIN
        keep = (out_row == source) & (in_row % HELD == e)
        sort8_ref[e] = keep.astype(f32).astype(bf16)


def plan(where, rest):
    blocks = PEERS * ZL
    rows = blocks * (MAIN + HELD)
    shapes = [
        jax.ShapeDtypeStruct((HELD, rows, TILE), f32),
        jax.ShapeDtypeStruct((blocks * MAIN, blocks * MAIN), bf16),
        jax.ShapeDtypeStruct((HELD, blocks, blocks * HELD), bf16),
    ]
    return pl.pallas_call(
        plan_kernel,
        grid_spec=pltpu.PrefetchScalarGridSpec(
            num_scalar_prefetch=1,
            grid=(1,),
            in_specs=[pl.BlockSpec((PEERS, 1, MAIN, D), lambda n, w: (0, LEFT, 0, 0))],
            out_specs=[
                pl.BlockSpec(s.shape, lambda n, w, r=len(s.shape): (0,) * r) for s in shapes
            ],
        ),
        out_shape=shapes,
        compiler_params=pltpu.CompilerParams(vmem_limit_bytes=32 * 1024 * 1024),
        cost_estimate=pl.CostEstimate(flops=10**8, bytes_accessed=10**6, transcendentals=0),
    )(where, rest)


def gather_rows(rows_ref, own_ref, rest_ref, own_last_ref, last_ref):
    at = 0
    half = rows_ref.shape[1]
    for ref in (own_ref, rest_ref):
        count = ref.shape[0] * ref.shape[1] * ref.shape[2]
        rows_ref[at : at + count, :] = ref[...].reshape(count, half)
        at += count
    count = PEERS * MAIN
    mine = iota((count, half), 0) % MAIN >= SAID
    own_last = own_last_ref[...].astype(f32).reshape(count, half)
    last = last_ref[...].astype(f32).reshape(count, half)
    rows_ref[at:, :] = jnp.where(mine, own_last, last).astype(bf16)


def near_kernel(where_ref, own_ref, rest_ref, own_last_ref, last_ref, weights_ref, out_ref, rows_ref):
    @pl.when(pl.program_id(1) == 0)
    def _():
        gather_rows(rows_ref, own_ref, rest_ref, own_last_ref, last_ref)

    weights = weights_ref[...].reshape(D // 2, weights_ref.shape[3])
    out_ref[0] = jnp.dot(rows_ref[...], weights, preferred_element_type=f32)


def near_part(where, own, rest, near):
    rows, half, tile = PEERS * ZL * (MAIN + HELD), D // 2, 2 * TILE
    return pl.pallas_call(
        near_kernel,
        grid_spec=pltpu.PrefetchScalarGridSpec(
            num_scalar_prefetch=1,
            grid=(HELD, 2 * FF // tile),
            in_specs=[
                pl.BlockSpec((PEERS, 1, MAIN, half), lambda e, n, w: (0, e, 0, w[1])),
                pl.BlockSpec((PEERS, ZL - 1, MAIN, half), lambda e, n, w: (0, e, 0, w[1])),
                pl.BlockSpec((PEERS, 1, MAIN, half), lambda e, n, w: (0, HELD, 0, w[1])),
                pl.BlockSpec((PEERS, 1, MAIN, half), lambda e, n, w: (0, LEFT, 0, w[1])),
                pl.BlockSpec((X, 1, D // 8, tile), lambda e, n, w: (0, e, 0, n)),
            ],
            out_specs=pl.BlockSpec((1, rows, tile), lambda e, n, w: (e, 0, n)),
            scratch_shapes=[pltpu.VMEM((rows, half), bf16)],
        ),
        out_shape=jax.ShapeDtypeStruct((HELD, rows, 2 * FF), f32),
        compiler_params=pltpu.CompilerParams(vmem_limit_bytes=60 * 1024 * 1024),
        cost_estimate=pl.CostEstimate(flops=10**11, bytes_accessed=10**7, transcendentals=0),
    )(where, own, rest, own, rest, near)


def expert_kernel(
    where_ref, own_ref, rest_ref, own_last_ref, last_ref, gate_ref, sort_ref, sort8_ref,
    before_ref, up_ref, *refs,
):
    g_refs, u_refs, (out_ref, rows_ref) = refs[:X], refs[X : 2 * X], refs[-2:]
    blocks = PEERS * ZL
    count = blocks * MAIN
    half = D // 2

    @pl.when(pl.program_id(0) == 0)
    def _():
        piece = D // 8
        for d in range(X):
            cols = pl.ds(pl.multiple_of(lax.rem(where_ref[2] - d + X, X) * piece, piece), piece)
            parts = [r.at[:, :, :, cols] for r in (own_ref, rest_ref, own_last_ref, last_ref)]
            gather_rows(rows_ref.at[:, d * piece : (d + 1) * piece], *parts)

    def added(sums_ref, weight_refs):
        weights = jnp.concatenate([ref[...] for ref in weight_refs], axis=0)
        return sums_ref[0] + jnp.dot(rows_ref[...], weights, preferred_element_type=f32)

    before = added(before_ref, g_refs)
    up = added(up_ref, u_refs)
    hidden = (before / (1.0 + jnp.exp(-before)) * up * gate_ref[0]).astype(bf16)
    main = jnp.dot(sort_ref[...], hidden[0:count], preferred_element_type=f32)
    out_ref[0, 0:MAIN] = main.astype(bf16).reshape(MAIN, blocks, TILE)
    last = jnp.dot(sort8_ref[0], hidden[count:], preferred_element_type=f32)
    out_ref[0, MAIN] = last.astype(bf16)


def expert(e, where, own, rest, slots, sums, far, other=None):
    blocks = PEERS * ZL
    tiles = FF // TILE
    rows, half = blocks * (MAIN + HELD), D // 2
    gates, sort, sort8 = slots
    others = [] if other is None else [other]
    return pl.pallas_call(
        expert_kernel,
        grid_spec=pltpu.PrefetchScalarGridSpec(
            num_scalar_prefetch=1,
            grid=(tiles,),
            in_specs=[
                pl.BlockSpec((PEERS, 1, MAIN, half), lambda n, w: (0, e, 0, 1 - w[1])),
                pl.BlockSpec((PEERS, ZL - 1, MAIN, half), lambda n, w: (0, e, 0, 1 - w[1])),
                pl.BlockSpec((PEERS, 1, MAIN, half), lambda n, w: (0, HELD, 0, 1 - w[1])),
                pl.BlockSpec((PEERS, 1, MAIN, half), lambda n, w: (0, LEFT, 0, 1 - w[1])),
                pl.BlockSpec((1, rows, TILE), lambda n, w: (e, 0, 0)),
                pl.BlockSpec(sort.shape, lambda n, w: (0, 0)),
                pl.BlockSpec((1,) + sort8.shape[1:], lambda n, w: (e, 0, 0)),
                pl.BlockSpec((1, rows, TILE), lambda n, w: (e, 0, n)),
                pl.BlockSpec((1, rows, TILE), lambda n, w: (e, 0, n + tiles)),
            ]
            + [pl.BlockSpec((D // 8, TILE), lambda n, w: (0, n))] * X
            + [pl.BlockSpec((D // 8, TILE), lambda n, w: (0, n + tiles))] * X
            + [pl.BlockSpec(memory_space=pl.ANY)] * len(others),
            out_specs=pl.BlockSpec((1, CAP, blocks, TILE), lambda n, w: (e, 0, 0, n)),
            scratch_shapes=[pltpu.VMEM((rows, half), bf16)],
        ),
        out_shape=jax.ShapeDtypeStruct((HELD, CAP, blocks, FF), bf16),
        input_output_aliases={10 + 2 * X: 0} if others else {},
        compiler_params=pltpu.CompilerParams(vmem_limit_bytes=60 * 1024 * 1024),
        cost_estimate=pl.CostEstimate(
            flops=rows * D * 2 * FF, bytes_accessed=10_000_000, transcendentals=10**6
        ),
    )(where, own, rest, own, rest, gates, sort, sort8, sums, sums, *far, *far, *others)


def over(axis, count, block):
    return [block] + [
        lax.ppermute(block, axis, [(i, (i + b) % count) for i in range(count)])
        for b in range(1, count)
    ]


def over_peers(message):
    return lax.all_to_all(message, ("y", "c"), split_axis=0, concat_axis=0, tiled=True)


def take_kernel(*refs):
    refs[-1][...] = refs[0][0]


def marks(*values):
    return [
        lax.slice(v, (0,) * v.ndim, (1,) * (v.ndim - 2) + (8, TOK)).reshape(8, TOK) for v in values
    ]


def take(weights, e, *others):
    shape = weights.shape[1:]
    others = marks(*others)
    return pl.pallas_call(
        take_kernel,
        grid=(1,),
        in_specs=[pl.BlockSpec((1,) + shape, lambda n: (e, 0, 0))]
        + [pl.BlockSpec(memory_space=pl.ANY)] * len(others),
        out_specs=pl.BlockSpec(shape, lambda n: (0, 0)),
        out_shape=jax.ShapeDtypeStruct(shape, weights.dtype),
        cost_estimate=pl.CostEstimate(flops=0, bytes_accessed=1_600_000, transcendentals=0),
    )(weights, *others)


def pass_kernel(*refs):
    pass


def after(value, *others):
    others = marks(*others)
    return pl.pallas_call(
        pass_kernel,
        in_specs=[pl.BlockSpec(memory_space=pl.ANY)] * (1 + len(others)),
        out_specs=pl.BlockSpec(memory_space=pl.ANY),
        out_shape=jax.ShapeDtypeStruct(value.shape, value.dtype),
        input_output_aliases={0: 0},
    )(value, *others)


def shards(moe_rows, expert_ids, expert_gates, expert_weights):
    zh, zl = lax.axis_index("zh"), lax.axis_index("zl")
    where = jnp.stack([zl, zh, lax.axis_index("x")])
    info = jnp.concatenate([expert_ids.T.astype(bf16), expert_gates.T], axis=1)
    packed = jnp.concatenate([moe_rows, jnp.pad(info, ((0, 0), (0, D - INFO)))], axis=0)
    blocks = over("zl", ZL, packed)
    near = lax.all_gather(expert_weights, "x", axis=0)
    own = over_peers(dispatch(zl.reshape(1), [packed]))
    swap = [(0, 1), (1, 0)]
    taken = take(expert_weights, 0, *blocks[1:])
    first = lax.ppermute(taken, "zh", swap)
    rest = over_peers(dispatch(zl.reshape(1), blocks, *marks(own, taken)))
    second = lax.ppermute(take(expert_weights, 1, first), "zh", swap)
    far = [over("x", X, first), over("x", X, second)]
    slots = plan(where, rest)
    sums = near_part(where, own, rest, near)
    hidden = expert(0, where, own, rest, slots, sums, far[0])
    hidden = expert(1, where, own, rest, slots, sums, far[1], hidden)
    return jnp.transpose(hidden, (0, 2, 1, 3))[None]


def solution(mesh):
    inner = Mesh(mesh.devices.reshape(ZH, X, ZL, Y, C), ("zh", "x", "zl", "y", "c"))
    tokens = P(("zh", "x", "zl", "y", "c"), None)
    in_specs = (tokens, tokens, tokens, P(("zl", "y", "c"), ("zh", "x"), None))
    out_specs = P(("zh", "x"), ("zl", "y", "c"), None, None, None)
    return jax.shard_map(
        shards, mesh=inner, in_specs=in_specs, out_specs=out_specs, check_vma=False
    )
```

time: 247 us -> 247 us (level)
  the two profiles are of different devices: /device:TPU:1 before, /device:TPU:64 now
where the time goes in v3:
time: 247 us; the launch traced here: 246 us
  waiting for transfers between devices  114 us (46%)
  starting transfers between devices  66.5 us (27%)
  Pallas kernels  40.2 us (16%)
  between operations  13.7 us (6%)
  local copies, waits for them, and re-layouts  8.92 us (4%)
  other arithmetic  3.04 us (1%)
    ppermute x9, waiting for transfers between devices, over(): lax.ppermute(block, axis, [(i, (i + b) % count) for i in range(count)])  61.2 us
    ppermute x9, starting transfers between devices, over(): lax.ppermute(block, axis, [(i, (i + b) % count) for i in range(count)])  36.3 us
    ppermute x1, waiting for transfers between devices, shards(): first = lax.ppermute(taken, 'zh', swap)  35 us
    ppermute x1, waiting for transfers between devices, shards(): second = lax.ppermute(take(expert_weights, 1, first), 'zh', swap)  17.1 us
    pallas_call x2, Pallas kernels, expert(): pl.pallas_call(expert_kernel, grid_spec=pltpu.PrefetchScalarGridSpec(num_...  16.8 us
    all_to_all x2, starting transfers between devices, over_peers(): lax.all_to_all(message, ('y', 'c'), split_axis=0, concat_axis=0, tiled=True)  14.4 us
    pallas_call x1, Pallas kernels, near_part(): pl.pallas_call(near_kernel, grid_spec=pltpu.PrefetchScalarGridSpec(num_sc...  11.2 us
    ppermute x1, starting transfers between devices, shards(): first = lax.ppermute(taken, 'zh', swap)  8.49 us
  transfers between devices with their start and end apart: 14, of which 6 were waited for; matrix products, arithmetic and copies ran while one was open for 2% of the time, Pallas kernels for 12%

profile of v3, /device:TPU:64, one launch (start us, length us, event | category | flops | bytes accessed | tf_op | source)
XLA Modules:
  0.0 246.3 jit_solution(4666737683758162081)
XLA Ops:
  6.5 0.7 convert_bitcast_fusion
  7.2 0.7 fusion.2
  7.9 1.1 pad_maximum_fusion.block.refs_0_
  9.0 2.6 %shard_map.46 = bf16[16,3,8,2048]{3,2,1,0:T(8,128)(2,1)} custom-call(s32[1]{0:T(128)} %bitcast.zl_ref, bf16[136,2048]{1,0:T(8,128)(2,1)S(1)} %pad_maximum_fusion.block.refs_0_), custom_call_target="tpu_custom_call" | custom-call | flops 201326592 | bytes 1572864 | tf_op jit(solution)/shard_map/pallas_call | solution.py:134
  11.6 7.3 %all-to-all-start = ((bf16[16,3,8,2048]{3,2,1,0:T(8,128)(2,1)}), bf16[16,3,8,2048]{3,2,1,0:T(8,128)(2,1)}, u32[]{:S(2)}, u32[]{:S(2)}) async-start(bf16[16,3,8,2048]{3,2,1,0:T(8,128)(2,1)} %shard_map.46), calls=%async_computation | async-start | bytes 3145728 | tf_op jit(solution)/shard_map/all_to_all | solution.py:342
  18.8 0.0 all-gather.3.cloned.1.call-start
  18.9 0.7 all-gather.3.cloned.1.call-update
  19.6 4.3 %collective-permute-start = (bf16[136,2048]{1,0:T(8,128)(2,1)S(1)}, bf16[136,2048]{1,0:T(8,128)(2,1)S(1)}, u32[]{:S(2)}, u32[]{:S(2)}) collective-permute-start(bf16[136,2048]{1,0:T(8,128)(2,1)S(1)} %pad_maximum_fusion.block.refs_0_), channel_id=1, source_target_pairs={{0,16},{16,32},{32,48},{48,0},{1,17},{17,33},{33,49},{49,1},{2,18}... | collective-permute-start | bytes 1671176 | tf_op jit(solution)/shard_map/ppermute | solution.py:336
  23.9 4.1 %collective-permute-start.1 = (bf16[136,2048]{1,0:T(8,128)(2,1)S(1)}, bf16[136,2048]{1,0:T(8,128)(2,1)S(1)}, u32[]{:S(2)}, u32[]{:S(2)}) collective-permute-start(bf16[136,2048]{1,0:T(8,128)(2,1)S(1)} %pad_maximum_fusion.block.refs_0_), channel_id=1, source_target_pairs={{0,32},{16,48},{32,0},{48,16},{1,33},{17,49},{33,1},{49,17},{2,34}... | collective-permute-start | bytes 1671176 | tf_op jit(solution)/shard_map/ppermute | solution.py:336
  27.9 3.6 %collective-permute-start.2 = (bf16[136,2048]{1,0:T(8,128)(2,1)S(1)}, bf16[136,2048]{1,0:T(8,128)(2,1)S(1)}, u32[]{:S(2)}, u32[]{:S(2)}) collective-permute-start(bf16[136,2048]{1,0:T(8,128)(2,1)S(1)} %pad_maximum_fusion.block.refs_0_), channel_id=1, source_target_pairs={{0,48},{16,0},{32,16},{48,32},{1,49},{17,1},{33,17},{49,33},{2,50}... | collective-permute-start | bytes 1671176 | tf_op jit(solution)/shard_map/ppermute | solution.py:336
  31.5 29.1 %collective-permute-done.refs_1_ = bf16[136,2048]{1,0:T(8,128)(2,1)S(1)} collective-permute-done((bf16[136,2048]{1,0:T(8,128)(2,1)S(1)}, bf16[136,2048]{1,0:T(8,128)(2,1)S(1)}, u32[]{:S(2)}, u32[]{:S(2)}) %collective-permute-start) | collective-permute-done | bytes 557088 | tf_op jit(solution)/shard_map/ppermute | solution.py:336
  60.7 0.6 slice.25.refs_1_
  61.3 10.8 %collective-permute-done.1.refs_2_ = bf16[136,2048]{1,0:T(8,128)(2,1)S(1)} collective-permute-done((bf16[136,2048]{1,0:T(8,128)(2,1)S(1)}, bf16[136,2048]{1,0:T(8,128)(2,1)S(1)}, u32[]{:S(2)}, u32[]{:S(2)}) %collective-permute-start.1) | collective-permute-done | bytes 557088 | tf_op jit(solution)/shard_map/ppermute | solution.py:336
  72.0 0.5 slice.26.refs_2_
  72.6 2.1 collective-permute-done.2.refs_3_
  74.6 0.6 slice.27.refs_3_
  75.2 2.1 shard_map.47
  77.3 0.7 slice.28.refs_5_
  78.0 0.0 all-to-all-done.own_ref.own_last_ref
  78.0 0.7 slice_bitcast_fusion.refs_4_
  78.6 2.9 %shard_map.48 = bf16[16,7,8,2048]{3,2,1,0:T(8,128)(2,1)S(1)} custom-call(s32[1]{0:T(128)} %bitcast.zl_ref, bf16[136,2048]{1,0:T(8,128)(2,1)S(1)} %pad_maximum_fusion.block.refs_0_, bf16[136,2048]{1,0:T(8,128)(2,1)S(1)} %collective-permute-done.refs_1_, bf16[136,2048]{1,0:T(8,128)(2,1)S(1)} %collective-permute-done.1.refs_2_, ...), custom_call_target="tpu_custom_call" | custom-call | flops 805306368 | bytes 3670016 | tf_op jit(solution)/shard_map/pallas_call | solution.py:134
  81.5 0.0 copy-start
  81.5 1.8 copy-done
  83.3 7.1 %all-to-all-start.1 = ((bf16[16,7,8,2048]{3,2,1,0:T(8,128)(2,1)}), bf16[16,7,8,2048]{3,2,1,0:T(8,128)(2,1)}, u32[]{:S(2)}, u32[]{:S(2)}) async-start(bf16[16,7,8,2048]{3,2,1,0:T(8,128)(2,1)} %copy-done), calls=%async_computation.1 | async-start | bytes 7340032 | tf_op jit(solution)/shard_map/all_to_all | solution.py:342
  90.4 0.0 copy-done.9
  90.4 8.5 %collective-permute-start.3 = (bf16[256,1536]{1,0:T(8,128)(2,1)S(1)}, bf16[256,1536]{1,0:T(8,128)(2,1)S(1)}, u32[]{:S(2)}, u32[]{:S(2)}) collective-permute-start(bf16[256,1536]{1,0:T(8,128)(2,1)S(1)} %copy-done.9), channel_id=1, source_target_pairs={{0,256},{256,0},{1,257},{257,1},{2,258},{258,2},{3,259},{259,3},{4... | collective-permute-start | bytes 2359304 | tf_op jit(solution)/shard_map/ppermute | solution.py:394
  98.9 35.0 %collective-permute-done.3.refs_0_.refs_4_ = bf16[256,1536]{1,0:T(8,128)(2,1)S(1)} collective-permute-done((bf16[256,1536]{1,0:T(8,128)(2,1)S(1)}, bf16[256,1536]{1,0:T(8,128)(2,1)S(1)}, u32[]{:S(2)}, u32[]{:S(2)}) %collective-permute-start.3) | collective-permute-done | bytes 786464 | tf_op jit(solution)/shard_map/ppermute | solution.py:394
  134.0 0.6 slice.29.refs_1_
  134.6 2.1 shard_map.51
  136.7 7.2 %collective-permute-start.4 = (bf16[256,1536]{1,0:T(8,128)(2,1)}, bf16[256,1536]{1,0:T(8,128)(2,1)S(1)}, u32[]{:S(2)}, u32[]{:S(2)}) collective-permute-start(bf16[256,1536]{1,0:T(8,128)(2,1)} %shard_map.51), channel_id=1, source_target_pairs={{0,256},{256,0},{1,257},{257,1},{2,258},{258,2},{3,259},{259,3},{4... | collective-permute-start | bytes 2359304 | tf_op jit(solution)/shard_map/ppermute | solution.py:396
  143.9 4.7 %collective-permute-start.10 = (bf16[256,1536]{1,0:T(8,128)(2,1)S(1)}, bf16[256,1536]{1,0:T(8,128)(2,1)S(1)}, u32[]{:S(2)}, u32[]{:S(2)}) collective-permute-start(bf16[256,1536]{1,0:T(8,128)(2,1)S(1)} %collective-permute-done.3.refs_0_.refs_4_), channel_id=1, source_target_pairs={{0,192},{64,0},{128,64},{192,128},{1,193},{65,1},{129,65},{193,129... | collective-permute-start | bytes 2359304 | tf_op jit(solution)/shard_map/ppermute | solution.py:336
  148.6 0.6 pad_add_fusion.where_ref
  149.2 1.9 collective-permute-start.8
  151.1 4.2 %collective-permute-start.9 = (bf16[256,1536]{1,0:T(8,128)(2,1)S(1)}, bf16[256,1536]{1,0:T(8,128)(2,1)}, u32[]{:S(2)}, u32[]{:S(2)}) collective-permute-start(bf16[256,1536]{1,0:T(8,128)(2,1)S(1)} %collective-permute-done.3.refs_0_.refs_4_), channel_id=1, source_target_pairs={{0,128},{64,192},{128,0},{192,64},{1,129},{65,193},{129,1},{193,65... | collective-permute-start | bytes 2359304 | tf_op jit(solution)/shard_map/ppermute | solution.py:336
  155.3 17.1 %collective-permute-done.4.refs_0_.refs_4_ = bf16[256,1536]{1,0:T(8,128)(2,1)S(1)} collective-permute-done((bf16[256,1536]{1,0:T(8,128)(2,1)}, bf16[256,1536]{1,0:T(8,128)(2,1)S(1)}, u32[]{:S(2)}, u32[]{:S(2)}) %collective-permute-start.4) | collective-permute-done | bytes 786464 | tf_op jit(solution)/shard_map/ppermute | solution.py:396
  172.4 0.0 copy-start.6
  172.4 3.4 %collective-permute-start.5 = (bf16[256,1536]{1,0:T(8,128)(2,1)S(1)}, bf16[256,1536]{1,0:T(8,128)(2,1)S(1)}, u32[]{:S(2)}, u32[]{:S(2)}) collective-permute-start(bf16[256,1536]{1,0:T(8,128)(2,1)S(1)} %collective-permute-done.4.refs_0_.refs_4_), channel_id=1, source_target_pairs={{0,64},{64,128},{128,192},{192,0},{1,65},{65,129},{129,193},{193,1... | collective-permute-start | bytes 2359304 | tf_op jit(solution)/shard_map/ppermute | solution.py:336
  175.8 4.6 %collective-permute-start.6 = (bf16[256,1536]{1,0:T(8,128)(2,1)S(1)}, bf16[256,1536]{1,0:T(8,128)(2,1)}, u32[]{:S(2)}, u32[]{:S(2)}) collective-permute-start(bf16[256,1536]{1,0:T(8,128)(2,1)S(1)} %collective-permute-done.4.refs_0_.refs_4_), channel_id=1, source_target_pairs={{0,128},{64,192},{128,0},{192,64},{1,129},{65,193},{129,1},{193,65... | collective-permute-start | bytes 2359304 | tf_op jit(solution)/shard_map/ppermute | solution.py:336
  180.4 19.2 %collective-permute-done.10.refs_3_.refs_7_ = bf16[256,1536]{1,0:T(8,128)(2,1)S(1)} collective-permute-done((bf16[256,1536]{1,0:T(8,128)(2,1)S(1)}, bf16[256,1536]{1,0:T(8,128)(2,1)S(1)}, u32[]{:S(2)}, u32[]{:S(2)}) %collective-permute-start.10) | collective-permute-done | bytes 786464 | tf_op jit(solution)/shard_map/ppermute | solution.py:336
  199.6 0.0 copy-start.7
  199.6 5.6 %collective-permute-start.7 = (bf16[256,1536]{1,0:T(8,128)(2,1)S(1)}, bf16[256,1536]{1,0:T(8,128)(2,1)}, u32[]{:S(2)}, u32[]{:S(2)}) collective-permute-start(bf16[256,1536]{1,0:T(8,128)(2,1)S(1)} %collective-permute-done.4.refs_0_.refs_4_), channel_id=1, source_target_pairs={{0,192},{64,0},{128,64},{192,128},{1,193},{65,1},{129,65},{193,129... | collective-permute-start | bytes 2359304 | tf_op jit(solution)/shard_map/ppermute | solution.py:336
  205.2 0.0 all-gather.3.cloned.1.call-done
  205.2 0.0 all-to-all-done.1.last_ref.rest_ref
  205.3 0.0 copy-start.4
  205.3 11.2 %shard_map.50.before_ref.up_ref = f32[2,640,1536]{2,1,0:T(8,128)} custom-call(s32[3]{0:T(128)} %pad_add_fusion.where_ref, bf16[16,3,8,2048]{3,2,1,0:T(8,128)(2,1)} %all-to-all-done.own_ref.own_last_ref, bf16[16,7,8,2048]{3,2,1,0:T(8,128)(2,1)} %all-to-all-done.1.last_ref.rest_ref, bf16[16,3,8,2048]{3,2,1,0:T(8,128)(2,1)} %all-to-all-done.own_ref.own_last_ref, ...), custom_call_target="tpu_custom_call" | custom-call | flops 99999997952 | bytes 10000000 | tf_op jit(solution)/shard_map/pallas_call | solution.py:246
  216.5 0.0 copy-done.5
  216.5 0.0 copy-done.6
  216.5 0.0 copy-done.7
  216.5 0.0 copy-done.4
  216.5 2.6 %shard_map.49 = (f32[2,640,256]{2,1,0:T(8,128)S(1)}, bf16[512,512]{1,0:T(8,128)(2,1)S(1)}, bf16[2,64,128]{2,1,0:T(8,128)(2,1)S(1)}) custom-call(s32[3]{0:T(128)S(1)} %copy-done.4, bf16[16,7,8,2048]{3,2,1,0:T(8,128)(2,1)} %all-to-all-done.1.last_ref.rest_ref), custom_call_target="tpu_custom_call" | custom-call | flops 100000000 | bytes 1000000 | tf_op jit(solution)/shard_map/pallas_call | solution.py:205
  219.1 0.0 copy-start.1
  219.1 1.2 copy-done.1
  220.3 0.0 copy-start.2
  220.3 0.8 copy-done.2
  221.1 0.6 copy-done.3
  221.7 0.0 collective-permute-done.8.refs_1_.refs_5_
  221.7 0.0 collective-permute-done.9.refs_2_.refs_6_
  221.7 8.4 %shard_map.52.refs_8_ = bf16[2,9,64,768]{3,2,1,0:T(8,128)(2,1)} custom-call(s32[3]{0:T(128)} %pad_add_fusion.where_ref, bf16[16,3,8,2048]{3,2,1,0:T(8,128)(2,1)} %all-to-all-done.own_ref.own_last_ref, bf16[16,7,8,2048]{3,2,1,0:T(8,128)(2,1)} %all-to-all-done.1.last_ref.rest_ref, bf16[16,3,8,2048]{3,2,1,0:T(8,128)(2,1)} %all-to-all-done.own_ref.own_last_ref, ...), custom_call_target="tpu_custom_call" | custom-call | flops 2013265920 | bytes 10000000 | tf_op jit(solution)/shard_map/pallas_call | solution.py:303
  230.1 0.0 collective-permute-done.5.refs_1_.refs_5_
  230.1 0.0 copy-start.8
  230.1 0.0 collective-permute-done.6.refs_2_.refs_6_
  230.2 0.0 collective-permute-done.7.refs_3_.refs_7_
  230.2 0.9 copy-done.8
  231.0 8.4 %shard_map.53 = bf16[2,9,64,768]{3,2,1,0:T(8,128)(2,1)} custom-call(s32[3]{0:T(128)} %pad_add_fusion.where_ref, bf16[16,3,8,2048]{3,2,1,0:T(8,128)(2,1)} %all-to-all-done.own_ref.own_last_ref, bf16[16,7,8,2048]{3,2,1,0:T(8,128)(2,1)} %all-to-all-done.1.last_ref.rest_ref, ...), custom_call_target="tpu_custom_call", output_to_operand_aliasing={{}: (18, {})} | custom-call | flops 2013265920 | bytes 10000000 | tf_op jit(solution)/shard_map/pallas_call | solution.py:303
  (3 shorter events, 0.0 us)
Async XLA Ops:
  11.6 66.4 %all-to-all-start = ((bf16[16,3,8,2048]{3,2,1,0:T(8,128)(2,1)}), bf16[16,3,8,2048]{3,2,1,0:T(8,128)(2,1)}, u32[]{:S(2)}, u32[]{:S(2)}) async-start(bf16[16,3,8,2048]{3,2,1,0:T(8,128)(2,1)} %shard_map.46), calls=%async_computation | async-start | bytes 3145728 | tf_op jit(solution)/shard_map/all_to_all | solution.py:342
  18.8 186.4 %all-gather.3.cloned.1.call-start = ((), (), s32[]{:S(2)}) async-start(), calls=%async_computation.2 | async-start | bytes 7864320 | tf_op jit(solution)/shard_map/all_gather | solution.py:390
  19.6 41.1 %collective-permute-start = (bf16[136,2048]{1,0:T(8,128)(2,1)S(1)}, bf16[136,2048]{1,0:T(8,128)(2,1)S(1)}, u32[]{:S(2)}, u32[]{:S(2)}) collective-permute-start(bf16[136,2048]{1,0:T(8,128)(2,1)S(1)} %pad_maximum_fusion.block.refs_0_), channel_id=1, source_target_pairs={{0,16},{16,32},{32,48},{48,0},{1,17},{17,33},{33,49},{49,1},{2,18}... | collective-permute-start | bytes 1671176 | tf_op jit(solution)/shard_map/ppermute | solution.py:336
  23.9 48.2 %collective-permute-start.1 = (bf16[136,2048]{1,0:T(8,128)(2,1)S(1)}, bf16[136,2048]{1,0:T(8,128)(2,1)S(1)}, u32[]{:S(2)}, u32[]{:S(2)}) collective-permute-start(bf16[136,2048]{1,0:T(8,128)(2,1)S(1)} %pad_maximum_fusion.block.refs_0_), channel_id=1, source_target_pairs={{0,32},{16,48},{32,0},{48,16},{1,33},{17,49},{33,1},{49,17},{2,34}... | collective-permute-start | bytes 1671176 | tf_op jit(solution)/shard_map/ppermute | solution.py:336
  27.9 46.7 %collective-permute-start.2 = (bf16[136,2048]{1,0:T(8,128)(2,1)S(1)}, bf16[136,2048]{1,0:T(8,128)(2,1)S(1)}, u32[]{:S(2)}, u32[]{:S(2)}) collective-permute-start(bf16[136,2048]{1,0:T(8,128)(2,1)S(1)} %pad_maximum_fusion.block.refs_0_), channel_id=1, source_target_pairs={{0,48},{16,0},{32,16},{48,32},{1,49},{17,1},{33,17},{49,33},{2,50}... | collective-permute-start | bytes 1671176 | tf_op jit(solution)/shard_map/ppermute | solution.py:336
  81.5 1.8 copy-start
  83.3 7.1 %copy-start.9 = (bf16[256,1536]{1,0:T(8,128)(2,1)S(1)}, bf16[256,1536]{1,0:T(8,128)(2,1)}, u32[]{:S(2)}) copy-start(bf16[256,1536]{1,0:T(8,128)(2,1)} %shard_map.47) | copy-start | bytes 2359300
  83.3 122.0 %all-to-all-start.1 = ((bf16[16,7,8,2048]{3,2,1,0:T(8,128)(2,1)}), bf16[16,7,8,2048]{3,2,1,0:T(8,128)(2,1)}, u32[]{:S(2)}, u32[]{:S(2)}) async-start(bf16[16,7,8,2048]{3,2,1,0:T(8,128)(2,1)} %copy-done), calls=%async_computation.1 | async-start | bytes 7340032 | tf_op jit(solution)/shard_map/all_to_all | solution.py:342
  90.4 43.5 %collective-permute-start.3 = (bf16[256,1536]{1,0:T(8,128)(2,1)S(1)}, bf16[256,1536]{1,0:T(8,128)(2,1)S(1)}, u32[]{:S(2)}, u32[]{:S(2)}) collective-permute-start(bf16[256,1536]{1,0:T(8,128)(2,1)S(1)} %copy-done.9), channel_id=1, source_target_pairs={{0,256},{256,0},{1,257},{257,1},{2,258},{258,2},{3,259},{259,3},{4... | collective-permute-start | bytes 2359304 | tf_op jit(solution)/shard_map/ppermute | solution.py:394
  134.0 82.5 %copy-start.5 = (bf16[256,1536]{1,0:T(8,128)(2,1)}, bf16[256,1536]{1,0:T(8,128)(2,1)S(1)}, u32[]{:S(2)}) copy-start(bf16[256,1536]{1,0:T(8,128)(2,1)S(1)} %collective-permute-done.3.refs_0_.refs_4_) | copy-start | bytes 2359300
  136.7 35.7 %collective-permute-start.4 = (bf16[256,1536]{1,0:T(8,128)(2,1)}, bf16[256,1536]{1,0:T(8,128)(2,1)S(1)}, u32[]{:S(2)}, u32[]{:S(2)}) collective-permute-start(bf16[256,1536]{1,0:T(8,128)(2,1)} %shard_map.51), channel_id=1, source_target_pairs={{0,256},{256,0},{1,257},{257,1},{2,258},{258,2},{3,259},{259,3},{4... | collective-permute-start | bytes 2359304 | tf_op jit(solution)/shard_map/ppermute | solution.py:396
  143.9 55.7 %collective-permute-start.10 = (bf16[256,1536]{1,0:T(8,128)(2,1)S(1)}, bf16[256,1536]{1,0:T(8,128)(2,1)S(1)}, u32[]{:S(2)}, u32[]{:S(2)}) collective-permute-start(bf16[256,1536]{1,0:T(8,128)(2,1)S(1)} %collective-permute-done.3.refs_0_.refs_4_), channel_id=1, source_target_pairs={{0,192},{64,0},{128,64},{192,128},{1,193},{65,1},{129,65},{193,129... | collective-permute-start | bytes 2359304 | tf_op jit(solution)/shard_map/ppermute | solution.py:336
  149.2 72.6 %collective-permute-start.8 = (bf16[256,1536]{1,0:T(8,128)(2,1)S(1)}, bf16[256,1536]{1,0:T(8,128)(2,1)}, u32[]{:S(2)}, u32[]{:S(2)}) collective-permute-start(bf16[256,1536]{1,0:T(8,128)(2,1)S(1)} %collective-permute-done.3.refs_0_.refs_4_), channel_id=1, source_target_pairs={{0,64},{64,128},{128,192},{192,0},{1,65},{65,129},{129,193},{193,1... | collective-permute-start | bytes 2359304 | tf_op jit(solution)/shard_map/ppermute | solution.py:336
  151.1 70.6 %collective-permute-start.9 = (bf16[256,1536]{1,0:T(8,128)(2,1)S(1)}, bf16[256,1536]{1,0:T(8,128)(2,1)}, u32[]{:S(2)}, u32[]{:S(2)}) collective-permute-start(bf16[256,1536]{1,0:T(8,128)(2,1)S(1)} %collective-permute-done.3.refs_0_.refs_4_), channel_id=1, source_target_pairs={{0,128},{64,192},{128,0},{192,64},{1,129},{65,193},{129,1},{193,65... | collective-permute-start | bytes 2359304 | tf_op jit(solution)/shard_map/ppermute | solution.py:336
  172.4 44.1 %copy-start.6 = (bf16[256,1536]{1,0:T(8,128)(2,1)}, bf16[256,1536]{1,0:T(8,128)(2,1)S(1)}, u32[]{:S(2)}) copy-start(bf16[256,1536]{1,0:T(8,128)(2,1)S(1)} %collective-permute-done.4.refs_0_.refs_4_) | copy-start | bytes 2359300
  172.4 57.7 %collective-permute-start.5 = (bf16[256,1536]{1,0:T(8,128)(2,1)S(1)}, bf16[256,1536]{1,0:T(8,128)(2,1)S(1)}, u32[]{:S(2)}, u32[]{:S(2)}) collective-permute-start(bf16[256,1536]{1,0:T(8,128)(2,1)S(1)} %collective-permute-done.4.refs_0_.refs_4_), channel_id=1, source_target_pairs={{0,64},{64,128},{128,192},{192,0},{1,65},{65,129},{129,193},{193,1... | collective-permute-start | bytes 2359304 | tf_op jit(solution)/shard_map/ppermute | solution.py:336
  175.8 54.4 %collective-permute-start.6 = (bf16[256,1536]{1,0:T(8,128)(2,1)S(1)}, bf16[256,1536]{1,0:T(8,128)(2,1)}, u32[]{:S(2)}, u32[]{:S(2)}) collective-permute-start(bf16[256,1536]{1,0:T(8,128)(2,1)S(1)} %collective-permute-done.4.refs_0_.refs_4_), channel_id=1, source_target_pairs={{0,128},{64,192},{128,0},{192,64},{1,129},{65,193},{129,1},{193,65... | collective-permute-start | bytes 2359304 | tf_op jit(solution)/shard_map/ppermute | solution.py:336
  199.6 16.9 %copy-start.7 = (bf16[256,1536]{1,0:T(8,128)(2,1)}, bf16[256,1536]{1,0:T(8,128)(2,1)S(1)}, u32[]{:S(2)}) copy-start(bf16[256,1536]{1,0:T(8,128)(2,1)S(1)} %collective-permute-done.10.refs_3_.refs_7_) | copy-start | bytes 2359300
  199.6 30.5 %collective-permute-start.7 = (bf16[256,1536]{1,0:T(8,128)(2,1)S(1)}, bf16[256,1536]{1,0:T(8,128)(2,1)}, u32[]{:S(2)}, u32[]{:S(2)}) collective-permute-start(bf16[256,1536]{1,0:T(8,128)(2,1)S(1)} %collective-permute-done.4.refs_0_.refs_4_), channel_id=1, source_target_pairs={{0,192},{64,0},{128,64},{192,128},{1,193},{65,1},{129,65},{193,129... | collective-permute-start | bytes 2359304 | tf_op jit(solution)/shard_map/ppermute | solution.py:336
  205.3 11.2 %copy-start.4 = (s32[3]{0:T(128)S(1)}, s32[3]{0:T(128)}, u32[]{:S(2)}) copy-start(s32[3]{0:T(128)} %pad_add_fusion.where_ref) | copy-start | bytes 40
  219.1 1.2 copy-start.1
  220.3 0.8 copy-start.2
  221.1 0.6 copy-start.3
  230.1 0.9 copy-start.8
Sparse Core Ops, SparseCore 0:
  21.8 74.8 all-gather.2

commit v4 on v3

--- a/solution.py
+++ b/solution.py
@@ -1,3 +1,5 @@
+import functools
+
 import jax
 import jax.numpy as jnp
 from jax import lax
@@ -163,7 +165,7 @@
     b = jnp.where(late >= 0, late % rest // MAIN + 1, 0)
     source = (zl - b + ZL) % ZL * PEERS + peer
     sort_ref[...] = (out_row == in_row % MAIN * blocks + source).astype(f32).astype(bf16)
-    ones = jnp.ones((TOK, TILE), bf16)
+    ones = jnp.ones((TOK, TOK), bf16)
     said = last_ref[...].astype(f32).reshape(PEERS, MAIN, D)[:, SAID, :]
     for e in range(HELD):
         starts = [(b * HELD + e) * INFO for b in range(ZL)]
@@ -175,19 +177,21 @@
         chosen = chosen.reshape(ZL, near_rows, TOK)
         gate_ref[e, 0:near_rows, :] = jnp.dot(
             chosen[0].astype(bf16), ones, preferred_element_type=f32
-        )
+        ).astype(bf16)
         others = jnp.concatenate(
             [chosen[b].reshape(PEERS, MAIN, TOK) for b in range(1, ZL)], axis=1
         ).reshape(PEERS * rest, TOK)
         gate_ref[e, near_rows:count, :] = jnp.dot(
             others.astype(bf16), ones, preferred_element_type=f32
-        )
+        ).astype(bf16)
         last = jnp.where(rank == MAIN, gate, 0.0).astype(bf16)
         last = jnp.dot(last, ones, preferred_element_type=f32).astype(bf16)
         row, col = iota((blocks * HELD, blocks), 0), iota((blocks * HELD, blocks), 1)
         b = (row // HELD + 1) % ZL
         spread = (col == b * PEERS + row // MAIN).astype(f32).astype(bf16)
-        gate_ref[e, count:, :] = jnp.dot(spread, last, preferred_element_type=f32)
+        gate_ref[e, count:, :] = jnp.dot(
+            spread, last, preferred_element_type=f32
+        ).astype(bf16)
         out_row, in_row = iota((blocks, blocks * HELD), 0), iota((blocks, blocks * HELD), 1)
         source = (zl - (in_row // HELD + 1) % ZL + ZL) % ZL * PEERS + in_row // MAIN
         keep = (out_row == source) & (in_row % HELD == e)
@@ -198,7 +202,7 @@
     blocks = PEERS * ZL
     rows = blocks * (MAIN + HELD)
     shapes = [
-        jax.ShapeDtypeStruct((HELD, rows, TILE), f32),
+        jax.ShapeDtypeStruct((HELD, rows, TOK), bf16),
         jax.ShapeDtypeStruct((blocks * MAIN, blocks * MAIN), bf16),
         jax.ShapeDtypeStruct((HELD, blocks, blocks * HELD), bf16),
     ]
@@ -232,103 +236,83 @@
     rows_ref[at:, :] = jnp.where(mine, own_last, last).astype(bf16)
 
 
-def near_kernel(where_ref, own_ref, rest_ref, own_last_ref, last_ref, weights_ref, out_ref, rows_ref):
-    @pl.when(pl.program_id(1) == 0)
-    def _():
-        gather_rows(rows_ref, own_ref, rest_ref, own_last_ref, last_ref)
-
-    weights = weights_ref[...].reshape(D // 2, weights_ref.shape[3])
-    out_ref[0] = jnp.dot(rows_ref[...], weights, preferred_element_type=f32)
-
-
-def near_part(where, own, rest, near):
-    rows, half, tile = PEERS * ZL * (MAIN + HELD), D // 2, 2 * TILE
-    return pl.pallas_call(
-        near_kernel,
-        grid_spec=pltpu.PrefetchScalarGridSpec(
-            num_scalar_prefetch=1,
-            grid=(HELD, 2 * FF // tile),
-            in_specs=[
-                pl.BlockSpec((PEERS, 1, MAIN, half), lambda e, n, w: (0, e, 0, w[1])),
-                pl.BlockSpec((PEERS, ZL - 1, MAIN, half), lambda e, n, w: (0, e, 0, w[1])),
-                pl.BlockSpec((PEERS, 1, MAIN, half), lambda e, n, w: (0, HELD, 0, w[1])),
-                pl.BlockSpec((PEERS, 1, MAIN, half), lambda e, n, w: (0, LEFT, 0, w[1])),
-                pl.BlockSpec((X, 1, D // 8, tile), lambda e, n, w: (0, e, 0, n)),
-            ],
-            out_specs=pl.BlockSpec((1, rows, tile), lambda e, n, w: (e, 0, n)),
-            scratch_shapes=[pltpu.VMEM((rows, half), bf16)],
-        ),
-        out_shape=jax.ShapeDtypeStruct((HELD, rows, 2 * FF), f32),
-        compiler_params=pltpu.CompilerParams(vmem_limit_bytes=60 * 1024 * 1024),
-        cost_estimate=pl.CostEstimate(flops=10**11, bytes_accessed=10**7, transcendentals=0),
-    )(where, own, rest, own, rest, near)
-
-
-def expert_kernel(
-    where_ref, own_ref, rest_ref, own_last_ref, last_ref, gate_ref, sort_ref, sort8_ref,
-    before_ref, up_ref, *refs,
-):
-    g_refs, u_refs, (out_ref, rows_ref) = refs[:X], refs[X : 2 * X], refs[-2:]
+def expert_kernel(pieces, *refs):
+    where_ref, own_ref, rest_ref, own_last_ref, last_ref, gate_ref, sort_ref, sort8_ref = refs[:8]
+    near_refs, far_refs, (out_ref, rows_ref) = refs[8:10], refs[10 : 10 + 2 * pieces], refs[-2:]
     blocks = PEERS * ZL
     count = blocks * MAIN
-    half = D // 2
+    half, width = D // 2, D // 2 // pieces
 
     @pl.when(pl.program_id(0) == 0)
     def _():
-        piece = D // 8
-        for d in range(X):
-            cols = pl.ds(pl.multiple_of(lax.rem(where_ref[2] - d + X, X) * piece, piece), piece)
+        zh, x = where_ref[1], where_ref[2]
+        moves = [(zh * half, 0, half)]
+        for d in range(pieces):
+            at = lax.rem(x - d + X, X) if pieces == X else 0
+            moves.append(((1 - zh) * half + at * width, half + d * width, width))
+        for start, to, wide in moves:
+            cols = pl.ds(pl.multiple_of(start, D // 8), wide)
             parts = [r.at[:, :, :, cols] for r in (own_ref, rest_ref, own_last_ref, last_ref)]
-            gather_rows(rows_ref.at[:, d * piece : (d + 1) * piece], *parts)
-
-    def added(sums_ref, weight_refs):
-        weights = jnp.concatenate([ref[...] for ref in weight_refs], axis=0)
-        return sums_ref[0] + jnp.dot(rows_ref[...], weights, preferred_element_type=f32)
-
-    before = added(before_ref, g_refs)
-    up = added(up_ref, u_refs)
-    hidden = (before / (1.0 + jnp.exp(-before)) * up * gate_ref[0]).astype(bf16)
+            gather_rows(rows_ref.at[:, to : to + wide], *parts)
+
+    near, far = rows_ref[:, 0:half], rows_ref[:, half:]
+
+    def product(near_ref, pieces_refs):
+        weights = jnp.concatenate([r[...].reshape(width, TILE) for r in pieces_refs], axis=0)
+        return jnp.dot(
+            near, near_ref[...].reshape(half, TILE), preferred_element_type=f32
+        ) + jnp.dot(far, weights, preferred_element_type=f32)
+
+    before = product(near_refs[0], far_refs[:pieces])
+    up = product(near_refs[1], far_refs[pieces:])
+    gate = gate_ref[0].astype(f32)
+    gate = jnp.concatenate([gate] * (TILE // TOK), axis=1)
+    hidden = (before / (1.0 + jnp.exp(-before)) * up * gate).astype(bf16)
     main = jnp.dot(sort_ref[...], hidden[0:count], preferred_element_type=f32)
     out_ref[0, 0:MAIN] = main.astype(bf16).reshape(MAIN, blocks, TILE)
     last = jnp.dot(sort8_ref[0], hidden[count:], preferred_element_type=f32)
     out_ref[0, MAIN] = last.astype(bf16)
 
 
-def expert(e, where, own, rest, slots, sums, far, other=None):
+def expert(e, where, own, rest, slots, near, far, other=None):
     blocks = PEERS * ZL
     tiles = FF // TILE
-    rows, half = blocks * (MAIN + HELD), D // 2
+    rows = blocks * (MAIN + HELD)
     gates, sort, sort8 = slots
     others = [] if other is None else [other]
-    return pl.pallas_call(
-        expert_kernel,
+    far = [f.reshape(-1, f.shape[-1]) for f in far]
+    deep = far[0].shape[0]
+    return pl.pallas_call(
+        functools.partial(expert_kernel, len(far)),
         grid_spec=pltpu.PrefetchScalarGridSpec(
             num_scalar_prefetch=1,
             grid=(tiles,),
             in_specs=[
-                pl.BlockSpec((PEERS, 1, MAIN, half), lambda n, w: (0, e, 0, 1 - w[1])),
-                pl.BlockSpec((PEERS, ZL - 1, MAIN, half), lambda n, w: (0, e, 0, 1 - w[1])),
-                pl.BlockSpec((PEERS, 1, MAIN, half), lambda n, w: (0, HELD, 0, 1 - w[1])),
-                pl.BlockSpec((PEERS, 1, MAIN, half), lambda n, w: (0, LEFT, 0, 1 - w[1])),
-                pl.BlockSpec((1, rows, TILE), lambda n, w: (e, 0, 0)),
+                pl.BlockSpec((PEERS, 1, MAIN, D), lambda n, w: (0, e, 0, 0)),
+                pl.BlockSpec((PEERS, ZL - 1, MAIN, D), lambda n, w: (0, e, 0, 0)),
+                pl.BlockSpec((PEERS, 1, MAIN, D), lambda n, w: (0, HELD, 0, 0)),
+                pl.BlockSpec((PEERS, 1, MAIN, D), lambda n, w: (0, LEFT, 0, 0)),
+                pl.BlockSpec((1,) + gates.shape[1:], lambda n, w: (e, 0, 0)),
                 pl.BlockSpec(sort.shape, lambda n, w: (0, 0)),
                 pl.BlockSpec((1,) + sort8.shape[1:], lambda n, w: (e, 0, 0)),
-                pl.BlockSpec((1, rows, TILE), lambda n, w: (e, 0, n)),
-                pl.BlockSpec((1, rows, TILE), lambda n, w: (e, 0, n + tiles)),
+                pl.BlockSpec((X, 1, D // 8, TILE), lambda n, w: (0, e, 0, n)),
+                pl.BlockSpec((X, 1, D // 8, TILE), lambda n, w: (0, e, 0, n + tiles)),
             ]
-            + [pl.BlockSpec((D // 8, TILE), lambda n, w: (0, n))] * X
-            + [pl.BlockSpec((D // 8, TILE), lambda n, w: (0, n + tiles))] * X
+            + [pl.BlockSpec((deep, TILE), lambda n, w: (0, n))] * len(far)
+            + [pl.BlockSpec((deep, TILE), lambda n, w: (0, n + tiles))] * len(far)
             + [pl.BlockSpec(memory_space=pl.ANY)] * len(others),
             out_specs=pl.BlockSpec((1, CAP, blocks, TILE), lambda n, w: (e, 0, 0, n)),
-            scratch_shapes=[pltpu.VMEM((rows, half), bf16)],
+            scratch_shapes=[pltpu.VMEM((rows, D), bf16)],
         ),
         out_shape=jax.ShapeDtypeStruct((HELD, CAP, blocks, FF), bf16),
-        input_output_aliases={10 + 2 * X: 0} if others else {},
+        input_output_aliases={10 + 2 * len(far): 0} if others else {},
         compiler_params=pltpu.CompilerParams(vmem_limit_bytes=60 * 1024 * 1024),
         cost_estimate=pl.CostEstimate(
-            flops=rows * D * 2 * FF, bytes_accessed=10_000_000, transcendentals=10**6
-        ),
-    )(where, own, rest, own, rest, gates, sort, sort8, sums, sums, *far, *far, *others)
+            flops=3*10**9 if e == 0 else 2 * rows * D * 2 * FF,
+            bytes_accessed=10_000_000,
+            transcendentals=10**6,
+        ),
+    )(where, own, rest, own, rest, gates, sort, sort8, near, near, *far, *far, *others)
 
 
 def over(axis, count, block):
@@ -394,11 +378,10 @@
     first = lax.ppermute(taken, "zh", swap)
     rest = over_peers(dispatch(zl.reshape(1), blocks, *marks(own, taken)))
     second = lax.ppermute(take(expert_weights, 1, first), "zh", swap)
-    far = [over("x", X, first), over("x", X, second)]
+    far = [[lax.all_gather(after(first, near), "x", axis=0)], over("x", X, second)]
     slots = plan(where, rest)
-    sums = near_part(where, own, rest, near)
-    hidden = expert(0, where, own, rest, slots, sums, far[0])
-    hidden = expert(1, where, own, rest, slots, sums, far[1], hidden)
+    hidden = expert(0, where, own, rest, slots, near, far[0])
+    hidden = expert(1, where, own, rest, slots, near, far[1], hidden)
     return jnp.transpose(hidden, (0, 2, 1, 3))[None]
 
 

time: 247 us -> 240 us (0.972)
  the two profiles are of different devices: /device:TPU:64 before, /device:TPU:203 now
where the time goes in v4:
time: 240 us; the launch traced here: 239 us
  waiting for transfers between devices  131 us (55%)
  starting transfers between devices  48.8 us (20%)
  Pallas kernels  32.9 us (14%)
  between operations  13.6 us (6%)
  local copies, waits for them, and re-layouts  10.9 us (5%)
    ppermute x6, waiting for transfers between devices, over(): lax.ppermute(block, axis, [(i, (i + b) % count) for i in range(count)])  42.8 us
    all_gather x1, waiting for transfers between devices, shards(): lax.all_gather(after(first, near), 'x', axis=0)  35.8 us
    ppermute x1, waiting for transfers between devices, shards(): first = lax.ppermute(taken, 'zh', swap)  24.5 us
    pallas_call x2, Pallas kernels, expert(): pl.pallas_call(functools.partial(expert_kernel, len(far)), grid_spec=pltp...  20.8 us
    ppermute x6, starting transfers between devices, over(): lax.ppermute(block, axis, [(i, (i + b) % count) for i in range(count)])  16.8 us
    all_to_all x2, waiting for transfers between devices, over_peers(): lax.all_to_all(message, ('y', 'c'), split_axis=0, concat_axis=0, tiled=True)  16.5 us
    all_to_all x2, starting transfers between devices, over_peers(): lax.all_to_all(message, ('y', 'c'), split_axis=0, concat_axis=0, tiled=True)  16 us
    ppermute x1, waiting for transfers between devices, shards(): second = lax.ppermute(take(expert_weights, 1, first), 'zh', swap)  10.9 us
  transfers between devices with their start and end apart: 12, of which 6 were waited for; matrix products, arithmetic and copies ran while one was open for 3% of the time, Pallas kernels for 9%

profile of v4, /device:TPU:203, one launch (start us, length us, event | category | flops | bytes accessed | tf_op | source)
XLA Modules:
  0.0 239.1 jit_solution(8177814092742400884)
XLA Ops:
  6.5 0.0 copy-start.11
  6.5 0.0 all-gather.5.cloned.1.call-start
  6.5 0.7 all-gather.5.cloned.1.call-update
  7.3 0.7 convert_bitcast_fusion
  8.0 0.7 fusion.2
  8.6 0.0 copy-done.11
  8.7 2.6 %shard_map.46 = bf16[16,3,8,2048]{3,2,1,0:T(8,128)(2,1)} custom-call(s32[1]{0:T(128)} %bitcast.zl_ref, bf16[136,2048]{1,0:T(8,128)(2,1)S(1)} %pad_maximum_fusion.block.refs_0_), custom_call_target="tpu_custom_call" | custom-call | flops 201326592 | bytes 1572864 | tf_op jit(solution)/shard_map/pallas_call | solution.py:136
  11.3 7.9 %all-to-all-start = ((bf16[16,3,8,2048]{3,2,1,0:T(8,128)(2,1)}), bf16[16,3,8,2048]{3,2,1,0:T(8,128)(2,1)}, u32[]{:S(2)}, u32[]{:S(2)}) async-start(bf16[16,3,8,2048]{3,2,1,0:T(8,128)(2,1)} %shard_map.46), calls=%async_computation | async-start | bytes 3145728 | tf_op jit(solution)/shard_map/all_to_all | solution.py:326
  19.1 1.9 collective-permute-start
  21.1 2.4 %collective-permute-start.1 = (bf16[136,2048]{1,0:T(8,128)(2,1)S(1)}, bf16[136,2048]{1,0:T(8,128)(2,1)S(1)}, u32[]{:S(2)}, u32[]{:S(2)}) collective-permute-start(bf16[136,2048]{1,0:T(8,128)(2,1)S(1)} %pad_maximum_fusion.block.refs_0_), channel_id=1, source_target_pairs={{0,32},{16,48},{32,0},{48,16},{1,33},{17,49},{33,1},{49,17},{2,34}... | collective-permute-start | bytes 1671176 | tf_op jit(solution)/shard_map/ppermute | solution.py:320
  23.5 2.8 %collective-permute-start.2 = (bf16[136,2048]{1,0:T(8,128)(2,1)S(1)}, bf16[136,2048]{1,0:T(8,128)(2,1)S(1)}, u32[]{:S(2)}, u32[]{:S(2)}) collective-permute-start(bf16[136,2048]{1,0:T(8,128)(2,1)S(1)} %pad_maximum_fusion.block.refs_0_), channel_id=1, source_target_pairs={{0,48},{16,0},{32,16},{48,32},{1,49},{17,1},{33,17},{49,33},{2,50}... | collective-permute-start | bytes 1671176 | tf_op jit(solution)/shard_map/ppermute | solution.py:320
  26.4 8.6 %collective-permute-done.refs_1_ = bf16[136,2048]{1,0:T(8,128)(2,1)S(1)} collective-permute-done((bf16[136,2048]{1,0:T(8,128)(2,1)S(1)}, bf16[136,2048]{1,0:T(8,128)(2,1)S(1)}, u32[]{:S(2)}, u32[]{:S(2)}) %collective-permute-start) | collective-permute-done | bytes 557088 | tf_op jit(solution)/shard_map/ppermute | solution.py:320
  35.0 0.6 slice.29.refs_1_
  35.6 34.2 %collective-permute-done.1.refs_2_ = bf16[136,2048]{1,0:T(8,128)(2,1)S(1)} collective-permute-done((bf16[136,2048]{1,0:T(8,128)(2,1)S(1)}, bf16[136,2048]{1,0:T(8,128)(2,1)S(1)}, u32[]{:S(2)}, u32[]{:S(2)}) %collective-permute-start.1) | collective-permute-done | bytes 557088 | tf_op jit(solution)/shard_map/ppermute | solution.py:320
  69.8 0.6 slice.30.refs_2_
  70.4 0.0 collective-permute-done.2.refs_3_
  70.4 0.5 slice.31.refs_3_
  70.9 2.1 shard_map.47
  72.9 0.6 slice.32.refs_5_
  73.6 0.0 all-to-all-done.refs_1_.refs_3_
  73.6 0.7 slice_bitcast_fusion.1.refs_4_
  74.2 2.9 %shard_map.48 = bf16[16,7,8,2048]{3,2,1,0:T(8,128)(2,1)S(1)} custom-call(s32[1]{0:T(128)} %bitcast.zl_ref, bf16[136,2048]{1,0:T(8,128)(2,1)S(1)} %pad_maximum_fusion.block.refs_0_, bf16[136,2048]{1,0:T(8,128)(2,1)S(1)} %collective-permute-done.refs_1_, bf16[136,2048]{1,0:T(8,128)(2,1)S(1)} %collective-permute-done.1.refs_2_, ...), custom_call_target="tpu_custom_call" | custom-call | flops 805306368 | bytes 3670016 | tf_op jit(solution)/shard_map/pallas_call | solution.py:136
  77.1 0.0 copy-start
  77.1 1.9 copy-done
  79.0 0.0 copy-start.10
  79.0 8.2 %all-to-all-start.1 = ((bf16[16,7,8,2048]{3,2,1,0:T(8,128)(2,1)}), bf16[16,7,8,2048]{3,2,1,0:T(8,128)(2,1)}, u32[]{:S(2)}, u32[]{:S(2)}) async-start(bf16[16,7,8,2048]{3,2,1,0:T(8,128)(2,1)} %copy-done), calls=%async_computation.1 | async-start | bytes 7340032 | tf_op jit(solution)/shard_map/all_to_all | solution.py:326
  87.2 0.0 copy-done.10
  87.2 8.8 %collective-permute-start.3 = (bf16[256,1536]{1,0:T(8,128)(2,1)S(1)}, bf16[256,1536]{1,0:T(8,128)(2,1)S(1)}, u32[]{:S(2)}, u32[]{:S(2)}) collective-permute-start(bf16[256,1536]{1,0:T(8,128)(2,1)S(1)} %copy-done.10), channel_id=1, source_target_pairs={{0,256},{256,0},{1,257},{257,1},{2,258},{258,2},{3,259},{259,3},{4... | collective-permute-start | bytes 2359304 | tf_op jit(solution)/shard_map/ppermute | solution.py:378
  96.1 24.5 %collective-permute-done.3.refs_0_ = bf16[256,1536]{1,0:T(8,128)(2,1)S(1)} collective-permute-done((bf16[256,1536]{1,0:T(8,128)(2,1)S(1)}, bf16[256,1536]{1,0:T(8,128)(2,1)S(1)}, u32[]{:S(2)}, u32[]{:S(2)}) %collective-permute-start.3) | collective-permute-done | bytes 786464 | tf_op jit(solution)/shard_map/ppermute | solution.py:378
  120.6 0.6 slice.33.refs_1_
  121.2 0.0 all-gather.7.cloned.1.call-start
  121.2 0.0 all-gather.5.cloned.1.call-done
  121.2 1.2 slice_bitcast_fusion.refs_1_
  122.5 0.0 copy-done.5
  122.5 0.0 all-gather.7.cloned.1.call-update
  122.5 2.1 shard_map.50
  124.5 7.1 %collective-permute-start.4 = (bf16[256,1536]{1,0:T(8,128)(2,1)}, bf16[256,1536]{1,0:T(8,128)(2,1)S(1)}, u32[]{:S(2)}, u32[]{:S(2)}) collective-permute-start(bf16[256,1536]{1,0:T(8,128)(2,1)} %shard_map.50), channel_id=1, source_target_pairs={{0,256},{256,0},{1,257},{257,1},{2,258},{258,2},{3,259},{259,3},{4... | collective-permute-start | bytes 2359304 | tf_op jit(solution)/shard_map/ppermute | solution.py:380
  131.7 10.9 %collective-permute-done.4.refs_10_.refs_14_ = bf16[256,1536]{1,0:T(8,128)(2,1)S(1)} collective-permute-done((bf16[256,1536]{1,0:T(8,128)(2,1)}, bf16[256,1536]{1,0:T(8,128)(2,1)S(1)}, u32[]{:S(2)}, u32[]{:S(2)}) %collective-permute-start.4) | collective-permute-done | bytes 786464 | tf_op jit(solution)/shard_map/ppermute | solution.py:380
  142.6 0.0 copy-start.6
  142.6 3.1 %collective-permute-start.5 = (bf16[256,1536]{1,0:T(8,128)(2,1)S(1)}, bf16[256,1536]{1,0:T(8,128)(2,1)S(1)}, u32[]{:S(2)}, u32[]{:S(2)}) collective-permute-start(bf16[256,1536]{1,0:T(8,128)(2,1)S(1)} %collective-permute-done.4.refs_10_.refs_14_), channel_id=1, source_target_pairs={{0,64},{64,128},{128,192},{192,0},{1,65},{65,129},{129,193},{193,1... | collective-permute-start | bytes 2359304 | tf_op jit(solution)/shard_map/ppermute | solution.py:320
  145.7 2.7 %collective-permute-start.6 = (bf16[256,1536]{1,0:T(8,128)(2,1)S(1)}, bf16[256,1536]{1,0:T(8,128)(2,1)S(1)}, u32[]{:S(2)}, u32[]{:S(2)}) collective-permute-start(bf16[256,1536]{1,0:T(8,128)(2,1)S(1)} %collective-permute-done.4.refs_10_.refs_14_), channel_id=1, source_target_pairs={{0,128},{64,192},{128,0},{192,64},{1,129},{65,193},{129,1},{193,65... | collective-permute-start | bytes 2359304 | tf_op jit(solution)/shard_map/ppermute | solution.py:320
  148.5 3.8 %collective-permute-start.7 = (bf16[256,1536]{1,0:T(8,128)(2,1)S(1)}, bf16[256,1536]{1,0:T(8,128)(2,1)S(1)}, u32[]{:S(2)}, u32[]{:S(2)}) collective-permute-start(bf16[256,1536]{1,0:T(8,128)(2,1)S(1)} %collective-permute-done.4.refs_10_.refs_14_), channel_id=1, source_target_pairs={{0,192},{64,0},{128,64},{192,128},{1,193},{65,1},{129,65},{193,129... | collective-permute-start | bytes 2359304 | tf_op jit(solution)/shard_map/ppermute | solution.py:320
  152.3 0.1 pad_add_fusion.where_ref.refs_0_
  152.3 0.0 copy-start.4
  152.3 16.5 %all-to-all-done.1.last_ref.refs_2_.refs_4_ = bf16[16,7,8,2048]{3,2,1,0:T(8,128)(2,1)} async-done(((bf16[16,7,8,2048]{3,2,1,0:T(8,128)(2,1)}), bf16[16,7,8,2048]{3,2,1,0:T(8,128)(2,1)}, u32[]{:S(2)}, u32[]{:S(2)}) %all-to-all-start.1) | async-done | bytes 3670048 | tf_op jit(solution)/shard_map/all_to_all | solution.py:326
  168.9 2.5 %shard_map.49 = (bf16[2,640,128]{2,1,0:T(8,128)(2,1)S(1)}, bf16[512,512]{1,0:T(8,128)(2,1)S(1)}, bf16[2,64,128]{2,1,0:T(8,128)(2,1)S(1)}) custom-call(s32[3]{0:T(128)S(1)} %pad_add_fusion.where_ref.refs_0_, bf16[16,7,8,2048]{3,2,1,0:T(8,128)(2,1)} %all-to-all-done.1.last_ref.refs_2_.refs_4_), custom_call_target="tpu_custom_call" | custom-call | flops 100000000 | bytes 1000000 | tf_op jit(solution)/shard_map/pallas_call | solution.py:209
  171.4 0.0 copy-done.6
  171.4 0.0 copy-done.4
  171.4 0.0 copy-start.1
  171.5 0.8 copy-done.1
  172.3 0.0 copy-start.2
  172.3 0.7 copy-done.2
  173.0 0.6 copy-done.3
  173.6 35.8 %all-gather.7.cloned.1.call-done.refs_10_.refs_11_ = bf16[1024,1536]{1,0:T(8,128)(2,1)} async-done(((bf16[256,1536]{1,0:T(8,128)(2,1)}), bf16[1024,1536]{1,0:T(8,128)(2,1)}) %all-gather.7.cloned.1.call-update) | async-done | bytes 3145744 | tf_op jit(solution)/shard_map/all_gather | solution.py:381
  209.4 10.3 %shard_map.52.refs_18_ = bf16[2,9,64,768]{3,2,1,0:T(8,128)(2,1)} custom-call(s32[3]{0:T(128)} %copy-done.4, bf16[16,3,8,2048]{3,2,1,0:T(8,128)(2,1)} %all-to-all-done.refs_1_.refs_3_, bf16[16,7,8,2048]{3,2,1,0:T(8,128)(2,1)} %all-to-all-done.1.last_ref.refs_2_.refs_4_, bf16[16,3,8,2048]{3,2,1,0:T(8,128)(2,1)} %all-to-all-done.refs_1_.refs_3_, ...), custom_call_target="tpu_custom_call" | custom-call | flops 3000000000 | bytes 10000000 | tf_op jit(solution)/shard_map/pallas_call | solution.py:285
  219.7 0.0 collective-permute-done.5.refs_11_.refs_15_
  219.8 0.0 copy-start.7
  219.8 0.0 collective-permute-done.6.refs_12_.refs_16_
  219.8 0.0 copy-start.8
  219.8 0.0 collective-permute-done.7.refs_13_.refs_17_
  219.8 0.8 copy-done.7
  220.6 0.3 copy-done.8
  220.9 0.9 copy-done.9
  221.8 10.4 %shard_map.53 = bf16[2,9,64,768]{3,2,1,0:T(8,128)(2,1)} custom-call(s32[3]{0:T(128)} %copy-done.4, bf16[16,3,8,2048]{3,2,1,0:T(8,128)(2,1)} %all-to-all-done.refs_1_.refs_3_, bf16[16,7,8,2048]{3,2,1,0:T(8,128)(2,1)} %all-to-all-done.1.last_ref.refs_2_.refs_4_, ...), custom_call_target="tpu_custom_call", output_to_operand_aliasing={{}: (18, {})} | custom-call | flops 4026531840 | bytes 10000000 | tf_op jit(solution)/shard_map/pallas_call | solution.py:285
  (5 shorter events, 0.0 us)
Async XLA Ops:
  6.5 2.1 copy-start.11
  6.5 114.7 %all-gather.5.cloned.1.call-start = ((), (), s32[]{:S(2)}) async-start(), calls=%async_computation.2 | async-start | bytes 7864320 | tf_op jit(solution)/shard_map/all_gather | solution.py:374
  11.3 62.3 %all-to-all-start = ((bf16[16,3,8,2048]{3,2,1,0:T(8,128)(2,1)}), bf16[16,3,8,2048]{3,2,1,0:T(8,128)(2,1)}, u32[]{:S(2)}, u32[]{:S(2)}) async-start(bf16[16,3,8,2048]{3,2,1,0:T(8,128)(2,1)} %shard_map.46), calls=%async_computation | async-start | bytes 3145728 | tf_op jit(solution)/shard_map/all_to_all | solution.py:326
  19.1 15.8 %collective-permute-start = (bf16[136,2048]{1,0:T(8,128)(2,1)S(1)}, bf16[136,2048]{1,0:T(8,128)(2,1)S(1)}, u32[]{:S(2)}, u32[]{:S(2)}) collective-permute-start(bf16[136,2048]{1,0:T(8,128)(2,1)S(1)} %pad_maximum_fusion.block.refs_0_), channel_id=1, source_target_pairs={{0,16},{16,32},{32,48},{48,0},{1,17},{17,33},{33,49},{49,1},{2,18}... | collective-permute-start | bytes 1671176 | tf_op jit(solution)/shard_map/ppermute | solution.py:320
  21.1 48.7 %collective-permute-start.1 = (bf16[136,2048]{1,0:T(8,128)(2,1)S(1)}, bf16[136,2048]{1,0:T(8,128)(2,1)S(1)}, u32[]{:S(2)}, u32[]{:S(2)}) collective-permute-start(bf16[136,2048]{1,0:T(8,128)(2,1)S(1)} %pad_maximum_fusion.block.refs_0_), channel_id=1, source_target_pairs={{0,32},{16,48},{32,0},{48,16},{1,33},{17,49},{33,1},{49,17},{2,34}... | collective-permute-start | bytes 1671176 | tf_op jit(solution)/shard_map/ppermute | solution.py:320
  23.5 46.8 %collective-permute-start.2 = (bf16[136,2048]{1,0:T(8,128)(2,1)S(1)}, bf16[136,2048]{1,0:T(8,128)(2,1)S(1)}, u32[]{:S(2)}, u32[]{:S(2)}) collective-permute-start(bf16[136,2048]{1,0:T(8,128)(2,1)S(1)} %pad_maximum_fusion.block.refs_0_), channel_id=1, source_target_pairs={{0,48},{16,0},{32,16},{48,32},{1,49},{17,1},{33,17},{49,33},{2,50}... | collective-permute-start | bytes 1671176 | tf_op jit(solution)/shard_map/ppermute | solution.py:320
  77.1 1.9 copy-start
  79.0 8.2 %copy-start.10 = (bf16[256,1536]{1,0:T(8,128)(2,1)S(1)}, bf16[256,1536]{1,0:T(8,128)(2,1)}, u32[]{:S(2)}) copy-start(bf16[256,1536]{1,0:T(8,128)(2,1)} %shard_map.47) | copy-start | bytes 2359300
  79.0 89.9 %all-to-all-start.1 = ((bf16[16,7,8,2048]{3,2,1,0:T(8,128)(2,1)}), bf16[16,7,8,2048]{3,2,1,0:T(8,128)(2,1)}, u32[]{:S(2)}, u32[]{:S(2)}) async-start(bf16[16,7,8,2048]{3,2,1,0:T(8,128)(2,1)} %copy-done), calls=%async_computation.1 | async-start | bytes 7340032 | tf_op jit(solution)/shard_map/all_to_all | solution.py:326
  87.2 33.4 %collective-permute-start.3 = (bf16[256,1536]{1,0:T(8,128)(2,1)S(1)}, bf16[256,1536]{1,0:T(8,128)(2,1)S(1)}, u32[]{:S(2)}, u32[]{:S(2)}) collective-permute-start(bf16[256,1536]{1,0:T(8,128)(2,1)S(1)} %copy-done.10), channel_id=1, source_target_pairs={{0,256},{256,0},{1,257},{257,1},{2,258},{258,2},{3,259},{259,3},{4... | collective-permute-start | bytes 2359304 | tf_op jit(solution)/shard_map/ppermute | solution.py:378
  120.6 1.9 copy-start.5
  121.2 88.2 %all-gather.7.cloned.1.call-start = ((), (), s32[]{:S(2)}) async-start(), calls=%async_computation.3 | async-start | bytes 3932160 | tf_op jit(solution)/shard_map/all_gather | solution.py:381
  124.5 18.1 %collective-permute-start.4 = (bf16[256,1536]{1,0:T(8,128)(2,1)}, bf16[256,1536]{1,0:T(8,128)(2,1)S(1)}, u32[]{:S(2)}, u32[]{:S(2)}) collective-permute-start(bf16[256,1536]{1,0:T(8,128)(2,1)} %shard_map.50), channel_id=1, source_target_pairs={{0,256},{256,0},{1,257},{257,1},{2,258},{258,2},{3,259},{259,3},{4... | collective-permute-start | bytes 2359304 | tf_op jit(solution)/shard_map/ppermute | solution.py:380
  142.6 28.8 %copy-start.6 = (bf16[256,1536]{1,0:T(8,128)(2,1)}, bf16[256,1536]{1,0:T(8,128)(2,1)S(1)}, u32[]{:S(2)}) copy-start(bf16[256,1536]{1,0:T(8,128)(2,1)S(1)} %collective-permute-done.4.refs_10_.refs_14_) | copy-start | bytes 2359300
  142.6 77.1 %collective-permute-start.5 = (bf16[256,1536]{1,0:T(8,128)(2,1)S(1)}, bf16[256,1536]{1,0:T(8,128)(2,1)S(1)}, u32[]{:S(2)}, u32[]{:S(2)}) collective-permute-start(bf16[256,1536]{1,0:T(8,128)(2,1)S(1)} %collective-permute-done.4.refs_10_.refs_14_), channel_id=1, source_target_pairs={{0,64},{64,128},{128,192},{192,0},{1,65},{65,129},{129,193},{193,1... | collective-permute-start | bytes 2359304 | tf_op jit(solution)/shard_map/ppermute | solution.py:320
  145.7 74.0 %collective-permute-start.6 = (bf16[256,1536]{1,0:T(8,128)(2,1)S(1)}, bf16[256,1536]{1,0:T(8,128)(2,1)S(1)}, u32[]{:S(2)}, u32[]{:S(2)}) collective-permute-start(bf16[256,1536]{1,0:T(8,128)(2,1)S(1)} %collective-permute-done.4.refs_10_.refs_14_), channel_id=1, source_target_pairs={{0,128},{64,192},{128,0},{192,64},{1,129},{65,193},{129,1},{193,65... | collective-permute-start | bytes 2359304 | tf_op jit(solution)/shard_map/ppermute | solution.py:320
  148.5 71.3 %collective-permute-start.7 = (bf16[256,1536]{1,0:T(8,128)(2,1)S(1)}, bf16[256,1536]{1,0:T(8,128)(2,1)S(1)}, u32[]{:S(2)}, u32[]{:S(2)}) collective-permute-start(bf16[256,1536]{1,0:T(8,128)(2,1)S(1)} %collective-permute-done.4.refs_10_.refs_14_), channel_id=1, source_target_pairs={{0,192},{64,0},{128,64},{192,128},{1,193},{65,1},{129,65},{193,129... | collective-permute-start | bytes 2359304 | tf_op jit(solution)/shard_map/ppermute | solution.py:320
  152.3 19.1 %copy-start.4 = (s32[3]{0:T(128)}, s32[3]{0:T(128)S(1)}, u32[]{:S(2)}) copy-start(s32[3]{0:T(128)S(1)} %pad_add_fusion.where_ref.refs_0_) | copy-start | bytes 40
  171.4 0.8 copy-start.1
  172.3 0.7 copy-start.2
  173.0 0.6 copy-start.3
  219.8 0.9 copy-start.7
  219.8 1.1 copy-start.8
  220.9 0.9 copy-start.9
Sparse Core Ops, SparseCore 0:
  9.5 73.0 all-gather.4
  124.1 85.2 all-gather.6

commit v5 on v4

--- a/solution.py
+++ b/solution.py
@@ -23,6 +23,7 @@
 TILE = 256
 INFO = 2 * TOK
 
+TAKE_COST = (0, 55 * 10**9)
 f32 = jnp.float32
 bf16 = jnp.bfloat16
 
@@ -346,7 +347,7 @@
         + [pl.BlockSpec(memory_space=pl.ANY)] * len(others),
         out_specs=pl.BlockSpec(shape, lambda n: (0, 0)),
         out_shape=jax.ShapeDtypeStruct(shape, weights.dtype),
-        cost_estimate=pl.CostEstimate(flops=0, bytes_accessed=1_600_000, transcendentals=0),
+        cost_estimate=pl.CostEstimate(flops=TAKE_COST[e], bytes_accessed=1_600_000, transcendentals=0),
     )(weights, *others)
 
 
@@ -378,7 +379,7 @@
     first = lax.ppermute(taken, "zh", swap)
     rest = over_peers(dispatch(zl.reshape(1), blocks, *marks(own, taken)))
     second = lax.ppermute(take(expert_weights, 1, first), "zh", swap)
-    far = [[lax.all_gather(after(first, near), "x", axis=0)], over("x", X, second)]
+    far = [over("x", X, first), over("x", X, second)]
     slots = plan(where, rest)
     hidden = expert(0, where, own, rest, slots, near, far[0])
     hidden = expert(1, where, own, rest, slots, near, far[1], hidden)

time: 240 us -> 237 us (0.988)
  the two profiles are of different devices: /device:TPU:203 before, /device:TPU:192 now
where the time goes in v5:
time: 237 us
  waiting for transfers between devices  99.8 us (42%)
  starting transfers between devices  78.2 us (33%)
  Pallas kernels  33.1 us (14%)
  between operations  13.6 us (6%)
  local copies, waits for them, and re-layouts  9.45 us (4%)
  other arithmetic  2.53 us (1%)
    ppermute x9, waiting for transfers between devices, over(): lax.ppermute(block, axis, [(i, (i + b) % count) for i in range(count)])  49.7 us
    ppermute x9, starting transfers between devices, over(): lax.ppermute(block, axis, [(i, (i + b) % count) for i in range(count)])  33.4 us
    ppermute x1, starting transfers between devices, shards(): first = lax.ppermute(taken, 'zh', swap)  26.1 us
    ppermute x1, waiting for transfers between devices, shards(): first = lax.ppermute(taken, 'zh', swap)  21.6 us
    pallas_call x2, Pallas kernels, expert(): pl.pallas_call(functools.partial(expert_kernel, len(far)), grid_spec=pltp...  21 us
    ppermute x1, waiting for transfers between devices, shards(): second = lax.ppermute(take(expert_weights, 1, first), 'zh', swap)  18.6 us
    all_to_all x2, starting transfers between devices, over_peers(): lax.all_to_all(message, ('y', 'c'), split_axis=0, concat_axis=0, tiled=True)  14.3 us
    all_to_all x2, waiting for transfers between devices, over_peers(): lax.all_to_all(message, ('y', 'c'), split_axis=0, concat_axis=0, tiled=True)  9.28 us
  transfers between devices with their start and end apart: 14, of which 6 were waited for; matrix products, arithmetic and copies ran while one was open for 2% of the time, Pallas kernels for 8%

profile of v5, /device:TPU:192, one launch (start us, length us, event | category | flops | bytes accessed | tf_op | source)
XLA Modules:
  0.0 236.6 jit_solution(4582149248111456677)
XLA Ops:
  6.5 0.7 convert_bitcast_fusion
  7.2 0.7 fusion.2
  7.9 1.1 pad_maximum_fusion.block.refs_0_
  9.0 2.6 %shard_map.46 = bf16[16,3,8,2048]{3,2,1,0:T(8,128)(2,1)} custom-call(s32[1]{0:T(128)} %bitcast.zl_ref, bf16[136,2048]{1,0:T(8,128)(2,1)S(1)} %pad_maximum_fusion.block.refs_0_), custom_call_target="tpu_custom_call" | custom-call | flops 201326592 | bytes 1572864 | tf_op jit(solution)/shard_map/pallas_call | solution.py:137
  11.6 7.3 %all-to-all-start = ((bf16[16,3,8,2048]{3,2,1,0:T(8,128)(2,1)}), bf16[16,3,8,2048]{3,2,1,0:T(8,128)(2,1)}, u32[]{:S(2)}, u32[]{:S(2)}) async-start(bf16[16,3,8,2048]{3,2,1,0:T(8,128)(2,1)} %shard_map.46), calls=%async_computation | async-start | bytes 3145728 | tf_op jit(solution)/shard_map/all_to_all | solution.py:327
  18.8 0.0 all-gather.3.cloned.1.call-start
  18.9 0.7 all-gather.3.cloned.1.call-update
  19.6 2.3 collective-permute-start
  21.8 2.7 %collective-permute-start.1 = (bf16[136,2048]{1,0:T(8,128)(2,1)S(1)}, bf16[136,2048]{1,0:T(8,128)(2,1)S(1)}, u32[]{:S(2)}, u32[]{:S(2)}) collective-permute-start(bf16[136,2048]{1,0:T(8,128)(2,1)S(1)} %pad_maximum_fusion.block.refs_0_), channel_id=1, source_target_pairs={{0,32},{16,48},{32,0},{48,16},{1,33},{17,49},{33,1},{49,17},{2,34}... | collective-permute-start | bytes 1671176 | tf_op jit(solution)/shard_map/ppermute | solution.py:321
  24.5 2.8 %collective-permute-start.2 = (bf16[136,2048]{1,0:T(8,128)(2,1)S(1)}, bf16[136,2048]{1,0:T(8,128)(2,1)S(1)}, u32[]{:S(2)}, u32[]{:S(2)}) collective-permute-start(bf16[136,2048]{1,0:T(8,128)(2,1)S(1)} %pad_maximum_fusion.block.refs_0_), channel_id=1, source_target_pairs={{0,48},{16,0},{32,16},{48,32},{1,49},{17,1},{33,17},{49,33},{2,50}... | collective-permute-start | bytes 1671176 | tf_op jit(solution)/shard_map/ppermute | solution.py:321
  27.4 9.0 %collective-permute-done.refs_1_ = bf16[136,2048]{1,0:T(8,128)(2,1)S(1)} collective-permute-done((bf16[136,2048]{1,0:T(8,128)(2,1)S(1)}, bf16[136,2048]{1,0:T(8,128)(2,1)S(1)}, u32[]{:S(2)}, u32[]{:S(2)}) %collective-permute-start) | collective-permute-done | bytes 557088 | tf_op jit(solution)/shard_map/ppermute | solution.py:321
  36.4 0.6 slice.25.refs_1_
  37.0 34.3 %collective-permute-done.1.refs_2_ = bf16[136,2048]{1,0:T(8,128)(2,1)S(1)} collective-permute-done((bf16[136,2048]{1,0:T(8,128)(2,1)S(1)}, bf16[136,2048]{1,0:T(8,128)(2,1)S(1)}, u32[]{:S(2)}, u32[]{:S(2)}) %collective-permute-start.1) | collective-permute-done | bytes 557088 | tf_op jit(solution)/shard_map/ppermute | solution.py:321
  71.2 0.6 slice.26.refs_2_
  71.8 0.0 collective-permute-done.2.refs_3_
  71.8 0.5 slice.27.refs_3_
  72.4 2.1 shard_map.47
  74.5 26.1 %collective-permute-start.3 = (bf16[256,1536]{1,0:T(8,128)(2,1)}, bf16[256,1536]{1,0:T(8,128)(2,1)S(1)}, u32[]{:S(2)}, u32[]{:S(2)}) collective-permute-start(bf16[256,1536]{1,0:T(8,128)(2,1)} %shard_map.47), channel_id=1, source_target_pairs={{0,256},{256,0},{1,257},{257,1},{2,258},{258,2},{3,259},{259,3},{4... | collective-permute-start | bytes 2359304 | tf_op jit(solution)/shard_map/ppermute | solution.py:379
  100.6 0.7 slice.28.refs_5_
  101.3 0.0 all-to-all-done.refs_1_.refs_3_
  101.3 0.7 slice_bitcast_fusion.refs_4_
  101.9 2.9 %shard_map.48 = bf16[16,7,8,2048]{3,2,1,0:T(8,128)(2,1)S(1)} custom-call(s32[1]{0:T(128)} %bitcast.zl_ref, bf16[136,2048]{1,0:T(8,128)(2,1)S(1)} %pad_maximum_fusion.block.refs_0_, bf16[136,2048]{1,0:T(8,128)(2,1)S(1)} %collective-permute-done.refs_1_, bf16[136,2048]{1,0:T(8,128)(2,1)S(1)} %collective-permute-done.1.refs_2_, ...), custom_call_target="tpu_custom_call" | custom-call | flops 805306368 | bytes 3670016 | tf_op jit(solution)/shard_map/pallas_call | solution.py:137
  104.8 0.0 copy-start
  104.8 1.9 copy-done
  106.7 7.0 %all-to-all-start.1 = ((bf16[16,7,8,2048]{3,2,1,0:T(8,128)(2,1)}), bf16[16,7,8,2048]{3,2,1,0:T(8,128)(2,1)}, u32[]{:S(2)}, u32[]{:S(2)}) async-start(bf16[16,7,8,2048]{3,2,1,0:T(8,128)(2,1)} %copy-done), calls=%async_computation.1 | async-start | bytes 7340032 | tf_op jit(solution)/shard_map/all_to_all | solution.py:327
  113.8 21.6 %collective-permute-done.3.refs_10_.refs_14_ = bf16[256,1536]{1,0:T(8,128)(2,1)S(1)} collective-permute-done((bf16[256,1536]{1,0:T(8,128)(2,1)}, bf16[256,1536]{1,0:T(8,128)(2,1)S(1)}, u32[]{:S(2)}, u32[]{:S(2)}) %collective-permute-start.3) | collective-permute-done | bytes 786464 | tf_op jit(solution)/shard_map/ppermute | solution.py:379
  135.3 0.0 copy-start.5
  135.3 0.6 slice.29.refs_1_
  135.9 2.1 shard_map.50
  138.0 4.3 %collective-permute-start.4 = (bf16[256,1536]{1,0:T(8,128)(2,1)}, bf16[256,1536]{1,0:T(8,128)(2,1)S(1)}, u32[]{:S(2)}, u32[]{:S(2)}) collective-permute-start(bf16[256,1536]{1,0:T(8,128)(2,1)} %shard_map.50), channel_id=1, source_target_pairs={{0,256},{256,0},{1,257},{257,1},{2,258},{258,2},{3,259},{259,3},{4... | collective-permute-start | bytes 2359304 | tf_op jit(solution)/shard_map/ppermute | solution.py:381
  142.3 4.8 %collective-permute-start.10 = (bf16[256,1536]{1,0:T(8,128)(2,1)S(1)}, bf16[256,1536]{1,0:T(8,128)(2,1)S(1)}, u32[]{:S(2)}, u32[]{:S(2)}) collective-permute-start(bf16[256,1536]{1,0:T(8,128)(2,1)S(1)} %collective-permute-done.3.refs_10_.refs_14_), channel_id=1, source_target_pairs={{0,192},{64,0},{128,64},{192,128},{1,193},{65,1},{129,65},{193,129... | collective-permute-start | bytes 2359304 | tf_op jit(solution)/shard_map/ppermute | solution.py:321
  147.2 1.9 collective-permute-start.8
  149.1 0.0 copy-done.5
  149.1 4.2 %collective-permute-start.9 = (bf16[256,1536]{1,0:T(8,128)(2,1)S(1)}, bf16[256,1536]{1,0:T(8,128)(2,1)}, u32[]{:S(2)}, u32[]{:S(2)}) collective-permute-start(bf16[256,1536]{1,0:T(8,128)(2,1)S(1)} %collective-permute-done.3.refs_10_.refs_14_), channel_id=1, source_target_pairs={{0,128},{64,192},{128,0},{192,64},{1,129},{65,193},{129,1},{193,65... | collective-permute-start | bytes 2359304 | tf_op jit(solution)/shard_map/ppermute | solution.py:321
  153.3 18.6 %collective-permute-done.4.refs_10_.refs_14_ = bf16[256,1536]{1,0:T(8,128)(2,1)S(1)} collective-permute-done((bf16[256,1536]{1,0:T(8,128)(2,1)}, bf16[256,1536]{1,0:T(8,128)(2,1)S(1)}, u32[]{:S(2)}, u32[]{:S(2)}) %collective-permute-start.4) | collective-permute-done | bytes 786464 | tf_op jit(solution)/shard_map/ppermute | solution.py:381
  171.9 0.0 copy-start.6
  171.9 6.7 %collective-permute-start.5 = (bf16[256,1536]{1,0:T(8,128)(2,1)S(1)}, bf16[256,1536]{1,0:T(8,128)(2,1)S(1)}, u32[]{:S(2)}, u32[]{:S(2)}) collective-permute-start(bf16[256,1536]{1,0:T(8,128)(2,1)S(1)} %collective-permute-done.4.refs_10_.refs_14_), channel_id=1, source_target_pairs={{0,64},{64,128},{128,192},{192,0},{1,65},{65,129},{129,193},{193,1... | collective-permute-start | bytes 2359304 | tf_op jit(solution)/shard_map/ppermute | solution.py:321
  178.6 3.5 %collective-permute-start.6 = (bf16[256,1536]{1,0:T(8,128)(2,1)S(1)}, bf16[256,1536]{1,0:T(8,128)(2,1)}, u32[]{:S(2)}, u32[]{:S(2)}) collective-permute-start(bf16[256,1536]{1,0:T(8,128)(2,1)S(1)} %collective-permute-done.4.refs_10_.refs_14_), channel_id=1, source_target_pairs={{0,128},{64,192},{128,0},{192,64},{1,129},{65,193},{129,1},{193,65... | collective-permute-start | bytes 2359304 | tf_op jit(solution)/shard_map/ppermute | solution.py:321
  182.0 0.0 collective-permute-done.10.refs_13_.refs_17_
  182.1 0.0 copy-start.8
  182.1 0.9 copy-done.8
  183.0 4.5 %collective-permute-start.7 = (bf16[256,1536]{1,0:T(8,128)(2,1)S(1)}, bf16[256,1536]{1,0:T(8,128)(2,1)}, u32[]{:S(2)}, u32[]{:S(2)}) collective-permute-start(bf16[256,1536]{1,0:T(8,128)(2,1)S(1)} %collective-permute-done.4.refs_10_.refs_14_), channel_id=1, source_target_pairs={{0,192},{64,0},{128,64},{192,128},{1,193},{65,1},{129,65},{193,129... | collective-permute-start | bytes 2359304 | tf_op jit(solution)/shard_map/ppermute | solution.py:321
  187.5 0.1 pad_add_fusion.where_ref.refs_0_
  187.6 0.0 copy-start.4
  187.6 9.3 %all-to-all-done.1.last_ref.refs_2_.refs_4_ = bf16[16,7,8,2048]{3,2,1,0:T(8,128)(2,1)} async-done(((bf16[16,7,8,2048]{3,2,1,0:T(8,128)(2,1)}), bf16[16,7,8,2048]{3,2,1,0:T(8,128)(2,1)}, u32[]{:S(2)}, u32[]{:S(2)}) %all-to-all-start.1) | async-done | bytes 3670048 | tf_op jit(solution)/shard_map/all_to_all | solution.py:327
  196.9 2.5 %shard_map.49 = (bf16[2,640,128]{2,1,0:T(8,128)(2,1)S(1)}, bf16[512,512]{1,0:T(8,128)(2,1)S(1)}, bf16[2,64,128]{2,1,0:T(8,128)(2,1)S(1)}) custom-call(s32[3]{0:T(128)S(1)} %pad_add_fusion.where_ref.refs_0_, bf16[16,7,8,2048]{3,2,1,0:T(8,128)(2,1)} %all-to-all-done.1.last_ref.refs_2_.refs_4_), custom_call_target="tpu_custom_call" | custom-call | flops 100000000 | bytes 1000000 | tf_op jit(solution)/shard_map/pallas_call | solution.py:210
  199.4 0.0 copy-done.6
  199.4 0.0 copy-done.4
  199.4 0.0 copy-start.1
  199.4 0.8 copy-done.1
  200.2 0.0 copy-start.2
  200.2 0.7 copy-done.2
  200.9 0.0 copy-start.3
  200.9 0.6 copy-done.3
  201.5 0.0 collective-permute-done.8.refs_11_.refs_15_
  201.5 0.0 collective-permute-done.9.refs_12_.refs_16_
  201.5 0.0 all-gather.3.cloned.1.call-done
  201.5 10.5 %shard_map.51.refs_18_ = bf16[2,9,64,768]{3,2,1,0:T(8,128)(2,1)} custom-call(s32[3]{0:T(128)} %copy-done.4, bf16[16,3,8,2048]{3,2,1,0:T(8,128)(2,1)} %all-to-all-done.refs_1_.refs_3_, bf16[16,7,8,2048]{3,2,1,0:T(8,128)(2,1)} %all-to-all-done.1.last_ref.refs_2_.refs_4_, bf16[16,3,8,2048]{3,2,1,0:T(8,128)(2,1)} %all-to-all-done.refs_1_.refs_3_, ...), custom_call_target="tpu_custom_call" | custom-call | flops 3000000000 | bytes 10000000 | tf_op jit(solution)/shard_map/pallas_call | solution.py:286
  212.0 6.4 %collective-permute-done.5.refs_11_.refs_15_ = bf16[256,1536]{1,0:T(8,128)(2,1)S(1)} collective-permute-done((bf16[256,1536]{1,0:T(8,128)(2,1)S(1)}, bf16[256,1536]{1,0:T(8,128)(2,1)S(1)}, u32[]{:S(2)}, u32[]{:S(2)}) %collective-permute-start.5) | collective-permute-done | bytes 786464 | tf_op jit(solution)/shard_map/ppermute | solution.py:321
  218.4 0.0 copy-start.7
  218.4 0.0 collective-permute-done.6.refs_12_.refs_16_
  218.4 0.0 collective-permute-done.7.refs_13_.refs_17_
  218.4 0.9 copy-done.7
  219.3 10.5 %shard_map.52 = bf16[2,9,64,768]{3,2,1,0:T(8,128)(2,1)} custom-call(s32[3]{0:T(128)} %copy-done.4, bf16[16,3,8,2048]{3,2,1,0:T(8,128)(2,1)} %all-to-all-done.refs_1_.refs_3_, bf16[16,7,8,2048]{3,2,1,0:T(8,128)(2,1)} %all-to-all-done.1.last_ref.refs_2_.refs_4_, ...), custom_call_target="tpu_custom_call", output_to_operand_aliasing={{}: (18, {})} | custom-call | flops 4026531840 | bytes 10000000 | tf_op jit(solution)/shard_map/pallas_call | solution.py:286
Async XLA Ops:
  11.6 89.7 %all-to-all-start = ((bf16[16,3,8,2048]{3,2,1,0:T(8,128)(2,1)}), bf16[16,3,8,2048]{3,2,1,0:T(8,128)(2,1)}, u32[]{:S(2)}, u32[]{:S(2)}) async-start(bf16[16,3,8,2048]{3,2,1,0:T(8,128)(2,1)} %shard_map.46), calls=%async_computation | async-start | bytes 3145728 | tf_op jit(solution)/shard_map/all_to_all | solution.py:327
  18.8 182.7 %all-gather.3.cloned.1.call-start = ((), (), s32[]{:S(2)}) async-start(), calls=%async_computation.2 | async-start | bytes 7864320 | tf_op jit(solution)/shard_map/all_gather | solution.py:375
  19.6 16.8 %collective-permute-start = (bf16[136,2048]{1,0:T(8,128)(2,1)S(1)}, bf16[136,2048]{1,0:T(8,128)(2,1)S(1)}, u32[]{:S(2)}, u32[]{:S(2)}) collective-permute-start(bf16[136,2048]{1,0:T(8,128)(2,1)S(1)} %pad_maximum_fusion.block.refs_0_), channel_id=1, source_target_pairs={{0,16},{16,32},{32,48},{48,0},{1,17},{17,33},{33,49},{49,1},{2,18}... | collective-permute-start | bytes 1671176 | tf_op jit(solution)/shard_map/ppermute | solution.py:321
  21.8 49.4 %collective-permute-start.1 = (bf16[136,2048]{1,0:T(8,128)(2,1)S(1)}, bf16[136,2048]{1,0:T(8,128)(2,1)S(1)}, u32[]{:S(2)}, u32[]{:S(2)}) collective-permute-start(bf16[136,2048]{1,0:T(8,128)(2,1)S(1)} %pad_maximum_fusion.block.refs_0_), channel_id=1, source_target_pairs={{0,32},{16,48},{32,0},{48,16},{1,33},{17,49},{33,1},{49,17},{2,34}... | collective-permute-start | bytes 1671176 | tf_op jit(solution)/shard_map/ppermute | solution.py:321
  24.5 47.3 %collective-permute-start.2 = (bf16[136,2048]{1,0:T(8,128)(2,1)S(1)}, bf16[136,2048]{1,0:T(8,128)(2,1)S(1)}, u32[]{:S(2)}, u32[]{:S(2)}) collective-permute-start(bf16[136,2048]{1,0:T(8,128)(2,1)S(1)} %pad_maximum_fusion.block.refs_0_), channel_id=1, source_target_pairs={{0,48},{16,0},{32,16},{48,32},{1,49},{17,1},{33,17},{49,33},{2,50}... | collective-permute-start | bytes 1671176 | tf_op jit(solution)/shard_map/ppermute | solution.py:321
  74.5 60.9 %collective-permute-start.3 = (bf16[256,1536]{1,0:T(8,128)(2,1)}, bf16[256,1536]{1,0:T(8,128)(2,1)S(1)}, u32[]{:S(2)}, u32[]{:S(2)}) collective-permute-start(bf16[256,1536]{1,0:T(8,128)(2,1)} %shard_map.47), channel_id=1, source_target_pairs={{0,256},{256,0},{1,257},{257,1},{2,258},{258,2},{3,259},{259,3},{4... | collective-permute-start | bytes 2359304 | tf_op jit(solution)/shard_map/ppermute | solution.py:379
  104.8 1.9 copy-start
  106.7 90.1 %all-to-all-start.1 = ((bf16[16,7,8,2048]{3,2,1,0:T(8,128)(2,1)}), bf16[16,7,8,2048]{3,2,1,0:T(8,128)(2,1)}, u32[]{:S(2)}, u32[]{:S(2)}) async-start(bf16[16,7,8,2048]{3,2,1,0:T(8,128)(2,1)} %copy-done), calls=%async_computation.1 | async-start | bytes 7340032 | tf_op jit(solution)/shard_map/all_to_all | solution.py:327
  135.3 13.8 %copy-start.5 = (bf16[256,1536]{1,0:T(8,128)(2,1)}, bf16[256,1536]{1,0:T(8,128)(2,1)S(1)}, u32[]{:S(2)}) copy-start(bf16[256,1536]{1,0:T(8,128)(2,1)S(1)} %collective-permute-done.3.refs_10_.refs_14_) | copy-start | bytes 2359300
  138.0 33.9 %collective-permute-start.4 = (bf16[256,1536]{1,0:T(8,128)(2,1)}, bf16[256,1536]{1,0:T(8,128)(2,1)S(1)}, u32[]{:S(2)}, u32[]{:S(2)}) collective-permute-start(bf16[256,1536]{1,0:T(8,128)(2,1)} %shard_map.50), channel_id=1, source_target_pairs={{0,256},{256,0},{1,257},{257,1},{2,258},{258,2},{3,259},{259,3},{4... | collective-permute-start | bytes 2359304 | tf_op jit(solution)/shard_map/ppermute | solution.py:381
  142.3 39.7 %collective-permute-start.10 = (bf16[256,1536]{1,0:T(8,128)(2,1)S(1)}, bf16[256,1536]{1,0:T(8,128)(2,1)S(1)}, u32[]{:S(2)}, u32[]{:S(2)}) collective-permute-start(bf16[256,1536]{1,0:T(8,128)(2,1)S(1)} %collective-permute-done.3.refs_10_.refs_14_), channel_id=1, source_target_pairs={{0,192},{64,0},{128,64},{192,128},{1,193},{65,1},{129,65},{193,129... | collective-permute-start | bytes 2359304 | tf_op jit(solution)/shard_map/ppermute | solution.py:321
  147.2 54.4 %collective-permute-start.8 = (bf16[256,1536]{1,0:T(8,128)(2,1)S(1)}, bf16[256,1536]{1,0:T(8,128)(2,1)}, u32[]{:S(2)}, u32[]{:S(2)}) collective-permute-start(bf16[256,1536]{1,0:T(8,128)(2,1)S(1)} %collective-permute-done.3.refs_10_.refs_14_), channel_id=1, source_target_pairs={{0,64},{64,128},{128,192},{192,0},{1,65},{65,129},{129,193},{193,1... | collective-permute-start | bytes 2359304 | tf_op jit(solution)/shard_map/ppermute | solution.py:321
  149.1 52.4 %collective-permute-start.9 = (bf16[256,1536]{1,0:T(8,128)(2,1)S(1)}, bf16[256,1536]{1,0:T(8,128)(2,1)}, u32[]{:S(2)}, u32[]{:S(2)}) collective-permute-start(bf16[256,1536]{1,0:T(8,128)(2,1)S(1)} %collective-permute-done.3.refs_10_.refs_14_), channel_id=1, source_target_pairs={{0,128},{64,192},{128,0},{192,64},{1,129},{65,193},{129,1},{193,65... | collective-permute-start | bytes 2359304 | tf_op jit(solution)/shard_map/ppermute | solution.py:321
  171.9 27.5 %copy-start.6 = (bf16[256,1536]{1,0:T(8,128)(2,1)}, bf16[256,1536]{1,0:T(8,128)(2,1)S(1)}, u32[]{:S(2)}) copy-start(bf16[256,1536]{1,0:T(8,128)(2,1)S(1)} %collective-permute-done.4.refs_10_.refs_14_) | copy-start | bytes 2359300
  171.9 46.5 %collective-permute-start.5 = (bf16[256,1536]{1,0:T(8,128)(2,1)S(1)}, bf16[256,1536]{1,0:T(8,128)(2,1)S(1)}, u32[]{:S(2)}, u32[]{:S(2)}) collective-permute-start(bf16[256,1536]{1,0:T(8,128)(2,1)S(1)} %collective-permute-done.4.refs_10_.refs_14_), channel_id=1, source_target_pairs={{0,64},{64,128},{128,192},{192,0},{1,65},{65,129},{129,193},{193,1... | collective-permute-start | bytes 2359304 | tf_op jit(solution)/shard_map/ppermute | solution.py:321
  178.6 39.8 %collective-permute-start.6 = (bf16[256,1536]{1,0:T(8,128)(2,1)S(1)}, bf16[256,1536]{1,0:T(8,128)(2,1)}, u32[]{:S(2)}, u32[]{:S(2)}) collective-permute-start(bf16[256,1536]{1,0:T(8,128)(2,1)S(1)} %collective-permute-done.4.refs_10_.refs_14_), channel_id=1, source_target_pairs={{0,128},{64,192},{128,0},{192,64},{1,129},{65,193},{129,1},{193,65... | collective-permute-start | bytes 2359304 | tf_op jit(solution)/shard_map/ppermute | solution.py:321
  182.1 0.9 copy-start.8
  183.0 35.4 %collective-permute-start.7 = (bf16[256,1536]{1,0:T(8,128)(2,1)S(1)}, bf16[256,1536]{1,0:T(8,128)(2,1)}, u32[]{:S(2)}, u32[]{:S(2)}) collective-permute-start(bf16[256,1536]{1,0:T(8,128)(2,1)S(1)} %collective-permute-done.4.refs_10_.refs_14_), channel_id=1, source_target_pairs={{0,192},{64,0},{128,64},{192,128},{1,193},{65,1},{129,65},{193,129... | collective-permute-start | bytes 2359304 | tf_op jit(solution)/shard_map/ppermute | solution.py:321
  187.6 11.8 %copy-start.4 = (s32[3]{0:T(128)}, s32[3]{0:T(128)S(1)}, u32[]{:S(2)}) copy-start(s32[3]{0:T(128)S(1)} %pad_add_fusion.where_ref.refs_0_) | copy-start | bytes 40
  199.4 0.8 copy-start.1
  200.2 0.7 copy-start.2
  200.9 0.6 copy-start.3
  218.4 0.9 copy-start.7
Sparse Core Ops, SparseCore 0:
  21.8 73.4 all-gather.2

commit v6 on v5

--- a/solution.py
+++ b/solution.py
@@ -23,7 +23,7 @@
 TILE = 256
 INFO = 2 * TOK
 
-TAKE_COST = (0, 55 * 10**9)
+TAKE_COST = (40 * 10**9, 0 * 10**9)
 f32 = jnp.float32
 bf16 = jnp.bfloat16
 

time: 237 us -> 229 us (0.966)
  the two profiles are of different devices: /device:TPU:192 before, /device:TPU:64 now
where the time goes in v6:
time: 229 us; the launch traced here: 228 us
  waiting for transfers between devices  105 us (46%)
  starting transfers between devices  64.9 us (28%)
  Pallas kernels  33.2 us (14%)
  between operations  13.6 us (6%)
  local copies, waits for them, and re-layouts  8.53 us (4%)
  other arithmetic  2.53 us (1%)
    ppermute x9, waiting for transfers between devices, over(): lax.ppermute(block, axis, [(i, (i + b) % count) for i in range(count)])  50.2 us
    ppermute x9, starting transfers between devices, over(): lax.ppermute(block, axis, [(i, (i + b) % count) for i in range(count)])  37.5 us
    ppermute x1, waiting for transfers between devices, shards(): first = lax.ppermute(taken, 'zh', swap)  35 us
    pallas_call x2, Pallas kernels, expert(): pl.pallas_call(functools.partial(expert_kernel, len(far)), grid_spec=pltp...  21.1 us
    ppermute x1, waiting for transfers between devices, shards(): second = lax.ppermute(take(expert_weights, 1, first), 'zh', swap)  17.7 us
    all_to_all x2, starting transfers between devices, over_peers(): lax.all_to_all(message, ('y', 'c'), split_axis=0, concat_axis=0, tiled=True)  11.6 us
    ppermute x1, starting transfers between devices, shards(): first = lax.ppermute(taken, 'zh', swap)  8.49 us
    ppermute x1, starting transfers between devices, shards(): second = lax.ppermute(take(expert_weights, 1, first), 'zh', swap)  7.24 us
  transfers between devices with their start and end apart: 14, of which 8 were waited for; matrix products, arithmetic and copies ran while one was open for 2% of the time, Pallas kernels for 10%

profile of v6, /device:TPU:64, one launch (start us, length us, event | category | flops | bytes accessed | tf_op | source)
XLA Modules:
  0.0 228.2 jit_solution(15665849349513264332)
XLA Ops:
  6.5 0.7 convert_bitcast_fusion
  7.2 0.7 fusion.2
  7.9 1.1 pad_maximum_fusion.block.refs_0_
  9.0 4.3 %collective-permute-start = (bf16[136,2048]{1,0:T(8,128)(2,1)S(1)}, bf16[136,2048]{1,0:T(8,128)(2,1)S(1)}, u32[]{:S(2)}, u32[]{:S(2)}) collective-permute-start(bf16[136,2048]{1,0:T(8,128)(2,1)S(1)} %pad_maximum_fusion.block.refs_0_), channel_id=1, source_target_pairs={{0,16},{16,32},{32,48},{48,0},{1,17},{17,33},{33,49},{49,1},{2,18}... | collective-permute-start | bytes 1671176 | tf_op jit(solution)/shard_map/ppermute | solution.py:321
  13.3 6.9 %collective-permute-start.1 = (bf16[136,2048]{1,0:T(8,128)(2,1)S(1)}, bf16[136,2048]{1,0:T(8,128)(2,1)S(1)}, u32[]{:S(2)}, u32[]{:S(2)}) collective-permute-start(bf16[136,2048]{1,0:T(8,128)(2,1)S(1)} %pad_maximum_fusion.block.refs_0_), channel_id=1, source_target_pairs={{0,32},{16,48},{32,0},{48,16},{1,33},{17,49},{33,1},{49,17},{2,34}... | collective-permute-start | bytes 1671176 | tf_op jit(solution)/shard_map/ppermute | solution.py:321
  20.2 1.9 collective-permute-start.2
  22.1 2.6 %shard_map.46 = bf16[16,3,8,2048]{3,2,1,0:T(8,128)(2,1)} custom-call(s32[1]{0:T(128)} %bitcast.zl_ref, bf16[136,2048]{1,0:T(8,128)(2,1)S(1)} %pad_maximum_fusion.block.refs_0_), custom_call_target="tpu_custom_call" | custom-call | flops 201326592 | bytes 1572864 | tf_op jit(solution)/shard_map/pallas_call | solution.py:137
  24.7 6.1 %all-to-all-start = ((bf16[16,3,8,2048]{3,2,1,0:T(8,128)(2,1)}), bf16[16,3,8,2048]{3,2,1,0:T(8,128)(2,1)}, u32[]{:S(2)}, u32[]{:S(2)}) async-start(bf16[16,3,8,2048]{3,2,1,0:T(8,128)(2,1)} %shard_map.46), calls=%async_computation | async-start | bytes 3145728 | tf_op jit(solution)/shard_map/all_to_all | solution.py:327
  30.8 0.0 all-gather.3.cloned.1.call-start
  30.8 0.7 all-gather.3.cloned.1.call-update
  31.5 18.6 %collective-permute-done.refs_1_ = bf16[136,2048]{1,0:T(8,128)(2,1)S(1)} collective-permute-done((bf16[136,2048]{1,0:T(8,128)(2,1)S(1)}, bf16[136,2048]{1,0:T(8,128)(2,1)S(1)}, u32[]{:S(2)}, u32[]{:S(2)}) %collective-permute-start) | collective-permute-done | bytes 557088 | tf_op jit(solution)/shard_map/ppermute | solution.py:321
  50.2 0.6 slice.25.refs_1_
  50.7 10.2 %collective-permute-done.1.refs_2_ = bf16[136,2048]{1,0:T(8,128)(2,1)S(1)} collective-permute-done((bf16[136,2048]{1,0:T(8,128)(2,1)S(1)}, bf16[136,2048]{1,0:T(8,128)(2,1)S(1)}, u32[]{:S(2)}, u32[]{:S(2)}) %collective-permute-start.1) | collective-permute-done | bytes 557088 | tf_op jit(solution)/shard_map/ppermute | solution.py:321
  61.0 0.5 slice.26.refs_2_
  61.5 2.1 collective-permute-done.2.refs_3_
  63.6 0.6 slice.27.refs_3_
  64.1 2.1 shard_map.47
  66.2 0.6 slice.28.refs_5_
  66.9 1.8 all-to-all-done.refs_1_.refs_3_
  68.7 0.7 slice_bitcast_fusion.refs_4_
  69.4 2.9 %shard_map.48 = bf16[16,7,8,2048]{3,2,1,0:T(8,128)(2,1)S(1)} custom-call(s32[1]{0:T(128)} %bitcast.zl_ref, bf16[136,2048]{1,0:T(8,128)(2,1)S(1)} %pad_maximum_fusion.block.refs_0_, bf16[136,2048]{1,0:T(8,128)(2,1)S(1)} %collective-permute-done.refs_1_, bf16[136,2048]{1,0:T(8,128)(2,1)S(1)} %collective-permute-done.1.refs_2_, ...), custom_call_target="tpu_custom_call" | custom-call | flops 805306368 | bytes 3670016 | tf_op jit(solution)/shard_map/pallas_call | solution.py:137
  72.2 0.0 copy-start
  72.2 1.9 copy-done
  74.2 0.0 copy-start.9
  74.2 5.5 %all-to-all-start.1 = ((bf16[16,7,8,2048]{3,2,1,0:T(8,128)(2,1)}), bf16[16,7,8,2048]{3,2,1,0:T(8,128)(2,1)}, u32[]{:S(2)}, u32[]{:S(2)}) async-start(bf16[16,7,8,2048]{3,2,1,0:T(8,128)(2,1)} %copy-done), calls=%async_computation.1 | async-start | bytes 7340032 | tf_op jit(solution)/shard_map/all_to_all | solution.py:327
  79.7 0.0 copy-done.9
  79.7 8.5 %collective-permute-start.3 = (bf16[256,1536]{1,0:T(8,128)(2,1)S(1)}, bf16[256,1536]{1,0:T(8,128)(2,1)S(1)}, u32[]{:S(2)}, u32[]{:S(2)}) collective-permute-start(bf16[256,1536]{1,0:T(8,128)(2,1)S(1)} %copy-done.9), channel_id=1, source_target_pairs={{0,256},{256,0},{1,257},{257,1},{2,258},{258,2},{3,259},{259,3},{4... | collective-permute-start | bytes 2359304 | tf_op jit(solution)/shard_map/ppermute | solution.py:379
  88.2 35.0 %collective-permute-done.3.refs_10_.refs_14_ = bf16[256,1536]{1,0:T(8,128)(2,1)S(1)} collective-permute-done((bf16[256,1536]{1,0:T(8,128)(2,1)S(1)}, bf16[256,1536]{1,0:T(8,128)(2,1)S(1)}, u32[]{:S(2)}, u32[]{:S(2)}) %collective-permute-start.3) | collective-permute-done | bytes 786464 | tf_op jit(solution)/shard_map/ppermute | solution.py:379
  123.3 0.0 copy-start.5
  123.3 0.6 slice.29.refs_1_
  123.9 2.1 shard_map.50
  125.9 7.2 %collective-permute-start.4 = (bf16[256,1536]{1,0:T(8,128)(2,1)}, bf16[256,1536]{1,0:T(8,128)(2,1)S(1)}, u32[]{:S(2)}, u32[]{:S(2)}) collective-permute-start(bf16[256,1536]{1,0:T(8,128)(2,1)} %shard_map.50), channel_id=1, source_target_pairs={{0,256},{256,0},{1,257},{257,1},{2,258},{258,2},{3,259},{259,3},{4... | collective-permute-start | bytes 2359304 | tf_op jit(solution)/shard_map/ppermute | solution.py:381
  133.2 4.7 %collective-permute-start.10 = (bf16[256,1536]{1,0:T(8,128)(2,1)S(1)}, bf16[256,1536]{1,0:T(8,128)(2,1)S(1)}, u32[]{:S(2)}, u32[]{:S(2)}) collective-permute-start(bf16[256,1536]{1,0:T(8,128)(2,1)S(1)} %collective-permute-done.3.refs_10_.refs_14_), channel_id=1, source_target_pairs={{0,192},{64,0},{128,64},{192,128},{1,193},{65,1},{129,65},{193,129... | collective-permute-start | bytes 2359304 | tf_op jit(solution)/shard_map/ppermute | solution.py:321
  137.8 1.9 collective-permute-start.8
  139.8 4.2 %collective-permute-start.9 = (bf16[256,1536]{1,0:T(8,128)(2,1)S(1)}, bf16[256,1536]{1,0:T(8,128)(2,1)}, u32[]{:S(2)}, u32[]{:S(2)}) collective-permute-start(bf16[256,1536]{1,0:T(8,128)(2,1)S(1)} %collective-permute-done.3.refs_10_.refs_14_), channel_id=1, source_target_pairs={{0,128},{64,192},{128,0},{192,64},{1,129},{65,193},{129,1},{193,65... | collective-permute-start | bytes 2359304 | tf_op jit(solution)/shard_map/ppermute | solution.py:321
  144.0 17.7 %collective-permute-done.4.refs_10_.refs_14_ = bf16[256,1536]{1,0:T(8,128)(2,1)S(1)} collective-permute-done((bf16[256,1536]{1,0:T(8,128)(2,1)}, bf16[256,1536]{1,0:T(8,128)(2,1)S(1)}, u32[]{:S(2)}, u32[]{:S(2)}) %collective-permute-start.4) | collective-permute-done | bytes 786464 | tf_op jit(solution)/shard_map/ppermute | solution.py:381
  161.7 0.0 copy-start.6
  161.7 3.4 %collective-permute-start.5 = (bf16[256,1536]{1,0:T(8,128)(2,1)S(1)}, bf16[256,1536]{1,0:T(8,128)(2,1)S(1)}, u32[]{:S(2)}, u32[]{:S(2)}) collective-permute-start(bf16[256,1536]{1,0:T(8,128)(2,1)S(1)} %collective-permute-done.4.refs_10_.refs_14_), channel_id=1, source_target_pairs={{0,64},{64,128},{128,192},{192,0},{1,65},{65,129},{129,193},{193,1... | collective-permute-start | bytes 2359304 | tf_op jit(solution)/shard_map/ppermute | solution.py:321
  165.1 4.6 %collective-permute-start.6 = (bf16[256,1536]{1,0:T(8,128)(2,1)S(1)}, bf16[256,1536]{1,0:T(8,128)(2,1)}, u32[]{:S(2)}, u32[]{:S(2)}) collective-permute-start(bf16[256,1536]{1,0:T(8,128)(2,1)S(1)} %collective-permute-done.4.refs_10_.refs_14_), channel_id=1, source_target_pairs={{0,128},{64,192},{128,0},{192,64},{1,129},{65,193},{129,1},{193,65... | collective-permute-start | bytes 2359304 | tf_op jit(solution)/shard_map/ppermute | solution.py:321
  169.7 19.2 %collective-permute-done.10.refs_13_.refs_17_ = bf16[256,1536]{1,0:T(8,128)(2,1)S(1)} collective-permute-done((bf16[256,1536]{1,0:T(8,128)(2,1)S(1)}, bf16[256,1536]{1,0:T(8,128)(2,1)S(1)}, u32[]{:S(2)}, u32[]{:S(2)}) %collective-permute-start.10) | collective-permute-done | bytes 786464 | tf_op jit(solution)/shard_map/ppermute | solution.py:321
  188.9 0.0 copy-start.8
  188.9 5.6 %collective-permute-start.7 = (bf16[256,1536]{1,0:T(8,128)(2,1)S(1)}, bf16[256,1536]{1,0:T(8,128)(2,1)}, u32[]{:S(2)}, u32[]{:S(2)}) collective-permute-start(bf16[256,1536]{1,0:T(8,128)(2,1)S(1)} %collective-permute-done.4.refs_10_.refs_14_), channel_id=1, source_target_pairs={{0,192},{64,0},{128,64},{192,128},{1,193},{65,1},{129,65},{193,129... | collective-permute-start | bytes 2359304 | tf_op jit(solution)/shard_map/ppermute | solution.py:321
  194.5 0.1 pad_add_fusion.where_ref.refs_0_
  194.6 0.0 copy-start.4
  194.6 0.0 all-to-all-done.1.last_ref.refs_2_.refs_4_
  194.6 2.5 %shard_map.49 = (bf16[2,640,128]{2,1,0:T(8,128)(2,1)S(1)}, bf16[512,512]{1,0:T(8,128)(2,1)S(1)}, bf16[2,64,128]{2,1,0:T(8,128)(2,1)S(1)}) custom-call(s32[3]{0:T(128)S(1)} %pad_add_fusion.where_ref.refs_0_, bf16[16,7,8,2048]{3,2,1,0:T(8,128)(2,1)} %all-to-all-done.1.last_ref.refs_2_.refs_4_), custom_call_target="tpu_custom_call" | custom-call | flops 100000000 | bytes 1000000 | tf_op jit(solution)/shard_map/pallas_call | solution.py:210
  197.1 0.0 copy-done.5
  197.1 0.0 copy-done.6
  197.1 0.0 copy-done.8
  197.2 0.0 copy-done.4
  197.2 0.0 copy-start.1
  197.2 0.8 copy-done.1
  198.0 0.0 copy-start.2
  198.0 0.7 copy-done.2
  198.7 0.0 copy-start.3
  198.7 0.6 copy-done.3
  199.3 0.0 collective-permute-done.8.refs_11_.refs_15_
  199.3 0.0 collective-permute-done.9.refs_12_.refs_16_
  199.3 10.6 %shard_map.51.refs_18_ = bf16[2,9,64,768]{3,2,1,0:T(8,128)(2,1)} custom-call(s32[3]{0:T(128)} %copy-done.4, bf16[16,3,8,2048]{3,2,1,0:T(8,128)(2,1)} %all-to-all-done.refs_1_.refs_3_, bf16[16,7,8,2048]{3,2,1,0:T(8,128)(2,1)} %all-to-all-done.1.last_ref.refs_2_.refs_4_, bf16[16,3,8,2048]{3,2,1,0:T(8,128)(2,1)} %all-to-all-done.refs_1_.refs_3_, ...), custom_call_target="tpu_custom_call" | custom-call | flops 3000000000 | bytes 10000000 | tf_op jit(solution)/shard_map/pallas_call | solution.py:286
  209.9 0.1 collective-permute-done.5.refs_11_.refs_15_
  210.0 0.0 collective-permute-done.6.refs_12_.refs_16_
  210.0 0.0 collective-permute-done.7.refs_13_.refs_17_
  210.0 0.9 copy-done.7
  210.8 10.5 %shard_map.52 = bf16[2,9,64,768]{3,2,1,0:T(8,128)(2,1)} custom-call(s32[3]{0:T(128)} %copy-done.4, bf16[16,3,8,2048]{3,2,1,0:T(8,128)(2,1)} %all-to-all-done.refs_1_.refs_3_, bf16[16,7,8,2048]{3,2,1,0:T(8,128)(2,1)} %all-to-all-done.1.last_ref.refs_2_.refs_4_, ...), custom_call_target="tpu_custom_call", output_to_operand_aliasing={{}: (18, {})} | custom-call | flops 4026531840 | bytes 10000000 | tf_op jit(solution)/shard_map/pallas_call | solution.py:286
  (2 shorter events, 0.0 us)
Async XLA Ops:
  9.0 41.2 %collective-permute-start = (bf16[136,2048]{1,0:T(8,128)(2,1)S(1)}, bf16[136,2048]{1,0:T(8,128)(2,1)S(1)}, u32[]{:S(2)}, u32[]{:S(2)}) collective-permute-start(bf16[136,2048]{1,0:T(8,128)(2,1)S(1)} %pad_maximum_fusion.block.refs_0_), channel_id=1, source_target_pairs={{0,16},{16,32},{32,48},{48,0},{1,17},{17,33},{33,49},{49,1},{2,18}... | collective-permute-start | bytes 1671176 | tf_op jit(solution)/shard_map/ppermute | solution.py:321
  13.3 47.7 %collective-permute-start.1 = (bf16[136,2048]{1,0:T(8,128)(2,1)S(1)}, bf16[136,2048]{1,0:T(8,128)(2,1)S(1)}, u32[]{:S(2)}, u32[]{:S(2)}) collective-permute-start(bf16[136,2048]{1,0:T(8,128)(2,1)S(1)} %pad_maximum_fusion.block.refs_0_), channel_id=1, source_target_pairs={{0,32},{16,48},{32,0},{48,16},{1,33},{17,49},{33,1},{49,17},{2,34}... | collective-permute-start | bytes 1671176 | tf_op jit(solution)/shard_map/ppermute | solution.py:321
  20.2 43.3 %collective-permute-start.2 = (bf16[136,2048]{1,0:T(8,128)(2,1)S(1)}, bf16[136,2048]{1,0:T(8,128)(2,1)S(1)}, u32[]{:S(2)}, u32[]{:S(2)}) collective-permute-start(bf16[136,2048]{1,0:T(8,128)(2,1)S(1)} %pad_maximum_fusion.block.refs_0_), channel_id=1, source_target_pairs={{0,48},{16,0},{32,16},{48,32},{1,49},{17,1},{33,17},{49,33},{2,50}... | collective-permute-start | bytes 1671176 | tf_op jit(solution)/shard_map/ppermute | solution.py:321
  24.7 44.0 %all-to-all-start = ((bf16[16,3,8,2048]{3,2,1,0:T(8,128)(2,1)}), bf16[16,3,8,2048]{3,2,1,0:T(8,128)(2,1)}, u32[]{:S(2)}, u32[]{:S(2)}) async-start(bf16[16,3,8,2048]{3,2,1,0:T(8,128)(2,1)} %shard_map.46), calls=%async_computation | async-start | bytes 3145728 | tf_op jit(solution)/shard_map/all_to_all | solution.py:327
  30.8 168.5 %all-gather.3.cloned.1.call-start = ((), (), s32[]{:S(2)}) async-start(), calls=%async_computation.2 | async-start | bytes 7864320 | tf_op jit(solution)/shard_map/all_gather | solution.py:375
  72.2 1.9 copy-start
  74.2 5.6 %copy-start.9 = (bf16[256,1536]{1,0:T(8,128)(2,1)S(1)}, bf16[256,1536]{1,0:T(8,128)(2,1)}, u32[]{:S(2)}) copy-start(bf16[256,1536]{1,0:T(8,128)(2,1)} %shard_map.47) | copy-start | bytes 2359300
  74.2 120.4 %all-to-all-start.1 = ((bf16[16,7,8,2048]{3,2,1,0:T(8,128)(2,1)}), bf16[16,7,8,2048]{3,2,1,0:T(8,128)(2,1)}, u32[]{:S(2)}, u32[]{:S(2)}) async-start(bf16[16,7,8,2048]{3,2,1,0:T(8,128)(2,1)} %copy-done), calls=%async_computation.1 | async-start | bytes 7340032 | tf_op jit(solution)/shard_map/all_to_all | solution.py:327
  79.7 43.5 %collective-permute-start.3 = (bf16[256,1536]{1,0:T(8,128)(2,1)S(1)}, bf16[256,1536]{1,0:T(8,128)(2,1)S(1)}, u32[]{:S(2)}, u32[]{:S(2)}) collective-permute-start(bf16[256,1536]{1,0:T(8,128)(2,1)S(1)} %copy-done.9), channel_id=1, source_target_pairs={{0,256},{256,0},{1,257},{257,1},{2,258},{258,2},{3,259},{259,3},{4... | collective-permute-start | bytes 2359304 | tf_op jit(solution)/shard_map/ppermute | solution.py:379
  123.3 73.9 %copy-start.5 = (bf16[256,1536]{1,0:T(8,128)(2,1)}, bf16[256,1536]{1,0:T(8,128)(2,1)S(1)}, u32[]{:S(2)}) copy-start(bf16[256,1536]{1,0:T(8,128)(2,1)S(1)} %collective-permute-done.3.refs_10_.refs_14_) | copy-start | bytes 2359300
  125.9 35.7 %collective-permute-start.4 = (bf16[256,1536]{1,0:T(8,128)(2,1)}, bf16[256,1536]{1,0:T(8,128)(2,1)S(1)}, u32[]{:S(2)}, u32[]{:S(2)}) collective-permute-start(bf16[256,1536]{1,0:T(8,128)(2,1)} %shard_map.50), channel_id=1, source_target_pairs={{0,256},{256,0},{1,257},{257,1},{2,258},{258,2},{3,259},{259,3},{4... | collective-permute-start | bytes 2359304 | tf_op jit(solution)/shard_map/ppermute | solution.py:381
  133.2 55.7 %collective-permute-start.10 = (bf16[256,1536]{1,0:T(8,128)(2,1)S(1)}, bf16[256,1536]{1,0:T(8,128)(2,1)S(1)}, u32[]{:S(2)}, u32[]{:S(2)}) collective-permute-start(bf16[256,1536]{1,0:T(8,128)(2,1)S(1)} %collective-permute-done.3.refs_10_.refs_14_), channel_id=1, source_target_pairs={{0,192},{64,0},{128,64},{192,128},{1,193},{65,1},{129,65},{193,129... | collective-permute-start | bytes 2359304 | tf_op jit(solution)/shard_map/ppermute | solution.py:321
  137.8 61.5 %collective-permute-start.8 = (bf16[256,1536]{1,0:T(8,128)(2,1)S(1)}, bf16[256,1536]{1,0:T(8,128)(2,1)}, u32[]{:S(2)}, u32[]{:S(2)}) collective-permute-start(bf16[256,1536]{1,0:T(8,128)(2,1)S(1)} %collective-permute-done.3.refs_10_.refs_14_), channel_id=1, source_target_pairs={{0,64},{64,128},{128,192},{192,0},{1,65},{65,129},{129,193},{193,1... | collective-permute-start | bytes 2359304 | tf_op jit(solution)/shard_map/ppermute | solution.py:321
  139.8 59.5 %collective-permute-start.9 = (bf16[256,1536]{1,0:T(8,128)(2,1)S(1)}, bf16[256,1536]{1,0:T(8,128)(2,1)}, u32[]{:S(2)}, u32[]{:S(2)}) collective-permute-start(bf16[256,1536]{1,0:T(8,128)(2,1)S(1)} %collective-permute-done.3.refs_10_.refs_14_), channel_id=1, source_target_pairs={{0,128},{64,192},{128,0},{192,64},{1,129},{65,193},{129,1},{193,65... | collective-permute-start | bytes 2359304 | tf_op jit(solution)/shard_map/ppermute | solution.py:321
  161.7 35.5 %copy-start.6 = (bf16[256,1536]{1,0:T(8,128)(2,1)}, bf16[256,1536]{1,0:T(8,128)(2,1)S(1)}, u32[]{:S(2)}) copy-start(bf16[256,1536]{1,0:T(8,128)(2,1)S(1)} %collective-permute-done.4.refs_10_.refs_14_) | copy-start | bytes 2359300
  161.7 48.3 %collective-permute-start.5 = (bf16[256,1536]{1,0:T(8,128)(2,1)S(1)}, bf16[256,1536]{1,0:T(8,128)(2,1)S(1)}, u32[]{:S(2)}, u32[]{:S(2)}) collective-permute-start(bf16[256,1536]{1,0:T(8,128)(2,1)S(1)} %collective-permute-done.4.refs_10_.refs_14_), channel_id=1, source_target_pairs={{0,64},{64,128},{128,192},{192,0},{1,65},{65,129},{129,193},{193,1... | collective-permute-start | bytes 2359304 | tf_op jit(solution)/shard_map/ppermute | solution.py:321
  165.1 44.9 %collective-permute-start.6 = (bf16[256,1536]{1,0:T(8,128)(2,1)S(1)}, bf16[256,1536]{1,0:T(8,128)(2,1)}, u32[]{:S(2)}, u32[]{:S(2)}) collective-permute-start(bf16[256,1536]{1,0:T(8,128)(2,1)S(1)} %collective-permute-done.4.refs_10_.refs_14_), channel_id=1, source_target_pairs={{0,128},{64,192},{128,0},{192,64},{1,129},{65,193},{129,1},{193,65... | collective-permute-start | bytes 2359304 | tf_op jit(solution)/shard_map/ppermute | solution.py:321
  188.9 8.3 %copy-start.8 = (bf16[256,1536]{1,0:T(8,128)(2,1)}, bf16[256,1536]{1,0:T(8,128)(2,1)S(1)}, u32[]{:S(2)}) copy-start(bf16[256,1536]{1,0:T(8,128)(2,1)S(1)} %collective-permute-done.10.refs_13_.refs_17_) | copy-start | bytes 2359300
  188.9 21.1 %collective-permute-start.7 = (bf16[256,1536]{1,0:T(8,128)(2,1)S(1)}, bf16[256,1536]{1,0:T(8,128)(2,1)}, u32[]{:S(2)}, u32[]{:S(2)}) collective-permute-start(bf16[256,1536]{1,0:T(8,128)(2,1)S(1)} %collective-permute-done.4.refs_10_.refs_14_), channel_id=1, source_target_pairs={{0,192},{64,0},{128,64},{192,128},{1,193},{65,1},{129,65},{193,129... | collective-permute-start | bytes 2359304 | tf_op jit(solution)/shard_map/ppermute | solution.py:321
  194.6 2.6 %copy-start.4 = (s32[3]{0:T(128)}, s32[3]{0:T(128)S(1)}, u32[]{:S(2)}) copy-start(s32[3]{0:T(128)S(1)} %pad_add_fusion.where_ref.refs_0_) | copy-start | bytes 40
  197.2 0.8 copy-start.1
  198.0 0.7 copy-start.2
  198.7 0.6 copy-start.3
  209.9 0.9 copy-start.7
Sparse Core Ops, SparseCore 0:
  33.7 73.9 all-gather.2

commit v7 on v6

--- a/solution.py
+++ b/solution.py
@@ -23,7 +23,7 @@
 TILE = 256
 INFO = 2 * TOK
 
-TAKE_COST = (40 * 10**9, 0 * 10**9)
+TAKE_COST = (40 * 10**9, 55 * 10**9)
 f32 = jnp.float32
 bf16 = jnp.bfloat16
 
@@ -239,12 +239,13 @@
 
 def expert_kernel(pieces, *refs):
     where_ref, own_ref, rest_ref, own_last_ref, last_ref, gate_ref, sort_ref, sort8_ref = refs[:8]
-    near_refs, far_refs, (out_ref, rows_ref) = refs[8:10], refs[10 : 10 + 2 * pieces], refs[-2:]
+    near_refs, far_refs, (out_ref, rows_ref, sums_ref) = refs[8:10], refs[10:-3], refs[-3:]
+    e, n = pl.program_id(0), pl.program_id(1)
     blocks = PEERS * ZL
     count = blocks * MAIN
     half, width = D // 2, D // 2 // pieces
 
-    @pl.when(pl.program_id(0) == 0)
+    @pl.when(n == 0)
     def _():
         zh, x = where_ref[1], where_ref[2]
         moves = [(zh * half, 0, half)]
@@ -264,8 +265,15 @@
             near, near_ref[...].reshape(half, TILE), preferred_element_type=f32
         ) + jnp.dot(far, weights, preferred_element_type=f32)
 
-    before = product(near_refs[0], far_refs[:pieces])
-    up = product(near_refs[1], far_refs[pieces:])
+    for mine in range(HELD):
+
+        @pl.when(e == mine)
+        def _():
+            for part in range(2):
+                at = (mine * 2 + part) * pieces
+                sums_ref[part] = product(near_refs[part], far_refs[at : at + pieces])
+
+    before, up = sums_ref[0], sums_ref[1]
     gate = gate_ref[0].astype(f32)
     gate = jnp.concatenate([gate] * (TILE // TOK), axis=1)
     hidden = (before / (1.0 + jnp.exp(-before)) * up * gate).astype(bf16)
@@ -275,45 +283,48 @@
     out_ref[0, MAIN] = last.astype(bf16)
 
 
-def expert(e, where, own, rest, slots, near, far, other=None):
+def experts(where, own, rest, slots, near, far):
     blocks = PEERS * ZL
     tiles = FF // TILE
     rows = blocks * (MAIN + HELD)
     gates, sort, sort8 = slots
-    others = [] if other is None else [other]
-    far = [f.reshape(-1, f.shape[-1]) for f in far]
-    deep = far[0].shape[0]
+    pieces = [p for mine in far for p in mine * 2]
+    width = D // 2 // len(far[0])
+    steps = [lambda e, n: n * (1 - e) + (tiles - 1) * e, lambda e, n: n * e]
+    far_specs = [
+        pl.BlockSpec((width, TILE), lambda e, n, w, step=step, at=at: (0, step(e, n) + at))
+        for step in steps
+        for at in (0, tiles)
+        for _ in far[0]
+    ]
     return pl.pallas_call(
-        functools.partial(expert_kernel, len(far)),
+        functools.partial(expert_kernel, len(far[0])),
         grid_spec=pltpu.PrefetchScalarGridSpec(
             num_scalar_prefetch=1,
-            grid=(tiles,),
+            grid=(HELD, tiles),
             in_specs=[
-                pl.BlockSpec((PEERS, 1, MAIN, D), lambda n, w: (0, e, 0, 0)),
-                pl.BlockSpec((PEERS, ZL - 1, MAIN, D), lambda n, w: (0, e, 0, 0)),
-                pl.BlockSpec((PEERS, 1, MAIN, D), lambda n, w: (0, HELD, 0, 0)),
-                pl.BlockSpec((PEERS, 1, MAIN, D), lambda n, w: (0, LEFT, 0, 0)),
-                pl.BlockSpec((1,) + gates.shape[1:], lambda n, w: (e, 0, 0)),
-                pl.BlockSpec(sort.shape, lambda n, w: (0, 0)),
-                pl.BlockSpec((1,) + sort8.shape[1:], lambda n, w: (e, 0, 0)),
-                pl.BlockSpec((X, 1, D // 8, TILE), lambda n, w: (0, e, 0, n)),
-                pl.BlockSpec((X, 1, D // 8, TILE), lambda n, w: (0, e, 0, n + tiles)),
+                pl.BlockSpec((PEERS, 1, MAIN, D), lambda e, n, w: (0, e, 0, 0)),
+                pl.BlockSpec((PEERS, ZL - 1, MAIN, D), lambda e, n, w: (0, e, 0, 0)),
+                pl.BlockSpec((PEERS, 1, MAIN, D), lambda e, n, w: (0, HELD, 0, 0)),
+                pl.BlockSpec((PEERS, 1, MAIN, D), lambda e, n, w: (0, LEFT, 0, 0)),
+                pl.BlockSpec((1,) + gates.shape[1:], lambda e, n, w: (e, 0, 0)),
+                pl.BlockSpec(sort.shape, lambda e, n, w: (0, 0)),
+                pl.BlockSpec((1,) + sort8.shape[1:], lambda e, n, w: (e, 0, 0)),
+                pl.BlockSpec((X, 1, D // 8, TILE), lambda e, n, w: (0, e, 0, n)),
+                pl.BlockSpec((X, 1, D // 8, TILE), lambda e, n, w: (0, e, 0, n + tiles)),
             ]
-            + [pl.BlockSpec((deep, TILE), lambda n, w: (0, n))] * len(far)
-            + [pl.BlockSpec((deep, TILE), lambda n, w: (0, n + tiles))] * len(far)
-            + [pl.BlockSpec(memory_space=pl.ANY)] * len(others),
-            out_specs=pl.BlockSpec((1, CAP, blocks, TILE), lambda n, w: (e, 0, 0, n)),
-            scratch_shapes=[pltpu.VMEM((rows, D), bf16)],
+            + far_specs,
+            out_specs=pl.BlockSpec((1, CAP, blocks, TILE), lambda e, n, w: (e, 0, 0, n)),
+            scratch_shapes=[pltpu.VMEM((rows, D), bf16), pltpu.VMEM((2, rows, TILE), f32)],
         ),
         out_shape=jax.ShapeDtypeStruct((HELD, CAP, blocks, FF), bf16),
-        input_output_aliases={10 + 2 * len(far): 0} if others else {},
         compiler_params=pltpu.CompilerParams(vmem_limit_bytes=60 * 1024 * 1024),
         cost_estimate=pl.CostEstimate(
-            flops=3*10**9 if e == 0 else 2 * rows * D * 2 * FF,
-            bytes_accessed=10_000_000,
+            flops=HELD * 2 * rows * D * 2 * FF,
+            bytes_accessed=20_000_000,
             transcendentals=10**6,
         ),
-    )(where, own, rest, own, rest, gates, sort, sort8, near, near, *far, *far, *others)
+    )(where, own, rest, own, rest, gates, sort, sort8, near, near, *pieces)
 
 
 def over(axis, count, block):
@@ -381,8 +392,7 @@
     second = lax.ppermute(take(expert_weights, 1, first), "zh", swap)
     far = [over("x", X, first), over("x", X, second)]
     slots = plan(where, rest)
-    hidden = expert(0, where, own, rest, slots, near, far[0])
-    hidden = expert(1, where, own, rest, slots, near, far[1], hidden)
+    hidden = experts(where, own, rest, slots, near, far)
     return jnp.transpose(hidden, (0, 2, 1, 3))[None]
 
 

time: 229 us -> 231 us (level)
  the two profiles are of different devices: /device:TPU:64 before, /device:TPU:250 now
where the time goes in v7:
time: 231 us; the launch traced here: 230 us
  waiting for transfers between devices  103 us (45%)
  starting transfers between devices  73.3 us (32%)
  Pallas kernels  30.3 us (13%)
  between operations  13.6 us (6%)
  local copies, waits for them, and re-layouts  7.72 us (3%)
  other arithmetic  2.53 us (1%)
    ppermute x9, waiting for transfers between devices, over(): lax.ppermute(block, axis, [(i, (i + b) % count) for i in range(count)])  49 us
    ppermute x9, starting transfers between devices, over(): lax.ppermute(block, axis, [(i, (i + b) % count) for i in range(count)])  29 us
    ppermute x1, starting transfers between devices, shards(): first = lax.ppermute(taken, 'zh', swap)  26.1 us
    ppermute x1, waiting for transfers between devices, shards(): first = lax.ppermute(taken, 'zh', swap)  21.1 us
    ppermute x1, waiting for transfers between devices, shards(): second = lax.ppermute(take(expert_weights, 1, first), 'zh', swap)  18.7 us
    pallas_call x1, Pallas kernels, experts(): pl.pallas_call(functools.partial(expert_kernel, len(far[0])), grid_spec=p...  18.2 us
    all_to_all x2, starting transfers between devices, over_peers(): lax.all_to_all(message, ('y', 'c'), split_axis=0, concat_axis=0, tiled=True)  13.8 us
    all_to_all x2, waiting for transfers between devices, over_peers(): lax.all_to_all(message, ('y', 'c'), split_axis=0, concat_axis=0, tiled=True)  13.2 us
  transfers between devices with their start and end apart: 14, of which 6 were waited for; matrix products, arithmetic and copies ran while one was open for 2% of the time, Pallas kernels for 5%

profile of v7, /device:TPU:250, one launch (start us, length us, event | category | flops | bytes accessed | tf_op | source)
XLA Modules:
  0.0 230.2 jit_solution(9218829510704135770)
XLA Ops:
  6.5 0.7 convert_bitcast_fusion
  7.2 0.7 fusion.2
  7.9 1.1 pad_maximum_fusion.block.refs_0_
  9.0 1.9 collective-permute-start
  10.9 3.0 %collective-permute-start.1 = (bf16[136,2048]{1,0:T(8,128)(2,1)S(1)}, bf16[136,2048]{1,0:T(8,128)(2,1)S(1)}, u32[]{:S(2)}, u32[]{:S(2)}) collective-permute-start(bf16[136,2048]{1,0:T(8,128)(2,1)S(1)} %pad_maximum_fusion.block.refs_0_), channel_id=1, source_target_pairs={{0,32},{16,48},{32,0},{48,16},{1,33},{17,49},{33,1},{49,17},{2,34}... | collective-permute-start | bytes 1671176 | tf_op jit(solution)/shard_map/ppermute | solution.py:332
  13.9 2.8 %collective-permute-start.2 = (bf16[136,2048]{1,0:T(8,128)(2,1)S(1)}, bf16[136,2048]{1,0:T(8,128)(2,1)S(1)}, u32[]{:S(2)}, u32[]{:S(2)}) collective-permute-start(bf16[136,2048]{1,0:T(8,128)(2,1)S(1)} %pad_maximum_fusion.block.refs_0_), channel_id=1, source_target_pairs={{0,48},{16,0},{32,16},{48,32},{1,49},{17,1},{33,17},{49,33},{2,50}... | collective-permute-start | bytes 1671176 | tf_op jit(solution)/shard_map/ppermute | solution.py:332
  16.8 2.6 %shard_map.46 = bf16[16,3,8,2048]{3,2,1,0:T(8,128)(2,1)} custom-call(s32[1]{0:T(128)} %bitcast.zl_ref, bf16[136,2048]{1,0:T(8,128)(2,1)S(1)} %pad_maximum_fusion.block.refs_0_), custom_call_target="tpu_custom_call" | custom-call | flops 201326592 | bytes 1572864 | tf_op jit(solution)/shard_map/pallas_call | solution.py:137
  19.3 6.9 %all-to-all-start = ((bf16[16,3,8,2048]{3,2,1,0:T(8,128)(2,1)}), bf16[16,3,8,2048]{3,2,1,0:T(8,128)(2,1)}, u32[]{:S(2)}, u32[]{:S(2)}) async-start(bf16[16,3,8,2048]{3,2,1,0:T(8,128)(2,1)} %shard_map.46), calls=%async_computation | async-start | bytes 3145728 | tf_op jit(solution)/shard_map/all_to_all | solution.py:338
  26.2 0.0 all-gather.3.cloned.1.call-start
  26.3 0.7 all-gather.3.cloned.1.call-update
  27.0 0.0 collective-permute-done.refs_1_
  27.0 0.6 slice.25.refs_1_
  27.6 32.6 %collective-permute-done.1.refs_2_ = bf16[136,2048]{1,0:T(8,128)(2,1)S(1)} collective-permute-done((bf16[136,2048]{1,0:T(8,128)(2,1)S(1)}, bf16[136,2048]{1,0:T(8,128)(2,1)S(1)}, u32[]{:S(2)}, u32[]{:S(2)}) %collective-permute-start.1) | collective-permute-done | bytes 557088 | tf_op jit(solution)/shard_map/ppermute | solution.py:332
  60.2 0.6 slice.26.refs_2_
  60.7 0.0 collective-permute-done.2.refs_3_
  60.7 0.6 slice.27.refs_3_
  61.3 2.1 shard_map.47
  63.4 26.1 %collective-permute-start.3 = (bf16[256,1536]{1,0:T(8,128)(2,1)}, bf16[256,1536]{1,0:T(8,128)(2,1)S(1)}, u32[]{:S(2)}, u32[]{:S(2)}) collective-permute-start(bf16[256,1536]{1,0:T(8,128)(2,1)} %shard_map.47), channel_id=1, source_target_pairs={{0,256},{256,0},{1,257},{257,1},{2,258},{258,2},{3,259},{259,3},{4... | collective-permute-start | bytes 2359304 | tf_op jit(solution)/shard_map/ppermute | solution.py:390
  89.5 0.6 slice.28.refs_5_
  90.2 0.0 all-to-all-done.refs_1_.refs_3_
  90.2 0.7 slice_bitcast_fusion.refs_4_
  90.9 2.9 %shard_map.48 = bf16[16,7,8,2048]{3,2,1,0:T(8,128)(2,1)S(1)} custom-call(s32[1]{0:T(128)} %bitcast.zl_ref, bf16[136,2048]{1,0:T(8,128)(2,1)S(1)} %pad_maximum_fusion.block.refs_0_, bf16[136,2048]{1,0:T(8,128)(2,1)S(1)} %collective-permute-done.refs_1_, bf16[136,2048]{1,0:T(8,128)(2,1)S(1)} %collective-permute-done.1.refs_2_, ...), custom_call_target="tpu_custom_call" | custom-call | flops 805306368 | bytes 3670016 | tf_op jit(solution)/shard_map/pallas_call | solution.py:137
  93.7 0.0 copy-start
  93.7 1.9 copy-done
  95.7 6.9 %all-to-all-start.1 = ((bf16[16,7,8,2048]{3,2,1,0:T(8,128)(2,1)}), bf16[16,7,8,2048]{3,2,1,0:T(8,128)(2,1)}, u32[]{:S(2)}, u32[]{:S(2)}) async-start(bf16[16,7,8,2048]{3,2,1,0:T(8,128)(2,1)} %copy-done), calls=%async_computation.1 | async-start | bytes 7340032 | tf_op jit(solution)/shard_map/all_to_all | solution.py:338
  102.5 21.1 %collective-permute-done.3.refs_10_.refs_14_ = bf16[256,1536]{1,0:T(8,128)(2,1)S(1)} collective-permute-done((bf16[256,1536]{1,0:T(8,128)(2,1)}, bf16[256,1536]{1,0:T(8,128)(2,1)S(1)}, u32[]{:S(2)}, u32[]{:S(2)}) %collective-permute-start.3) | collective-permute-done | bytes 786464 | tf_op jit(solution)/shard_map/ppermute | solution.py:390
  123.6 0.0 copy-start.5
  123.6 0.6 slice.29.refs_1_
  124.2 2.1 shard_map.50
  126.3 4.3 %collective-permute-start.7 = (bf16[256,1536]{1,0:T(8,128)(2,1)}, bf16[256,1536]{1,0:T(8,128)(2,1)S(1)}, u32[]{:S(2)}, u32[]{:S(2)}) collective-permute-start(bf16[256,1536]{1,0:T(8,128)(2,1)} %shard_map.50), channel_id=1, source_target_pairs={{0,256},{256,0},{1,257},{257,1},{2,258},{258,2},{3,259},{259,3},{4... | collective-permute-start | bytes 2359304 | tf_op jit(solution)/shard_map/ppermute | solution.py:392
  130.6 3.6 %collective-permute-start.4 = (bf16[256,1536]{1,0:T(8,128)(2,1)S(1)}, bf16[256,1536]{1,0:T(8,128)(2,1)S(1)}, u32[]{:S(2)}, u32[]{:S(2)}) collective-permute-start(bf16[256,1536]{1,0:T(8,128)(2,1)S(1)} %collective-permute-done.3.refs_10_.refs_14_), channel_id=1, source_target_pairs={{0,64},{64,128},{128,192},{192,0},{1,65},{65,129},{129,193},{193,1... | collective-permute-start | bytes 2359304 | tf_op jit(solution)/shard_map/ppermute | solution.py:332
  134.2 2.9 %collective-permute-start.5 = (bf16[256,1536]{1,0:T(8,128)(2,1)S(1)}, bf16[256,1536]{1,0:T(8,128)(2,1)}, u32[]{:S(2)}, u32[]{:S(2)}) collective-permute-start(bf16[256,1536]{1,0:T(8,128)(2,1)S(1)} %collective-permute-done.3.refs_10_.refs_14_), channel_id=1, source_target_pairs={{0,128},{64,192},{128,0},{192,64},{1,129},{65,193},{129,1},{193,65... | collective-permute-start | bytes 2359304 | tf_op jit(solution)/shard_map/ppermute | solution.py:332
  137.1 0.0 copy-done.5
  137.1 4.1 %collective-permute-start.6 = (bf16[256,1536]{1,0:T(8,128)(2,1)S(1)}, bf16[256,1536]{1,0:T(8,128)(2,1)}, u32[]{:S(2)}, u32[]{:S(2)}) collective-permute-start(bf16[256,1536]{1,0:T(8,128)(2,1)S(1)} %collective-permute-done.3.refs_10_.refs_14_), channel_id=1, source_target_pairs={{0,192},{64,0},{128,64},{192,128},{1,193},{65,1},{129,65},{193,129... | collective-permute-start | bytes 2359304 | tf_op jit(solution)/shard_map/ppermute | solution.py:332
  141.2 18.7 %collective-permute-done.7.refs_18_.refs_22_ = bf16[256,1536]{1,0:T(8,128)(2,1)S(1)} collective-permute-done((bf16[256,1536]{1,0:T(8,128)(2,1)}, bf16[256,1536]{1,0:T(8,128)(2,1)S(1)}, u32[]{:S(2)}, u32[]{:S(2)}) %collective-permute-start.7) | collective-permute-done | bytes 786464 | tf_op jit(solution)/shard_map/ppermute | solution.py:392
  159.9 0.0 copy-start.6
  159.9 2.1 collective-permute-start.10
  162.0 4.1 %collective-permute-start.8 = (bf16[256,1536]{1,0:T(8,128)(2,1)S(1)}, bf16[256,1536]{1,0:T(8,128)(2,1)}, u32[]{:S(2)}, u32[]{:S(2)}) collective-permute-start(bf16[256,1536]{1,0:T(8,128)(2,1)S(1)} %collective-permute-done.7.refs_18_.refs_22_), channel_id=1, source_target_pairs={{0,64},{64,128},{128,192},{192,0},{1,65},{65,129},{129,193},{193,1... | collective-permute-start | bytes 2359304 | tf_op jit(solution)/shard_map/ppermute | solution.py:332
  166.1 0.0 collective-permute-done.4.refs_11_.refs_15_
  166.1 0.0 copy-start.7
  166.1 4.6 %collective-permute-start.9 = (bf16[256,1536]{1,0:T(8,128)(2,1)S(1)}, bf16[256,1536]{1,0:T(8,128)(2,1)}, u32[]{:S(2)}, u32[]{:S(2)}) collective-permute-start(bf16[256,1536]{1,0:T(8,128)(2,1)S(1)} %collective-permute-done.7.refs_18_.refs_22_), channel_id=1, source_target_pairs={{0,128},{64,192},{128,0},{192,64},{1,129},{65,193},{129,1},{193,65... | collective-permute-start | bytes 2359304 | tf_op jit(solution)/shard_map/ppermute | solution.py:332
  170.7 0.1 pad_add_fusion.where_ref.refs_0_
  170.8 0.0 copy-start.4
  170.8 13.2 %all-to-all-done.1.last_ref.refs_2_.refs_4_ = bf16[16,7,8,2048]{3,2,1,0:T(8,128)(2,1)} async-done(((bf16[16,7,8,2048]{3,2,1,0:T(8,128)(2,1)}), bf16[16,7,8,2048]{3,2,1,0:T(8,128)(2,1)}, u32[]{:S(2)}, u32[]{:S(2)}) %all-to-all-start.1) | async-done | bytes 3670048 | tf_op jit(solution)/shard_map/all_to_all | solution.py:338
  184.0 2.5 %shard_map.49 = (bf16[2,640,128]{2,1,0:T(8,128)(2,1)S(1)}, bf16[512,512]{1,0:T(8,128)(2,1)S(1)}, bf16[2,64,128]{2,1,0:T(8,128)(2,1)S(1)}) custom-call(s32[3]{0:T(128)S(1)} %pad_add_fusion.where_ref.refs_0_, bf16[16,7,8,2048]{3,2,1,0:T(8,128)(2,1)} %all-to-all-done.1.last_ref.refs_2_.refs_4_), custom_call_target="tpu_custom_call" | custom-call | flops 100000000 | bytes 1000000 | tf_op jit(solution)/shard_map/pallas_call | solution.py:210
  186.5 0.0 copy-done.6
  186.6 0.0 copy-done.7
  186.6 0.0 copy-done.4
  186.6 0.0 copy-start.1
  186.6 0.8 copy-done.1
  187.4 0.0 copy-start.2
  187.4 0.7 copy-done.2
  188.1 0.0 copy-start.3
  188.1 0.6 copy-done.3
  188.8 0.0 collective-permute-done.5.refs_12_.refs_16_
  188.8 0.0 collective-permute-done.6.refs_13_.refs_17_
  188.8 3.0 %collective-permute-done.10.refs_21_.refs_25_ = bf16[256,1536]{1,0:T(8,128)(2,1)} collective-permute-done((bf16[256,1536]{1,0:T(8,128)(2,1)S(1)}, bf16[256,1536]{1,0:T(8,128)(2,1)}, u32[]{:S(2)}, u32[]{:S(2)}) %collective-permute-start.10) | collective-permute-done | bytes 786464 | tf_op jit(solution)/shard_map/ppermute | solution.py:332
  191.8 0.0 collective-permute-done.8.refs_19_.refs_23_
  191.8 13.3 %collective-permute-done.9.refs_20_.refs_24_ = bf16[256,1536]{1,0:T(8,128)(2,1)} collective-permute-done((bf16[256,1536]{1,0:T(8,128)(2,1)S(1)}, bf16[256,1536]{1,0:T(8,128)(2,1)}, u32[]{:S(2)}, u32[]{:S(2)}) %collective-permute-start.9) | collective-permute-done | bytes 786464 | tf_op jit(solution)/shard_map/ppermute | solution.py:332
  205.2 0.0 all-gather.3.cloned.1.call-done
  205.2 18.2 %shard_map.51 = bf16[2,9,64,768]{3,2,1,0:T(8,128)(2,1)} custom-call(s32[3]{0:T(128)} %copy-done.4, bf16[16,3,8,2048]{3,2,1,0:T(8,128)(2,1)} %all-to-all-done.refs_1_.refs_3_, bf16[16,7,8,2048]{3,2,1,0:T(8,128)(2,1)} %all-to-all-done.1.last_ref.refs_2_.refs_4_, bf16[16,3,8,2048]{3,2,1,0:T(8,128)(2,1)} %all-to-all-done.refs_1_.refs_3_, ...), custom_call_target="tpu_custom_call" | custom-call | flops 8053063680 | bytes 20000000 | tf_op jit(solution)/shard_map/pallas_call | solution.py:300
Async XLA Ops:
  9.0 18.0 %collective-permute-start = (bf16[136,2048]{1,0:T(8,128)(2,1)S(1)}, bf16[136,2048]{1,0:T(8,128)(2,1)S(1)}, u32[]{:S(2)}, u32[]{:S(2)}) collective-permute-start(bf16[136,2048]{1,0:T(8,128)(2,1)S(1)} %pad_maximum_fusion.block.refs_0_), channel_id=1, source_target_pairs={{0,16},{16,32},{32,48},{48,0},{1,17},{17,33},{33,49},{49,1},{2,18}... | collective-permute-start | bytes 1671176 | tf_op jit(solution)/shard_map/ppermute | solution.py:332
  10.9 49.2 %collective-permute-start.1 = (bf16[136,2048]{1,0:T(8,128)(2,1)S(1)}, bf16[136,2048]{1,0:T(8,128)(2,1)S(1)}, u32[]{:S(2)}, u32[]{:S(2)}) collective-permute-start(bf16[136,2048]{1,0:T(8,128)(2,1)S(1)} %pad_maximum_fusion.block.refs_0_), channel_id=1, source_target_pairs={{0,32},{16,48},{32,0},{48,16},{1,33},{17,49},{33,1},{49,17},{2,34}... | collective-permute-start | bytes 1671176 | tf_op jit(solution)/shard_map/ppermute | solution.py:332
  13.9 46.8 %collective-permute-start.2 = (bf16[136,2048]{1,0:T(8,128)(2,1)S(1)}, bf16[136,2048]{1,0:T(8,128)(2,1)S(1)}, u32[]{:S(2)}, u32[]{:S(2)}) collective-permute-start(bf16[136,2048]{1,0:T(8,128)(2,1)S(1)} %pad_maximum_fusion.block.refs_0_), channel_id=1, source_target_pairs={{0,48},{16,0},{32,16},{48,32},{1,49},{17,1},{33,17},{49,33},{2,50}... | collective-permute-start | bytes 1671176 | tf_op jit(solution)/shard_map/ppermute | solution.py:332
  19.3 70.8 %all-to-all-start = ((bf16[16,3,8,2048]{3,2,1,0:T(8,128)(2,1)}), bf16[16,3,8,2048]{3,2,1,0:T(8,128)(2,1)}, u32[]{:S(2)}, u32[]{:S(2)}) async-start(bf16[16,3,8,2048]{3,2,1,0:T(8,128)(2,1)} %shard_map.46), calls=%async_computation | async-start | bytes 3145728 | tf_op jit(solution)/shard_map/all_to_all | solution.py:338
  26.2 178.9 %all-gather.3.cloned.1.call-start = ((), (), s32[]{:S(2)}) async-start(), calls=%async_computation.2 | async-start | bytes 7864320 | tf_op jit(solution)/shard_map/all_gather | solution.py:386
  63.4 60.2 %collective-permute-start.3 = (bf16[256,1536]{1,0:T(8,128)(2,1)}, bf16[256,1536]{1,0:T(8,128)(2,1)S(1)}, u32[]{:S(2)}, u32[]{:S(2)}) collective-permute-start(bf16[256,1536]{1,0:T(8,128)(2,1)} %shard_map.47), channel_id=1, source_target_pairs={{0,256},{256,0},{1,257},{257,1},{2,258},{258,2},{3,259},{259,3},{4... | collective-permute-start | bytes 2359304 | tf_op jit(solution)/shard_map/ppermute | solution.py:390
  93.7 1.9 copy-start
  95.7 88.3 %all-to-all-start.1 = ((bf16[16,7,8,2048]{3,2,1,0:T(8,128)(2,1)}), bf16[16,7,8,2048]{3,2,1,0:T(8,128)(2,1)}, u32[]{:S(2)}, u32[]{:S(2)}) async-start(bf16[16,7,8,2048]{3,2,1,0:T(8,128)(2,1)} %copy-done), calls=%async_computation.1 | async-start | bytes 7340032 | tf_op jit(solution)/shard_map/all_to_all | solution.py:338
  123.6 13.4 %copy-start.5 = (bf16[256,1536]{1,0:T(8,128)(2,1)}, bf16[256,1536]{1,0:T(8,128)(2,1)S(1)}, u32[]{:S(2)}) copy-start(bf16[256,1536]{1,0:T(8,128)(2,1)S(1)} %collective-permute-done.3.refs_10_.refs_14_) | copy-start | bytes 2359300
  126.3 33.6 %collective-permute-start.7 = (bf16[256,1536]{1,0:T(8,128)(2,1)}, bf16[256,1536]{1,0:T(8,128)(2,1)S(1)}, u32[]{:S(2)}, u32[]{:S(2)}) collective-permute-start(bf16[256,1536]{1,0:T(8,128)(2,1)} %shard_map.50), channel_id=1, source_target_pairs={{0,256},{256,0},{1,257},{257,1},{2,258},{258,2},{3,259},{259,3},{4... | collective-permute-start | bytes 2359304 | tf_op jit(solution)/shard_map/ppermute | solution.py:392
  130.6 35.5 %collective-permute-start.4 = (bf16[256,1536]{1,0:T(8,128)(2,1)S(1)}, bf16[256,1536]{1,0:T(8,128)(2,1)S(1)}, u32[]{:S(2)}, u32[]{:S(2)}) collective-permute-start(bf16[256,1536]{1,0:T(8,128)(2,1)S(1)} %collective-permute-done.3.refs_10_.refs_14_), channel_id=1, source_target_pairs={{0,64},{64,128},{128,192},{192,0},{1,65},{65,129},{129,193},{193,1... | collective-permute-start | bytes 2359304 | tf_op jit(solution)/shard_map/ppermute | solution.py:332
  134.2 54.6 %collective-permute-start.5 = (bf16[256,1536]{1,0:T(8,128)(2,1)S(1)}, bf16[256,1536]{1,0:T(8,128)(2,1)}, u32[]{:S(2)}, u32[]{:S(2)}) collective-permute-start(bf16[256,1536]{1,0:T(8,128)(2,1)S(1)} %collective-permute-done.3.refs_10_.refs_14_), channel_id=1, source_target_pairs={{0,128},{64,192},{128,0},{192,64},{1,129},{65,193},{129,1},{193,65... | collective-permute-start | bytes 2359304 | tf_op jit(solution)/shard_map/ppermute | solution.py:332
  137.1 51.7 %collective-permute-start.6 = (bf16[256,1536]{1,0:T(8,128)(2,1)S(1)}, bf16[256,1536]{1,0:T(8,128)(2,1)}, u32[]{:S(2)}, u32[]{:S(2)}) collective-permute-start(bf16[256,1536]{1,0:T(8,128)(2,1)S(1)} %collective-permute-done.3.refs_10_.refs_14_), channel_id=1, source_target_pairs={{0,192},{64,0},{128,64},{192,128},{1,193},{65,1},{129,65},{193,129... | collective-permute-start | bytes 2359304 | tf_op jit(solution)/shard_map/ppermute | solution.py:332
  159.9 26.6 %copy-start.6 = (bf16[256,1536]{1,0:T(8,128)(2,1)}, bf16[256,1536]{1,0:T(8,128)(2,1)S(1)}, u32[]{:S(2)}) copy-start(bf16[256,1536]{1,0:T(8,128)(2,1)S(1)} %collective-permute-done.7.refs_18_.refs_22_) | copy-start | bytes 2359300
  159.9 31.9 %collective-permute-start.10 = (bf16[256,1536]{1,0:T(8,128)(2,1)S(1)}, bf16[256,1536]{1,0:T(8,128)(2,1)}, u32[]{:S(2)}, u32[]{:S(2)}) collective-permute-start(bf16[256,1536]{1,0:T(8,128)(2,1)S(1)} %collective-permute-done.7.refs_18_.refs_22_), channel_id=1, source_target_pairs={{0,192},{64,0},{128,64},{192,128},{1,193},{65,1},{129,65},{193,129... | collective-permute-start | bytes 2359304 | tf_op jit(solution)/shard_map/ppermute | solution.py:332
  162.0 29.8 %collective-permute-start.8 = (bf16[256,1536]{1,0:T(8,128)(2,1)S(1)}, bf16[256,1536]{1,0:T(8,128)(2,1)}, u32[]{:S(2)}, u32[]{:S(2)}) collective-permute-start(bf16[256,1536]{1,0:T(8,128)(2,1)S(1)} %collective-permute-done.7.refs_18_.refs_22_), channel_id=1, source_target_pairs={{0,64},{64,128},{128,192},{192,0},{1,65},{65,129},{129,193},{193,1... | collective-permute-start | bytes 2359304 | tf_op jit(solution)/shard_map/ppermute | solution.py:332
  166.1 20.4 %copy-start.7 = (bf16[256,1536]{1,0:T(8,128)(2,1)}, bf16[256,1536]{1,0:T(8,128)(2,1)S(1)}, u32[]{:S(2)}) copy-start(bf16[256,1536]{1,0:T(8,128)(2,1)S(1)} %collective-permute-done.4.refs_11_.refs_15_) | copy-start | bytes 2359300
  166.1 39.0 %collective-permute-start.9 = (bf16[256,1536]{1,0:T(8,128)(2,1)S(1)}, bf16[256,1536]{1,0:T(8,128)(2,1)}, u32[]{:S(2)}, u32[]{:S(2)}) collective-permute-start(bf16[256,1536]{1,0:T(8,128)(2,1)S(1)} %collective-permute-done.7.refs_18_.refs_22_), channel_id=1, source_target_pairs={{0,128},{64,192},{128,0},{192,64},{1,129},{65,193},{129,1},{193,65... | collective-permute-start | bytes 2359304 | tf_op jit(solution)/shard_map/ppermute | solution.py:332
  170.8 15.8 %copy-start.4 = (s32[3]{0:T(128)}, s32[3]{0:T(128)S(1)}, u32[]{:S(2)}) copy-start(s32[3]{0:T(128)S(1)} %pad_add_fusion.where_ref.refs_0_) | copy-start | bytes 40
  186.6 0.8 copy-start.1
  187.4 0.7 copy-start.2
  188.1 0.6 copy-start.3
Sparse Core Ops, SparseCore 0:
  29.2 76.0 all-gather.2

commit v8 on v7

--- a/solution.py
+++ b/solution.py
@@ -23,7 +23,7 @@
 TILE = 256
 INFO = 2 * TOK
 
-TAKE_COST = (40 * 10**9, 55 * 10**9)
+TAKE_COST = (40 * 10**9, 0 * 10**9)
 f32 = jnp.float32
 bf16 = jnp.bfloat16
 

time: 231 us -> 235 us (1.017)
  the two profiles are of different devices: /device:TPU:250 before, /device:TPU:66 now
where the time goes in v8:
time: 235 us; the launch traced here: 234 us
  waiting for transfers between devices  118 us (50%)
  starting transfers between devices  62.1 us (26%)
  Pallas kernels  30.3 us (13%)
  between operations  13.6 us (6%)
  local copies, waits for them, and re-layouts  7.63 us (3%)
  other arithmetic  2.53 us (1%)
    ppermute x9, waiting for transfers between devices, over(): lax.ppermute(block, axis, [(i, (i + b) % count) for i in range(count)])  62.4 us
    ppermute x1, waiting for transfers between devices, shards(): first = lax.ppermute(taken, 'zh', swap)  35 us
    ppermute x9, starting transfers between devices, over(): lax.ppermute(block, axis, [(i, (i + b) % count) for i in range(count)])  33.5 us
    pallas_call x1, Pallas kernels, experts(): pl.pallas_call(functools.partial(expert_kernel, len(far[0])), grid_spec=p...  18.2 us
    ppermute x1, waiting for transfers between devices, shards(): second = lax.ppermute(take(expert_weights, 1, first), 'zh', swap)  18 us
    all_to_all x2, starting transfers between devices, over_peers(): lax.all_to_all(message, ('y', 'c'), split_axis=0, concat_axis=0, tiled=True)  12.8 us
    ppermute x1, starting transfers between devices, shards(): first = lax.ppermute(taken, 'zh', swap)  8.47 us
    ppermute x1, starting transfers between devices, shards(): second = lax.ppermute(take(expert_weights, 1, first), 'zh', swap)  7.24 us
  transfers between devices with their start and end apart: 14, of which 8 were waited for; matrix products, arithmetic and copies ran while one was open for 2% of the time, Pallas kernels for 5%

profile of v8, /device:TPU:66, one launch (start us, length us, event | category | flops | bytes accessed | tf_op | source)
XLA Modules:
  0.0 234.2 jit_solution(13329274608248221973)
XLA Ops:
  6.5 0.7 convert_bitcast_fusion
  7.2 0.7 fusion.2
  7.9 1.1 pad_maximum_fusion.block.refs_0_
  9.0 4.3 %collective-permute-start = (bf16[136,2048]{1,0:T(8,128)(2,1)S(1)}, bf16[136,2048]{1,0:T(8,128)(2,1)S(1)}, u32[]{:S(2)}, u32[]{:S(2)}) collective-permute-start(bf16[136,2048]{1,0:T(8,128)(2,1)S(1)} %pad_maximum_fusion.block.refs_0_), channel_id=1, source_target_pairs={{0,16},{16,32},{32,48},{48,0},{1,17},{17,33},{33,49},{49,1},{2,18}... | collective-permute-start | bytes 1671176 | tf_op jit(solution)/shard_map/ppermute | solution.py:332
  13.3 3.7 %collective-permute-start.1 = (bf16[136,2048]{1,0:T(8,128)(2,1)S(1)}, bf16[136,2048]{1,0:T(8,128)(2,1)S(1)}, u32[]{:S(2)}, u32[]{:S(2)}) collective-permute-start(bf16[136,2048]{1,0:T(8,128)(2,1)S(1)} %pad_maximum_fusion.block.refs_0_), channel_id=1, source_target_pairs={{0,32},{16,48},{32,0},{48,16},{1,33},{17,49},{33,1},{49,17},{2,34}... | collective-permute-start | bytes 1671176 | tf_op jit(solution)/shard_map/ppermute | solution.py:332
  17.0 3.9 %collective-permute-start.2 = (bf16[136,2048]{1,0:T(8,128)(2,1)S(1)}, bf16[136,2048]{1,0:T(8,128)(2,1)S(1)}, u32[]{:S(2)}, u32[]{:S(2)}) collective-permute-start(bf16[136,2048]{1,0:T(8,128)(2,1)S(1)} %pad_maximum_fusion.block.refs_0_), channel_id=1, source_target_pairs={{0,48},{16,0},{32,16},{48,32},{1,49},{17,1},{33,17},{49,33},{2,50}... | collective-permute-start | bytes 1671176 | tf_op jit(solution)/shard_map/ppermute | solution.py:332
  21.0 2.6 %shard_map.46 = bf16[16,3,8,2048]{3,2,1,0:T(8,128)(2,1)} custom-call(s32[1]{0:T(128)} %bitcast.zl_ref, bf16[136,2048]{1,0:T(8,128)(2,1)S(1)} %pad_maximum_fusion.block.refs_0_), custom_call_target="tpu_custom_call" | custom-call | flops 201326592 | bytes 1572864 | tf_op jit(solution)/shard_map/pallas_call | solution.py:137
  23.5 7.2 %all-to-all-start = ((bf16[16,3,8,2048]{3,2,1,0:T(8,128)(2,1)}), bf16[16,3,8,2048]{3,2,1,0:T(8,128)(2,1)}, u32[]{:S(2)}, u32[]{:S(2)}) async-start(bf16[16,3,8,2048]{3,2,1,0:T(8,128)(2,1)} %shard_map.46), calls=%async_computation | async-start | bytes 3145728 | tf_op jit(solution)/shard_map/all_to_all | solution.py:338
  30.8 0.0 all-gather.3.cloned.1.call-start
  30.8 0.7 all-gather.3.cloned.1.call-update
  31.5 18.7 %collective-permute-done.refs_1_ = bf16[136,2048]{1,0:T(8,128)(2,1)S(1)} collective-permute-done((bf16[136,2048]{1,0:T(8,128)(2,1)S(1)}, bf16[136,2048]{1,0:T(8,128)(2,1)S(1)}, u32[]{:S(2)}, u32[]{:S(2)}) %collective-permute-start) | collective-permute-done | bytes 557088 | tf_op jit(solution)/shard_map/ppermute | solution.py:332
  50.2 0.6 slice.25.refs_1_
  50.7 10.2 %collective-permute-done.1.refs_2_ = bf16[136,2048]{1,0:T(8,128)(2,1)S(1)} collective-permute-done((bf16[136,2048]{1,0:T(8,128)(2,1)S(1)}, bf16[136,2048]{1,0:T(8,128)(2,1)S(1)}, u32[]{:S(2)}, u32[]{:S(2)}) %collective-permute-start.1) | collective-permute-done | bytes 557088 | tf_op jit(solution)/shard_map/ppermute | solution.py:332
  61.0 0.5 slice.26.refs_2_
  61.5 2.1 collective-permute-done.2.refs_3_
  63.6 0.6 slice.27.refs_3_
  64.1 2.1 shard_map.47
  66.2 0.6 slice.28.refs_5_
  66.9 1.8 all-to-all-done.refs_1_.refs_3_
  68.7 0.7 slice_bitcast_fusion.refs_4_
  69.4 2.9 %shard_map.48 = bf16[16,7,8,2048]{3,2,1,0:T(8,128)(2,1)S(1)} custom-call(s32[1]{0:T(128)} %bitcast.zl_ref, bf16[136,2048]{1,0:T(8,128)(2,1)S(1)} %pad_maximum_fusion.block.refs_0_, bf16[136,2048]{1,0:T(8,128)(2,1)S(1)} %collective-permute-done.refs_1_, bf16[136,2048]{1,0:T(8,128)(2,1)S(1)} %collective-permute-done.1.refs_2_, ...), custom_call_target="tpu_custom_call" | custom-call | flops 805306368 | bytes 3670016 | tf_op jit(solution)/shard_map/pallas_call | solution.py:137
  72.2 0.0 copy-start
  72.2 1.9 copy-done
  74.2 0.0 copy-start.9
  74.2 5.6 %all-to-all-start.1 = ((bf16[16,7,8,2048]{3,2,1,0:T(8,128)(2,1)}), bf16[16,7,8,2048]{3,2,1,0:T(8,128)(2,1)}, u32[]{:S(2)}, u32[]{:S(2)}) async-start(bf16[16,7,8,2048]{3,2,1,0:T(8,128)(2,1)} %copy-done), calls=%async_computation.1 | async-start | bytes 7340032 | tf_op jit(solution)/shard_map/all_to_all | solution.py:338
  79.7 0.0 copy-done.9
  79.7 8.5 %collective-permute-start.3 = (bf16[256,1536]{1,0:T(8,128)(2,1)S(1)}, bf16[256,1536]{1,0:T(8,128)(2,1)S(1)}, u32[]{:S(2)}, u32[]{:S(2)}) collective-permute-start(bf16[256,1536]{1,0:T(8,128)(2,1)S(1)} %copy-done.9), channel_id=1, source_target_pairs={{0,256},{256,0},{1,257},{257,1},{2,258},{258,2},{3,259},{259,3},{4... | collective-permute-start | bytes 2359304 | tf_op jit(solution)/shard_map/ppermute | solution.py:390
  88.2 35.0 %collective-permute-done.3.refs_10_.refs_14_ = bf16[256,1536]{1,0:T(8,128)(2,1)S(1)} collective-permute-done((bf16[256,1536]{1,0:T(8,128)(2,1)S(1)}, bf16[256,1536]{1,0:T(8,128)(2,1)S(1)}, u32[]{:S(2)}, u32[]{:S(2)}) %collective-permute-start.3) | collective-permute-done | bytes 786464 | tf_op jit(solution)/shard_map/ppermute | solution.py:390
  123.3 0.0 copy-start.5
  123.3 0.6 slice.29.refs_1_
  123.8 2.1 shard_map.50
  125.9 7.2 %collective-permute-start.7 = (bf16[256,1536]{1,0:T(8,128)(2,1)}, bf16[256,1536]{1,0:T(8,128)(2,1)S(1)}, u32[]{:S(2)}, u32[]{:S(2)}) collective-permute-start(bf16[256,1536]{1,0:T(8,128)(2,1)} %shard_map.50), channel_id=1, source_target_pairs={{0,256},{256,0},{1,257},{257,1},{2,258},{258,2},{3,259},{259,3},{4... | collective-permute-start | bytes 2359304 | tf_op jit(solution)/shard_map/ppermute | solution.py:392
  133.1 3.4 %collective-permute-start.4 = (bf16[256,1536]{1,0:T(8,128)(2,1)S(1)}, bf16[256,1536]{1,0:T(8,128)(2,1)S(1)}, u32[]{:S(2)}, u32[]{:S(2)}) collective-permute-start(bf16[256,1536]{1,0:T(8,128)(2,1)S(1)} %collective-permute-done.3.refs_10_.refs_14_), channel_id=1, source_target_pairs={{0,64},{64,128},{128,192},{192,0},{1,65},{65,129},{129,193},{193,1... | collective-permute-start | bytes 2359304 | tf_op jit(solution)/shard_map/ppermute | solution.py:332
  136.6 3.0 %collective-permute-start.5 = (bf16[256,1536]{1,0:T(8,128)(2,1)S(1)}, bf16[256,1536]{1,0:T(8,128)(2,1)S(1)}, u32[]{:S(2)}, u32[]{:S(2)}) collective-permute-start(bf16[256,1536]{1,0:T(8,128)(2,1)S(1)} %collective-permute-done.3.refs_10_.refs_14_), channel_id=1, source_target_pairs={{0,128},{64,192},{128,0},{192,64},{1,129},{65,193},{129,1},{193,65... | collective-permute-start | bytes 2359304 | tf_op jit(solution)/shard_map/ppermute | solution.py:332
  139.6 4.1 %collective-permute-start.6 = (bf16[256,1536]{1,0:T(8,128)(2,1)S(1)}, bf16[256,1536]{1,0:T(8,128)(2,1)}, u32[]{:S(2)}, u32[]{:S(2)}) collective-permute-start(bf16[256,1536]{1,0:T(8,128)(2,1)S(1)} %collective-permute-done.3.refs_10_.refs_14_), channel_id=1, source_target_pairs={{0,192},{64,0},{128,64},{192,128},{1,193},{65,1},{129,65},{193,129... | collective-permute-start | bytes 2359304 | tf_op jit(solution)/shard_map/ppermute | solution.py:332
  143.7 18.0 %collective-permute-done.7.refs_18_.refs_22_ = bf16[256,1536]{1,0:T(8,128)(2,1)S(1)} collective-permute-done((bf16[256,1536]{1,0:T(8,128)(2,1)}, bf16[256,1536]{1,0:T(8,128)(2,1)S(1)}, u32[]{:S(2)}, u32[]{:S(2)}) %collective-permute-start.7) | collective-permute-done | bytes 786464 | tf_op jit(solution)/shard_map/ppermute | solution.py:392
  161.7 0.0 copy-start.6
  161.7 2.4 %collective-permute-start.10 = (bf16[256,1536]{1,0:T(8,128)(2,1)S(1)}, bf16[256,1536]{1,0:T(8,128)(2,1)}, u32[]{:S(2)}, u32[]{:S(2)}) collective-permute-start(bf16[256,1536]{1,0:T(8,128)(2,1)S(1)} %collective-permute-done.7.refs_18_.refs_22_), channel_id=1, source_target_pairs={{0,192},{64,0},{128,64},{192,128},{1,193},{65,1},{129,65},{193,129... | collective-permute-start | bytes 2359304 | tf_op jit(solution)/shard_map/ppermute | solution.py:332
  164.1 3.4 %collective-permute-start.8 = (bf16[256,1536]{1,0:T(8,128)(2,1)S(1)}, bf16[256,1536]{1,0:T(8,128)(2,1)}, u32[]{:S(2)}, u32[]{:S(2)}) collective-permute-start(bf16[256,1536]{1,0:T(8,128)(2,1)S(1)} %collective-permute-done.7.refs_18_.refs_22_), channel_id=1, source_target_pairs={{0,64},{64,128},{128,192},{192,0},{1,65},{65,129},{129,193},{193,1... | collective-permute-start | bytes 2359304 | tf_op jit(solution)/shard_map/ppermute | solution.py:332
  167.5 0.0 collective-permute-done.4.refs_11_.refs_15_
  167.5 0.0 copy-start.7
  167.5 5.3 %collective-permute-start.9 = (bf16[256,1536]{1,0:T(8,128)(2,1)S(1)}, bf16[256,1536]{1,0:T(8,128)(2,1)}, u32[]{:S(2)}, u32[]{:S(2)}) collective-permute-start(bf16[256,1536]{1,0:T(8,128)(2,1)S(1)} %collective-permute-done.7.refs_18_.refs_22_), channel_id=1, source_target_pairs={{0,128},{64,192},{128,0},{192,64},{1,129},{65,193},{129,1},{193,65... | collective-permute-start | bytes 2359304 | tf_op jit(solution)/shard_map/ppermute | solution.py:332
  172.8 0.1 pad_add_fusion.where_ref.refs_0_
  172.9 0.0 copy-start.4
  172.9 0.0 all-to-all-done.1.last_ref.refs_2_.refs_4_
  172.9 2.5 %shard_map.49 = (bf16[2,640,128]{2,1,0:T(8,128)(2,1)S(1)}, bf16[512,512]{1,0:T(8,128)(2,1)S(1)}, bf16[2,64,128]{2,1,0:T(8,128)(2,1)S(1)}) custom-call(s32[3]{0:T(128)S(1)} %pad_add_fusion.where_ref.refs_0_, bf16[16,7,8,2048]{3,2,1,0:T(8,128)(2,1)} %all-to-all-done.1.last_ref.refs_2_.refs_4_), custom_call_target="tpu_custom_call" | custom-call | flops 100000000 | bytes 1000000 | tf_op jit(solution)/shard_map/pallas_call | solution.py:210
  175.4 0.0 copy-done.5
  175.4 0.0 copy-done.6
  175.4 0.0 copy-done.7
  175.5 0.0 copy-done.4
  175.5 0.0 copy-start.1
  175.5 0.8 copy-done.1
  176.3 0.0 copy-start.2
  176.3 0.7 copy-done.2
  177.0 0.6 copy-done.3
  177.6 0.0 collective-permute-done.5.refs_12_.refs_16_
  177.6 0.0 copy-start.8
  177.6 0.0 collective-permute-done.6.refs_13_.refs_17_
  177.6 16.6 %collective-permute-done.10.refs_21_.refs_25_ = bf16[256,1536]{1,0:T(8,128)(2,1)} collective-permute-done((bf16[256,1536]{1,0:T(8,128)(2,1)S(1)}, bf16[256,1536]{1,0:T(8,128)(2,1)}, u32[]{:S(2)}, u32[]{:S(2)}) %collective-permute-start.10) | collective-permute-done | bytes 786464 | tf_op jit(solution)/shard_map/ppermute | solution.py:332
  194.2 0.0 collective-permute-done.8.refs_19_.refs_23_
  194.2 14.9 %collective-permute-done.9.refs_20_.refs_24_ = bf16[256,1536]{1,0:T(8,128)(2,1)} collective-permute-done((bf16[256,1536]{1,0:T(8,128)(2,1)S(1)}, bf16[256,1536]{1,0:T(8,128)(2,1)}, u32[]{:S(2)}, u32[]{:S(2)}) %collective-permute-start.9) | collective-permute-done | bytes 786464 | tf_op jit(solution)/shard_map/ppermute | solution.py:332
  209.1 0.0 all-gather.3.cloned.1.call-done
  209.1 0.0 copy-done.8
  209.1 18.2 %shard_map.51 = bf16[2,9,64,768]{3,2,1,0:T(8,128)(2,1)} custom-call(s32[3]{0:T(128)} %copy-done.4, bf16[16,3,8,2048]{3,2,1,0:T(8,128)(2,1)} %all-to-all-done.refs_1_.refs_3_, bf16[16,7,8,2048]{3,2,1,0:T(8,128)(2,1)} %all-to-all-done.1.last_ref.refs_2_.refs_4_, bf16[16,3,8,2048]{3,2,1,0:T(8,128)(2,1)} %all-to-all-done.refs_1_.refs_3_, ...), custom_call_target="tpu_custom_call" | custom-call | flops 8053063680 | bytes 20000000 | tf_op jit(solution)/shard_map/pallas_call | solution.py:300
  (1 shorter events, 0.0 us)
Async XLA Ops:
  9.0 41.2 %collective-permute-start = (bf16[136,2048]{1,0:T(8,128)(2,1)S(1)}, bf16[136,2048]{1,0:T(8,128)(2,1)S(1)}, u32[]{:S(2)}, u32[]{:S(2)}) collective-permute-start(bf16[136,2048]{1,0:T(8,128)(2,1)S(1)} %pad_maximum_fusion.block.refs_0_), channel_id=1, source_target_pairs={{0,16},{16,32},{32,48},{48,0},{1,17},{17,33},{33,49},{49,1},{2,18}... | collective-permute-start | bytes 1671176 | tf_op jit(solution)/shard_map/ppermute | solution.py:332
  13.3 47.7 %collective-permute-start.1 = (bf16[136,2048]{1,0:T(8,128)(2,1)S(1)}, bf16[136,2048]{1,0:T(8,128)(2,1)S(1)}, u32[]{:S(2)}, u32[]{:S(2)}) collective-permute-start(bf16[136,2048]{1,0:T(8,128)(2,1)S(1)} %pad_maximum_fusion.block.refs_0_), channel_id=1, source_target_pairs={{0,32},{16,48},{32,0},{48,16},{1,33},{17,49},{33,1},{49,17},{2,34}... | collective-permute-start | bytes 1671176 | tf_op jit(solution)/shard_map/ppermute | solution.py:332
  17.0 46.5 %collective-permute-start.2 = (bf16[136,2048]{1,0:T(8,128)(2,1)S(1)}, bf16[136,2048]{1,0:T(8,128)(2,1)S(1)}, u32[]{:S(2)}, u32[]{:S(2)}) collective-permute-start(bf16[136,2048]{1,0:T(8,128)(2,1)S(1)} %pad_maximum_fusion.block.refs_0_), channel_id=1, source_target_pairs={{0,48},{16,0},{32,16},{48,32},{1,49},{17,1},{33,17},{49,33},{2,50}... | collective-permute-start | bytes 1671176 | tf_op jit(solution)/shard_map/ppermute | solution.py:332
  23.5 45.2 %all-to-all-start = ((bf16[16,3,8,2048]{3,2,1,0:T(8,128)(2,1)}), bf16[16,3,8,2048]{3,2,1,0:T(8,128)(2,1)}, u32[]{:S(2)}, u32[]{:S(2)}) async-start(bf16[16,3,8,2048]{3,2,1,0:T(8,128)(2,1)} %shard_map.46), calls=%async_computation | async-start | bytes 3145728 | tf_op jit(solution)/shard_map/all_to_all | solution.py:338
  30.8 178.3 %all-gather.3.cloned.1.call-start = ((), (), s32[]{:S(2)}) async-start(), calls=%async_computation.2 | async-start | bytes 7864320 | tf_op jit(solution)/shard_map/all_gather | solution.py:386
  72.2 1.9 copy-start
  74.2 5.6 %copy-start.9 = (bf16[256,1536]{1,0:T(8,128)(2,1)S(1)}, bf16[256,1536]{1,0:T(8,128)(2,1)}, u32[]{:S(2)}) copy-start(bf16[256,1536]{1,0:T(8,128)(2,1)} %shard_map.47) | copy-start | bytes 2359300
  74.2 98.7 %all-to-all-start.1 = ((bf16[16,7,8,2048]{3,2,1,0:T(8,128)(2,1)}), bf16[16,7,8,2048]{3,2,1,0:T(8,128)(2,1)}, u32[]{:S(2)}, u32[]{:S(2)}) async-start(bf16[16,7,8,2048]{3,2,1,0:T(8,128)(2,1)} %copy-done), calls=%async_computation.1 | async-start | bytes 7340032 | tf_op jit(solution)/shard_map/all_to_all | solution.py:338
  79.7 43.5 %collective-permute-start.3 = (bf16[256,1536]{1,0:T(8,128)(2,1)S(1)}, bf16[256,1536]{1,0:T(8,128)(2,1)S(1)}, u32[]{:S(2)}, u32[]{:S(2)}) collective-permute-start(bf16[256,1536]{1,0:T(8,128)(2,1)S(1)} %copy-done.9), channel_id=1, source_target_pairs={{0,256},{256,0},{1,257},{257,1},{2,258},{258,2},{3,259},{259,3},{4... | collective-permute-start | bytes 2359304 | tf_op jit(solution)/shard_map/ppermute | solution.py:390
  123.3 52.2 %copy-start.5 = (bf16[256,1536]{1,0:T(8,128)(2,1)}, bf16[256,1536]{1,0:T(8,128)(2,1)S(1)}, u32[]{:S(2)}) copy-start(bf16[256,1536]{1,0:T(8,128)(2,1)S(1)} %collective-permute-done.3.refs_10_.refs_14_) | copy-start | bytes 2359300
  125.9 35.8 %collective-permute-start.7 = (bf16[256,1536]{1,0:T(8,128)(2,1)}, bf16[256,1536]{1,0:T(8,128)(2,1)S(1)}, u32[]{:S(2)}, u32[]{:S(2)}) collective-permute-start(bf16[256,1536]{1,0:T(8,128)(2,1)} %shard_map.50), channel_id=1, source_target_pairs={{0,256},{256,0},{1,257},{257,1},{2,258},{258,2},{3,259},{259,3},{4... | collective-permute-start | bytes 2359304 | tf_op jit(solution)/shard_map/ppermute | solution.py:392
  133.1 34.4 %collective-permute-start.4 = (bf16[256,1536]{1,0:T(8,128)(2,1)S(1)}, bf16[256,1536]{1,0:T(8,128)(2,1)S(1)}, u32[]{:S(2)}, u32[]{:S(2)}) collective-permute-start(bf16[256,1536]{1,0:T(8,128)(2,1)S(1)} %collective-permute-done.3.refs_10_.refs_14_), channel_id=1, source_target_pairs={{0,64},{64,128},{128,192},{192,0},{1,65},{65,129},{129,193},{193,1... | collective-permute-start | bytes 2359304 | tf_op jit(solution)/shard_map/ppermute | solution.py:332
  136.6 41.0 %collective-permute-start.5 = (bf16[256,1536]{1,0:T(8,128)(2,1)S(1)}, bf16[256,1536]{1,0:T(8,128)(2,1)S(1)}, u32[]{:S(2)}, u32[]{:S(2)}) collective-permute-start(bf16[256,1536]{1,0:T(8,128)(2,1)S(1)} %collective-permute-done.3.refs_10_.refs_14_), channel_id=1, source_target_pairs={{0,128},{64,192},{128,0},{192,64},{1,129},{65,193},{129,1},{193,65... | collective-permute-start | bytes 2359304 | tf_op jit(solution)/shard_map/ppermute | solution.py:332
  139.6 38.0 %collective-permute-start.6 = (bf16[256,1536]{1,0:T(8,128)(2,1)S(1)}, bf16[256,1536]{1,0:T(8,128)(2,1)}, u32[]{:S(2)}, u32[]{:S(2)}) collective-permute-start(bf16[256,1536]{1,0:T(8,128)(2,1)S(1)} %collective-permute-done.3.refs_10_.refs_14_), channel_id=1, source_target_pairs={{0,192},{64,0},{128,64},{192,128},{1,193},{65,1},{129,65},{193,129... | collective-permute-start | bytes 2359304 | tf_op jit(solution)/shard_map/ppermute | solution.py:332
  161.7 13.8 %copy-start.6 = (bf16[256,1536]{1,0:T(8,128)(2,1)}, bf16[256,1536]{1,0:T(8,128)(2,1)S(1)}, u32[]{:S(2)}) copy-start(bf16[256,1536]{1,0:T(8,128)(2,1)S(1)} %collective-permute-done.7.refs_18_.refs_22_) | copy-start | bytes 2359300
  161.7 32.5 %collective-permute-start.10 = (bf16[256,1536]{1,0:T(8,128)(2,1)S(1)}, bf16[256,1536]{1,0:T(8,128)(2,1)}, u32[]{:S(2)}, u32[]{:S(2)}) collective-permute-start(bf16[256,1536]{1,0:T(8,128)(2,1)S(1)} %collective-permute-done.7.refs_18_.refs_22_), channel_id=1, source_target_pairs={{0,192},{64,0},{128,64},{192,128},{1,193},{65,1},{129,65},{193,129... | collective-permute-start | bytes 2359304 | tf_op jit(solution)/shard_map/ppermute | solution.py:332
  164.1 30.1 %collective-permute-start.8 = (bf16[256,1536]{1,0:T(8,128)(2,1)S(1)}, bf16[256,1536]{1,0:T(8,128)(2,1)}, u32[]{:S(2)}, u32[]{:S(2)}) collective-permute-start(bf16[256,1536]{1,0:T(8,128)(2,1)S(1)} %collective-permute-done.7.refs_18_.refs_22_), channel_id=1, source_target_pairs={{0,64},{64,128},{128,192},{192,0},{1,65},{65,129},{129,193},{193,1... | collective-permute-start | bytes 2359304 | tf_op jit(solution)/shard_map/ppermute | solution.py:332
  167.5 7.9 %copy-start.7 = (bf16[256,1536]{1,0:T(8,128)(2,1)}, bf16[256,1536]{1,0:T(8,128)(2,1)S(1)}, u32[]{:S(2)}) copy-start(bf16[256,1536]{1,0:T(8,128)(2,1)S(1)} %collective-permute-done.4.refs_11_.refs_15_) | copy-start | bytes 2359300
  167.5 41.6 %collective-permute-start.9 = (bf16[256,1536]{1,0:T(8,128)(2,1)S(1)}, bf16[256,1536]{1,0:T(8,128)(2,1)}, u32[]{:S(2)}, u32[]{:S(2)}) collective-permute-start(bf16[256,1536]{1,0:T(8,128)(2,1)S(1)} %collective-permute-done.7.refs_18_.refs_22_), channel_id=1, source_target_pairs={{0,128},{64,192},{128,0},{192,64},{1,129},{65,193},{129,1},{193,65... | collective-permute-start | bytes 2359304 | tf_op jit(solution)/shard_map/ppermute | solution.py:332
  172.9 2.6 %copy-start.4 = (s32[3]{0:T(128)}, s32[3]{0:T(128)S(1)}, u32[]{:S(2)}) copy-start(s32[3]{0:T(128)S(1)} %pad_add_fusion.where_ref.refs_0_) | copy-start | bytes 40
  175.5 0.8 copy-start.1
  176.3 0.7 copy-start.2
  177.0 0.6 copy-start.3
  177.6 31.5 %copy-start.8 = (bf16[256,1536]{1,0:T(8,128)(2,1)}, bf16[256,1536]{1,0:T(8,128)(2,1)S(1)}, u32[]{:S(2)}) copy-start(bf16[256,1536]{1,0:T(8,128)(2,1)S(1)} %collective-permute-done.5.refs_12_.refs_16_) | copy-start | bytes 2359300
Sparse Core Ops, SparseCore 0:
  33.7 73.6 all-gather.2

commit v9 on v6

--- a/solution.py
+++ b/solution.py
@@ -23,7 +23,7 @@
 TILE = 256
 INFO = 2 * TOK
 
-TAKE_COST = (40 * 10**9, 0 * 10**9)
+TAKE_COST = (40 * 10**9, 55 * 10**9)
 f32 = jnp.float32
 bf16 = jnp.bfloat16
 

time: 229 us -> 225 us (0.983)
  the two profiles are of different devices: /device:TPU:64 before, /device:TPU:248 now
where the time goes in v9:
time: 225 us; the launch traced here: 224 us
  waiting for transfers between devices  89.8 us (40%)
  starting transfers between devices  75.6 us (34%)
  Pallas kernels  33.1 us (15%)
  between operations  13.6 us (6%)
  local copies, waits for them, and re-layouts  9.45 us (4%)
  other arithmetic  2.53 us (1%)
    ppermute x9, waiting for transfers between devices, over(): lax.ppermute(block, axis, [(i, (i + b) % count) for i in range(count)])  39.3 us
    ppermute x9, starting transfers between devices, over(): lax.ppermute(block, axis, [(i, (i + b) % count) for i in range(count)])  31.4 us
    ppermute x1, starting transfers between devices, shards(): first = lax.ppermute(taken, 'zh', swap)  26.1 us
    ppermute x1, waiting for transfers between devices, shards(): first = lax.ppermute(taken, 'zh', swap)  21.1 us
    pallas_call x2, Pallas kernels, expert(): pl.pallas_call(functools.partial(expert_kernel, len(far)), grid_spec=pltp...  21 us
    ppermute x1, waiting for transfers between devices, shards(): second = lax.ppermute(take(expert_weights, 1, first), 'zh', swap)  18.1 us
    all_to_all x2, starting transfers between devices, over_peers(): lax.all_to_all(message, ('y', 'c'), split_axis=0, concat_axis=0, tiled=True)  13.8 us
    all_to_all x2, waiting for transfers between devices, over_peers(): lax.all_to_all(message, ('y', 'c'), split_axis=0, concat_axis=0, tiled=True)  10.6 us
  transfers between devices with their start and end apart: 14, of which 5 were waited for; matrix products, arithmetic and copies ran while one was open for 2% of the time, Pallas kernels for 10%

profile of v9, /device:TPU:248, one launch (start us, length us, event | category | flops | bytes accessed | tf_op | source)
XLA Modules:
  0.0 224.1 jit_solution(5075630182378948269)
XLA Ops:
  6.5 0.7 convert_bitcast_fusion
  7.2 0.7 fusion.2
  7.9 1.1 pad_maximum_fusion.block.refs_0_
  9.0 1.9 collective-permute-start
  10.9 3.0 %collective-permute-start.1 = (bf16[136,2048]{1,0:T(8,128)(2,1)S(1)}, bf16[136,2048]{1,0:T(8,128)(2,1)S(1)}, u32[]{:S(2)}, u32[]{:S(2)}) collective-permute-start(bf16[136,2048]{1,0:T(8,128)(2,1)S(1)} %pad_maximum_fusion.block.refs_0_), channel_id=1, source_target_pairs={{0,32},{16,48},{32,0},{48,16},{1,33},{17,49},{33,1},{49,17},{2,34}... | collective-permute-start | bytes 1671176 | tf_op jit(solution)/shard_map/ppermute | solution.py:321
  13.9 2.8 %collective-permute-start.2 = (bf16[136,2048]{1,0:T(8,128)(2,1)S(1)}, bf16[136,2048]{1,0:T(8,128)(2,1)S(1)}, u32[]{:S(2)}, u32[]{:S(2)}) collective-permute-start(bf16[136,2048]{1,0:T(8,128)(2,1)S(1)} %pad_maximum_fusion.block.refs_0_), channel_id=1, source_target_pairs={{0,48},{16,0},{32,16},{48,32},{1,49},{17,1},{33,17},{49,33},{2,50}... | collective-permute-start | bytes 1671176 | tf_op jit(solution)/shard_map/ppermute | solution.py:321
  16.8 2.6 %shard_map.46 = bf16[16,3,8,2048]{3,2,1,0:T(8,128)(2,1)} custom-call(s32[1]{0:T(128)} %bitcast.zl_ref, bf16[136,2048]{1,0:T(8,128)(2,1)S(1)} %pad_maximum_fusion.block.refs_0_), custom_call_target="tpu_custom_call" | custom-call | flops 201326592 | bytes 1572864 | tf_op jit(solution)/shard_map/pallas_call | solution.py:137
  19.3 6.9 %all-to-all-start = ((bf16[16,3,8,2048]{3,2,1,0:T(8,128)(2,1)}), bf16[16,3,8,2048]{3,2,1,0:T(8,128)(2,1)}, u32[]{:S(2)}, u32[]{:S(2)}) async-start(bf16[16,3,8,2048]{3,2,1,0:T(8,128)(2,1)} %shard_map.46), calls=%async_computation | async-start | bytes 3145728 | tf_op jit(solution)/shard_map/all_to_all | solution.py:327
  26.2 0.0 all-gather.3.cloned.1.call-start
  26.3 0.7 all-gather.3.cloned.1.call-update
  27.0 0.0 collective-permute-done.refs_1_
  27.0 0.6 slice.25.refs_1_
  27.6 32.6 %collective-permute-done.1.refs_2_ = bf16[136,2048]{1,0:T(8,128)(2,1)S(1)} collective-permute-done((bf16[136,2048]{1,0:T(8,128)(2,1)S(1)}, bf16[136,2048]{1,0:T(8,128)(2,1)S(1)}, u32[]{:S(2)}, u32[]{:S(2)}) %collective-permute-start.1) | collective-permute-done | bytes 557088 | tf_op jit(solution)/shard_map/ppermute | solution.py:321
  60.2 0.6 slice.26.refs_2_
  60.7 0.0 collective-permute-done.2.refs_3_
  60.7 0.5 slice.27.refs_3_
  61.3 2.1 shard_map.47
  63.4 26.1 %collective-permute-start.3 = (bf16[256,1536]{1,0:T(8,128)(2,1)}, bf16[256,1536]{1,0:T(8,128)(2,1)S(1)}, u32[]{:S(2)}, u32[]{:S(2)}) collective-permute-start(bf16[256,1536]{1,0:T(8,128)(2,1)} %shard_map.47), channel_id=1, source_target_pairs={{0,256},{256,0},{1,257},{257,1},{2,258},{258,2},{3,259},{259,3},{4... | collective-permute-start | bytes 2359304 | tf_op jit(solution)/shard_map/ppermute | solution.py:379
  89.5 0.7 slice.28.refs_5_
  90.2 0.0 all-to-all-done.refs_1_.refs_3_
  90.2 0.7 slice_bitcast_fusion.refs_4_
  90.9 2.9 %shard_map.48 = bf16[16,7,8,2048]{3,2,1,0:T(8,128)(2,1)S(1)} custom-call(s32[1]{0:T(128)} %bitcast.zl_ref, bf16[136,2048]{1,0:T(8,128)(2,1)S(1)} %pad_maximum_fusion.block.refs_0_, bf16[136,2048]{1,0:T(8,128)(2,1)S(1)} %collective-permute-done.refs_1_, bf16[136,2048]{1,0:T(8,128)(2,1)S(1)} %collective-permute-done.1.refs_2_, ...), custom_call_target="tpu_custom_call" | custom-call | flops 805306368 | bytes 3670016 | tf_op jit(solution)/shard_map/pallas_call | solution.py:137
  93.7 0.0 copy-start
  93.7 1.9 copy-done
  95.7 6.9 %all-to-all-start.1 = ((bf16[16,7,8,2048]{3,2,1,0:T(8,128)(2,1)}), bf16[16,7,8,2048]{3,2,1,0:T(8,128)(2,1)}, u32[]{:S(2)}, u32[]{:S(2)}) async-start(bf16[16,7,8,2048]{3,2,1,0:T(8,128)(2,1)} %copy-done), calls=%async_computation.1 | async-start | bytes 7340032 | tf_op jit(solution)/shard_map/all_to_all | solution.py:327
  102.6 21.1 %collective-permute-done.3.refs_10_.refs_14_ = bf16[256,1536]{1,0:T(8,128)(2,1)S(1)} collective-permute-done((bf16[256,1536]{1,0:T(8,128)(2,1)}, bf16[256,1536]{1,0:T(8,128)(2,1)S(1)}, u32[]{:S(2)}, u32[]{:S(2)}) %collective-permute-start.3) | collective-permute-done | bytes 786464 | tf_op jit(solution)/shard_map/ppermute | solution.py:379
  123.7 0.0 copy-start.5
  123.7 0.6 slice.29.refs_1_
  124.3 2.1 shard_map.50
  126.3 4.3 %collective-permute-start.4 = (bf16[256,1536]{1,0:T(8,128)(2,1)}, bf16[256,1536]{1,0:T(8,128)(2,1)S(1)}, u32[]{:S(2)}, u32[]{:S(2)}) collective-permute-start(bf16[256,1536]{1,0:T(8,128)(2,1)} %shard_map.50), channel_id=1, source_target_pairs={{0,256},{256,0},{1,257},{257,1},{2,258},{258,2},{3,259},{259,3},{4... | collective-permute-start | bytes 2359304 | tf_op jit(solution)/shard_map/ppermute | solution.py:381
  130.6 4.7 %collective-permute-start.10 = (bf16[256,1536]{1,0:T(8,128)(2,1)S(1)}, bf16[256,1536]{1,0:T(8,128)(2,1)S(1)}, u32[]{:S(2)}, u32[]{:S(2)}) collective-permute-start(bf16[256,1536]{1,0:T(8,128)(2,1)S(1)} %collective-permute-done.3.refs_10_.refs_14_), channel_id=1, source_target_pairs={{0,192},{64,0},{128,64},{192,128},{1,193},{65,1},{129,65},{193,129... | collective-permute-start | bytes 2359304 | tf_op jit(solution)/shard_map/ppermute | solution.py:321
  135.3 1.9 collective-permute-start.8
  137.3 0.0 copy-done.5
  137.3 4.1 %collective-permute-start.9 = (bf16[256,1536]{1,0:T(8,128)(2,1)S(1)}, bf16[256,1536]{1,0:T(8,128)(2,1)}, u32[]{:S(2)}, u32[]{:S(2)}) collective-permute-start(bf16[256,1536]{1,0:T(8,128)(2,1)S(1)} %collective-permute-done.3.refs_10_.refs_14_), channel_id=1, source_target_pairs={{0,128},{64,192},{128,0},{192,64},{1,129},{65,193},{129,1},{193,65... | collective-permute-start | bytes 2359304 | tf_op jit(solution)/shard_map/ppermute | solution.py:321
  141.4 18.1 %collective-permute-done.4.refs_10_.refs_14_ = bf16[256,1536]{1,0:T(8,128)(2,1)S(1)} collective-permute-done((bf16[256,1536]{1,0:T(8,128)(2,1)}, bf16[256,1536]{1,0:T(8,128)(2,1)S(1)}, u32[]{:S(2)}, u32[]{:S(2)}) %collective-permute-start.4) | collective-permute-done | bytes 786464 | tf_op jit(solution)/shard_map/ppermute | solution.py:381
  159.6 0.0 copy-start.6
  159.6 3.7 %collective-permute-start.5 = (bf16[256,1536]{1,0:T(8,128)(2,1)S(1)}, bf16[256,1536]{1,0:T(8,128)(2,1)S(1)}, u32[]{:S(2)}, u32[]{:S(2)}) collective-permute-start(bf16[256,1536]{1,0:T(8,128)(2,1)S(1)} %collective-permute-done.4.refs_10_.refs_14_), channel_id=1, source_target_pairs={{0,64},{64,128},{128,192},{192,0},{1,65},{65,129},{129,193},{193,1... | collective-permute-start | bytes 2359304 | tf_op jit(solution)/shard_map/ppermute | solution.py:321
  163.3 4.3 %collective-permute-start.6 = (bf16[256,1536]{1,0:T(8,128)(2,1)S(1)}, bf16[256,1536]{1,0:T(8,128)(2,1)}, u32[]{:S(2)}, u32[]{:S(2)}) collective-permute-start(bf16[256,1536]{1,0:T(8,128)(2,1)S(1)} %collective-permute-done.4.refs_10_.refs_14_), channel_id=1, source_target_pairs={{0,128},{64,192},{128,0},{192,64},{1,129},{65,193},{129,1},{193,65... | collective-permute-start | bytes 2359304 | tf_op jit(solution)/shard_map/ppermute | solution.py:321
  167.6 0.0 collective-permute-done.10.refs_13_.refs_17_
  167.6 0.0 copy-start.8
  167.7 0.9 copy-done.8
  168.5 4.8 %collective-permute-start.7 = (bf16[256,1536]{1,0:T(8,128)(2,1)S(1)}, bf16[256,1536]{1,0:T(8,128)(2,1)}, u32[]{:S(2)}, u32[]{:S(2)}) collective-permute-start(bf16[256,1536]{1,0:T(8,128)(2,1)S(1)} %collective-permute-done.4.refs_10_.refs_14_), channel_id=1, source_target_pairs={{0,192},{64,0},{128,64},{192,128},{1,193},{65,1},{129,65},{193,129... | collective-permute-start | bytes 2359304 | tf_op jit(solution)/shard_map/ppermute | solution.py:321
  173.4 0.1 pad_add_fusion.where_ref.refs_0_
  173.4 0.0 copy-start.4
  173.4 10.6 %all-to-all-done.1.last_ref.refs_2_.refs_4_ = bf16[16,7,8,2048]{3,2,1,0:T(8,128)(2,1)} async-done(((bf16[16,7,8,2048]{3,2,1,0:T(8,128)(2,1)}), bf16[16,7,8,2048]{3,2,1,0:T(8,128)(2,1)}, u32[]{:S(2)}, u32[]{:S(2)}) %all-to-all-start.1) | async-done | bytes 3670048 | tf_op jit(solution)/shard_map/all_to_all | solution.py:327
  184.0 2.5 %shard_map.49 = (bf16[2,640,128]{2,1,0:T(8,128)(2,1)S(1)}, bf16[512,512]{1,0:T(8,128)(2,1)S(1)}, bf16[2,64,128]{2,1,0:T(8,128)(2,1)S(1)}) custom-call(s32[3]{0:T(128)S(1)} %pad_add_fusion.where_ref.refs_0_, bf16[16,7,8,2048]{3,2,1,0:T(8,128)(2,1)} %all-to-all-done.1.last_ref.refs_2_.refs_4_), custom_call_target="tpu_custom_call" | custom-call | flops 100000000 | bytes 1000000 | tf_op jit(solution)/shard_map/pallas_call | solution.py:210
  186.6 0.0 copy-done.6
  186.6 0.0 copy-done.4
  186.6 0.0 copy-start.1
  186.6 0.8 copy-done.1
  187.4 0.0 copy-start.2
  187.4 0.7 copy-done.2
  188.1 0.0 copy-start.3
  188.1 0.6 copy-done.3
  188.7 0.0 collective-permute-done.8.refs_11_.refs_15_
  188.7 0.0 collective-permute-done.9.refs_12_.refs_16_
  188.7 0.0 all-gather.3.cloned.1.call-done
  188.7 10.5 %shard_map.51.refs_18_ = bf16[2,9,64,768]{3,2,1,0:T(8,128)(2,1)} custom-call(s32[3]{0:T(128)} %copy-done.4, bf16[16,3,8,2048]{3,2,1,0:T(8,128)(2,1)} %all-to-all-done.refs_1_.refs_3_, bf16[16,7,8,2048]{3,2,1,0:T(8,128)(2,1)} %all-to-all-done.1.last_ref.refs_2_.refs_4_, bf16[16,3,8,2048]{3,2,1,0:T(8,128)(2,1)} %all-to-all-done.refs_1_.refs_3_, ...), custom_call_target="tpu_custom_call" | custom-call | flops 3000000000 | bytes 10000000 | tf_op jit(solution)/shard_map/pallas_call | solution.py:286
  199.2 6.7 %collective-permute-done.5.refs_11_.refs_15_ = bf16[256,1536]{1,0:T(8,128)(2,1)S(1)} collective-permute-done((bf16[256,1536]{1,0:T(8,128)(2,1)S(1)}, bf16[256,1536]{1,0:T(8,128)(2,1)S(1)}, u32[]{:S(2)}, u32[]{:S(2)}) %collective-permute-start.5) | collective-permute-done | bytes 786464 | tf_op jit(solution)/shard_map/ppermute | solution.py:321
  205.9 0.0 copy-start.7
  205.9 0.0 collective-permute-done.6.refs_12_.refs_16_
  205.9 0.0 collective-permute-done.7.refs_13_.refs_17_
  205.9 0.9 copy-done.7
  206.8 10.5 %shard_map.52 = bf16[2,9,64,768]{3,2,1,0:T(8,128)(2,1)} custom-call(s32[3]{0:T(128)} %copy-done.4, bf16[16,3,8,2048]{3,2,1,0:T(8,128)(2,1)} %all-to-all-done.refs_1_.refs_3_, bf16[16,7,8,2048]{3,2,1,0:T(8,128)(2,1)} %all-to-all-done.1.last_ref.refs_2_.refs_4_, ...), custom_call_target="tpu_custom_call", output_to_operand_aliasing={{}: (18, {})} | custom-call | flops 4026531840 | bytes 10000000 | tf_op jit(solution)/shard_map/pallas_call | solution.py:286
Async XLA Ops:
  9.0 18.0 %collective-permute-start = (bf16[136,2048]{1,0:T(8,128)(2,1)S(1)}, bf16[136,2048]{1,0:T(8,128)(2,1)S(1)}, u32[]{:S(2)}, u32[]{:S(2)}) collective-permute-start(bf16[136,2048]{1,0:T(8,128)(2,1)S(1)} %pad_maximum_fusion.block.refs_0_), channel_id=1, source_target_pairs={{0,16},{16,32},{32,48},{48,0},{1,17},{17,33},{33,49},{49,1},{2,18}... | collective-permute-start | bytes 1671176 | tf_op jit(solution)/shard_map/ppermute | solution.py:321
  10.9 49.2 %collective-permute-start.1 = (bf16[136,2048]{1,0:T(8,128)(2,1)S(1)}, bf16[136,2048]{1,0:T(8,128)(2,1)S(1)}, u32[]{:S(2)}, u32[]{:S(2)}) collective-permute-start(bf16[136,2048]{1,0:T(8,128)(2,1)S(1)} %pad_maximum_fusion.block.refs_0_), channel_id=1, source_target_pairs={{0,32},{16,48},{32,0},{48,16},{1,33},{17,49},{33,1},{49,17},{2,34}... | collective-permute-start | bytes 1671176 | tf_op jit(solution)/shard_map/ppermute | solution.py:321
  13.9 46.8 %collective-permute-start.2 = (bf16[136,2048]{1,0:T(8,128)(2,1)S(1)}, bf16[136,2048]{1,0:T(8,128)(2,1)S(1)}, u32[]{:S(2)}, u32[]{:S(2)}) collective-permute-start(bf16[136,2048]{1,0:T(8,128)(2,1)S(1)} %pad_maximum_fusion.block.refs_0_), channel_id=1, source_target_pairs={{0,48},{16,0},{32,16},{48,32},{1,49},{17,1},{33,17},{49,33},{2,50}... | collective-permute-start | bytes 1671176 | tf_op jit(solution)/shard_map/ppermute | solution.py:321
  19.3 70.9 %all-to-all-start = ((bf16[16,3,8,2048]{3,2,1,0:T(8,128)(2,1)}), bf16[16,3,8,2048]{3,2,1,0:T(8,128)(2,1)}, u32[]{:S(2)}, u32[]{:S(2)}) async-start(bf16[16,3,8,2048]{3,2,1,0:T(8,128)(2,1)} %shard_map.46), calls=%async_computation | async-start | bytes 3145728 | tf_op jit(solution)/shard_map/all_to_all | solution.py:327
  26.2 162.4 %all-gather.3.cloned.1.call-start = ((), (), s32[]{:S(2)}) async-start(), calls=%async_computation.2 | async-start | bytes 7864320 | tf_op jit(solution)/shard_map/all_gather | solution.py:375
  63.4 60.3 %collective-permute-start.3 = (bf16[256,1536]{1,0:T(8,128)(2,1)}, bf16[256,1536]{1,0:T(8,128)(2,1)S(1)}, u32[]{:S(2)}, u32[]{:S(2)}) collective-permute-start(bf16[256,1536]{1,0:T(8,128)(2,1)} %shard_map.47), channel_id=1, source_target_pairs={{0,256},{256,0},{1,257},{257,1},{2,258},{258,2},{3,259},{259,3},{4... | collective-permute-start | bytes 2359304 | tf_op jit(solution)/shard_map/ppermute | solution.py:379
  93.7 1.9 copy-start
  95.7 88.3 %all-to-all-start.1 = ((bf16[16,7,8,2048]{3,2,1,0:T(8,128)(2,1)}), bf16[16,7,8,2048]{3,2,1,0:T(8,128)(2,1)}, u32[]{:S(2)}, u32[]{:S(2)}) async-start(bf16[16,7,8,2048]{3,2,1,0:T(8,128)(2,1)} %copy-done), calls=%async_computation.1 | async-start | bytes 7340032 | tf_op jit(solution)/shard_map/all_to_all | solution.py:327
  123.7 13.6 %copy-start.5 = (bf16[256,1536]{1,0:T(8,128)(2,1)}, bf16[256,1536]{1,0:T(8,128)(2,1)S(1)}, u32[]{:S(2)}) copy-start(bf16[256,1536]{1,0:T(8,128)(2,1)S(1)} %collective-permute-done.3.refs_10_.refs_14_) | copy-start | bytes 2359300
  126.3 33.2 %collective-permute-start.4 = (bf16[256,1536]{1,0:T(8,128)(2,1)}, bf16[256,1536]{1,0:T(8,128)(2,1)S(1)}, u32[]{:S(2)}, u32[]{:S(2)}) collective-permute-start(bf16[256,1536]{1,0:T(8,128)(2,1)} %shard_map.50), channel_id=1, source_target_pairs={{0,256},{256,0},{1,257},{257,1},{2,258},{258,2},{3,259},{259,3},{4... | collective-permute-start | bytes 2359304 | tf_op jit(solution)/shard_map/ppermute | solution.py:381
  130.6 37.0 %collective-permute-start.10 = (bf16[256,1536]{1,0:T(8,128)(2,1)S(1)}, bf16[256,1536]{1,0:T(8,128)(2,1)S(1)}, u32[]{:S(2)}, u32[]{:S(2)}) collective-permute-start(bf16[256,1536]{1,0:T(8,128)(2,1)S(1)} %collective-permute-done.3.refs_10_.refs_14_), channel_id=1, source_target_pairs={{0,192},{64,0},{128,64},{192,128},{1,193},{65,1},{129,65},{193,129... | collective-permute-start | bytes 2359304 | tf_op jit(solution)/shard_map/ppermute | solution.py:321
  135.3 53.3 %collective-permute-start.8 = (bf16[256,1536]{1,0:T(8,128)(2,1)S(1)}, bf16[256,1536]{1,0:T(8,128)(2,1)}, u32[]{:S(2)}, u32[]{:S(2)}) collective-permute-start(bf16[256,1536]{1,0:T(8,128)(2,1)S(1)} %collective-permute-done.3.refs_10_.refs_14_), channel_id=1, source_target_pairs={{0,64},{64,128},{128,192},{192,0},{1,65},{65,129},{129,193},{193,1... | collective-permute-start | bytes 2359304 | tf_op jit(solution)/shard_map/ppermute | solution.py:321
  137.3 51.4 %collective-permute-start.9 = (bf16[256,1536]{1,0:T(8,128)(2,1)S(1)}, bf16[256,1536]{1,0:T(8,128)(2,1)}, u32[]{:S(2)}, u32[]{:S(2)}) collective-permute-start(bf16[256,1536]{1,0:T(8,128)(2,1)S(1)} %collective-permute-done.3.refs_10_.refs_14_), channel_id=1, source_target_pairs={{0,128},{64,192},{128,0},{192,64},{1,129},{65,193},{129,1},{193,65... | collective-permute-start | bytes 2359304 | tf_op jit(solution)/shard_map/ppermute | solution.py:321
  159.6 27.0 %copy-start.6 = (bf16[256,1536]{1,0:T(8,128)(2,1)}, bf16[256,1536]{1,0:T(8,128)(2,1)S(1)}, u32[]{:S(2)}) copy-start(bf16[256,1536]{1,0:T(8,128)(2,1)S(1)} %collective-permute-done.4.refs_10_.refs_14_) | copy-start | bytes 2359300
  159.6 46.3 %collective-permute-start.5 = (bf16[256,1536]{1,0:T(8,128)(2,1)S(1)}, bf16[256,1536]{1,0:T(8,128)(2,1)S(1)}, u32[]{:S(2)}, u32[]{:S(2)}) collective-permute-start(bf16[256,1536]{1,0:T(8,128)(2,1)S(1)} %collective-permute-done.4.refs_10_.refs_14_), channel_id=1, source_target_pairs={{0,64},{64,128},{128,192},{192,0},{1,65},{65,129},{129,193},{193,1... | collective-permute-start | bytes 2359304 | tf_op jit(solution)/shard_map/ppermute | solution.py:321
  163.3 42.6 %collective-permute-start.6 = (bf16[256,1536]{1,0:T(8,128)(2,1)S(1)}, bf16[256,1536]{1,0:T(8,128)(2,1)}, u32[]{:S(2)}, u32[]{:S(2)}) collective-permute-start(bf16[256,1536]{1,0:T(8,128)(2,1)S(1)} %collective-permute-done.4.refs_10_.refs_14_), channel_id=1, source_target_pairs={{0,128},{64,192},{128,0},{192,64},{1,129},{65,193},{129,1},{193,65... | collective-permute-start | bytes 2359304 | tf_op jit(solution)/shard_map/ppermute | solution.py:321
  167.6 0.9 copy-start.8
  168.5 37.3 %collective-permute-start.7 = (bf16[256,1536]{1,0:T(8,128)(2,1)S(1)}, bf16[256,1536]{1,0:T(8,128)(2,1)}, u32[]{:S(2)}, u32[]{:S(2)}) collective-permute-start(bf16[256,1536]{1,0:T(8,128)(2,1)S(1)} %collective-permute-done.4.refs_10_.refs_14_), channel_id=1, source_target_pairs={{0,192},{64,0},{128,64},{192,128},{1,193},{65,1},{129,65},{193,129... | collective-permute-start | bytes 2359304 | tf_op jit(solution)/shard_map/ppermute | solution.py:321
  173.4 13.1 %copy-start.4 = (s32[3]{0:T(128)}, s32[3]{0:T(128)S(1)}, u32[]{:S(2)}) copy-start(s32[3]{0:T(128)S(1)} %pad_add_fusion.where_ref.refs_0_) | copy-start | bytes 40
  186.6 0.8 copy-start.1
  187.4 0.7 copy-start.2
  188.1 0.6 copy-start.3
  205.9 0.9 copy-start.7
Sparse Core Ops, SparseCore 0:
  29.2 76.4 all-gather.2
